TPU v7x, 32 devices: a whole 2x2x4 slice. The times are simulated.
32 devices in a mesh: fsdp: 4 (over y, x), ctx: 4 (over z), tp: 2 (over core).
Axes of the slice: x: 2, y: 2, z: 4, core: 2. Of those that a mesh axis runs over, the one named last changes fastest.
Arguments:
- tokens: bfloat16 [4096, 2048], P(('fsdp', 'ctx')), may hold values from -6 to 6
- cotangent: bfloat16 [4096, 2048], P(('fsdp', 'ctx')), may hold values from -6 to 6
- segments: int32 [4096], P(('fsdp', 'ctx')), may hold values from 0 to 12, as said below
- depths: int32 [4096], P(('fsdp', 'ctx')), may hold values from 0 to 542, as said below
- parents: int32 [4, 13], P('fsdp'), may hold values from 0 to 4, as said below
- tree_adapter_index: int32 [4], P('fsdp'), may hold values from 0 to 7
- layer_norm_gains: float32 [2, 2, 2048], replicated, may hold values from 0.5 to 1.5
- difference_lambda: float32 [2, 8], P(None, 'tp'), may hold values from 0.2 to 0.8
- query_key_value_weight: bfloat16 [2, 2048, 3, 2048], P(None, ('fsdp', 'ctx'), None, 'tp'), may hold values from -0.125 to 0.125
- output_weight: bfloat16 [2, 2048, 2048], P(None, ('fsdp', 'ctx'), 'tp'), may hold values from -0.125 to 0.125
- gate_up_weight: bfloat16 [2, 2048, 2, 5632], P(None, ('fsdp', 'ctx'), None, 'tp'), may hold values from -0.125 to 0.125
- down_weight: bfloat16 [2, 2048, 5632], P(None, ('fsdp', 'ctx'), 'tp'), may hold values from -0.078125 to 0.078125
- adapter_model_factors: bfloat16 [2, 11, 8, 16, 2048], replicated, may hold values from -0.29882812 to 0.29882812
- adapter_hidden_factors: bfloat16 [2, 3, 8, 16, 5632], replicated, may hold values from -0.29882812 to 0.29882812
Outputs:
- outputs: bfloat16 [4096, 2048], P(('fsdp', 'ctx'))
- tokens_grad: float32 [4096, 2048], P(('fsdp', 'ctx'))
- grad_lora_model: float32 [2, 11, 8, 16, 2048], P(None, None, 'fsdp', None, ('ctx', 'tp'))
- grad_lora_hidden: float32 [2, 3, 8, 16, 5632], P(None, None, 'fsdp', None, ('ctx', 'tp'))
Inputs may be any that keep to these rules, and one draw needn't show every extreme that they name: `parents`: segment 0 is a tree's trunk and its own parent; segments 1 to 4 are branches with parent 0; segments 5 to 12 are leaves, two on each branch. `segments`: within each tree of 1024 tokens the segment numbers never fall, every segment is nonempty and the trunk fills the first 384 tokens; each branch with its two leaves holds (640) / 4 tokens. `depths`: A token's depth is the total length of its proper ancestor segments plus its offset within its own segment; the largest is reached in every tree.
All inputs are finite; a program needn't handle non-finite values.
Results may differ from a plain program's by a relative error of at most 0.028.
Values may be sent and summed in bfloat16 or wider, within the bound.
A program may use at most 320 MiB of HBM per device.

v0:
```python
import math

import jax
import jax.numpy as jnp
from jax import lax
from jax.sharding import PartitionSpec as P

HD = 128
VD = 256
NSEG = 13


EPSILON = 1e-05
ADAPTER_SCALE = 0.5
NEGATIVE_BIG = -1e30


def matrix_product(left_side, right_side):
    return jnp.dot(left_side, right_side, preferred_element_type=jnp.float32)


def multiply_transposed(left_side, right_side):
    return lax.dot_general(
        left_side, right_side, (((1,), (1,)), ((), ())), preferred_element_type=jnp.float32
    )


def contract_over_rows(left_side, right_side):
    return lax.dot_general(
        left_side, right_side, (((0,), (0,)), ((), ())), preferred_element_type=jnp.float32
    )


def einsum_single(formula, left_side, right_side):
    return jnp.einsum(formula, left_side, right_side, preferred_element_type=jnp.float32)


def rms_scale(values):
    return lax.rsqrt(jnp.mean(values * values, axis=-1, keepdims=True) + EPSILON)


def norm_back(grad_normed, inputs, scale_rows, gain):
    gaussian_draw = inputs * scale_rows
    scaled = grad_normed * gain
    return scale_rows * (
        scaled - gaussian_draw * jnp.mean(scaled * gaussian_draw, axis=-1, keepdims=True)
    )


def angles_of(depths):
    half_width = HD // 2
    frequency = 10000.0 ** (-jnp.arange(half_width).astype(jnp.float32) / half_width)
    return depths.astype(jnp.float32)[:, None] * frequency[None, :]


def rotate(vectors, angles, direction):
    half_width = vectors.shape[-1] // 2
    cosine = jnp.cos(angles)[:, None, None, :]
    sine_part = direction * jnp.sin(angles)[:, None, None, :]
    first_half = vectors[..., :half_width]
    second_half = vectors[..., half_width:]
    return jnp.concatenate(
        [
            first_half * cosine - second_half * sine_part,
            first_half * sine_part + second_half * cosine,
        ],
        axis=-1,
    )


def ancestors(parents):
    parent_table = (parents[:, None] == jnp.arange(NSEG)[None, :]).astype(jnp.float32)
    identity = jnp.eye(NSEG, dtype=jnp.float32)
    return jnp.minimum(identity + parent_table + jnp.dot(parent_table, parent_table), 1.0)


def keep_factor(current_layer_index):
    return 0.2 + 0.6 * math.exp(-0.3 * current_layer_index)


def key_mask(reach_rows, query_segments, query_index, key_segments, first_row):
    piece_rows = key_segments.shape[0]
    key_table = (key_segments[:, None] == jnp.arange(NSEG)[None, :]).astype(jnp.float32)
    allowed = multiply_transposed(reach_rows, key_table) > 0.5
    key_index = first_row + jnp.arange(piece_rows)
    same_segment = query_segments[:, None] == key_segments[None, :]
    causal = query_index[:, None] >= key_index[None, :]
    return allowed & (causal | jnp.logical_not(same_segment))


def branch_total(pair):
    return lax.psum((pair[0], pair[1]), "tp")


def grad_total(pair):
    return lax.psum((pair[0], pair[1]), "tp")


def attend_forward(queries, key_vectors, value_vectors, segments, reach_rows, query_index):
    token_row_count, head_count = (queries.shape[0], queries.shape[1])
    score_scale = HD ** (-0.5)
    key_rows, value_rows, segment_rows = (
        lax.all_gather(key_vectors, "ctx", axis=0, tiled=True),
        lax.all_gather(value_vectors, "ctx", axis=0, tiled=True),
        lax.all_gather(segments, "ctx", axis=0, tiled=True),
    )
    block_rows = 2 * token_row_count
    block_count = key_rows.shape[0] // block_rows

    def block_scores(block_index):
        first_row = block_index * block_rows
        key_block = lax.dynamic_slice_in_dim(key_rows, first_row, block_rows, 0).reshape(
            block_rows, head_count, 2, HD
        )
        value_block = lax.dynamic_slice_in_dim(value_rows, first_row, block_rows, 0).reshape(
            block_rows, head_count, VD
        )
        segment_block = lax.dynamic_slice_in_dim(segment_rows, first_row, block_rows, 0)
        visible = key_mask(reach_rows, segments, query_index, segment_block, first_row)
        scores = einsum_single("qhcd,khcd->hcqk", queries, key_block) * score_scale
        return (jnp.where(visible, scores, NEGATIVE_BIG), visible, value_block)

    def first_pass(state, block_index):
        running_max, running_sum = state
        scores, visible, unused = block_scores(block_index)
        new_max = jnp.maximum(running_max, jnp.max(scores, axis=-1))
        weights = jnp.where(visible, jnp.exp(scores - new_max[..., None]), 0.0)
        running_sum = running_sum * jnp.exp(running_max - new_max) + jnp.sum(weights, axis=-1)
        return ((new_max, running_sum), None)

    start_state = (
        jnp.full((head_count, 2, token_row_count), NEGATIVE_BIG, jnp.float32),
        jnp.zeros((head_count, 2, token_row_count), jnp.float32),
    )
    (running_max, running_sum), unused_out = lax.scan(
        first_pass, start_state, jnp.arange(block_count)
    )
    log_total = running_max + jnp.log(running_sum)

    def second_pass(accumulated, block_index):
        scores, visible, value_block = block_scores(block_index)
        probability = jnp.exp(jnp.where(visible, scores - log_total[..., None], NEGATIVE_BIG))
        return (
            accumulated
            + einsum_single("hcqk,khv->hcqv", probability.astype(jnp.bfloat16), value_block),
            None,
        )

    zero_mix = jnp.zeros((head_count, 2, token_row_count, VD), jnp.float32)
    softmax_mixes, unused_out = lax.scan(second_pass, zero_mix, jnp.arange(block_count))
    return (log_total, softmax_mixes)


def softmax_terms(lambdas, softmax_mixes, grad_mixed):
    factor = jnp.stack([jnp.ones_like(lambdas), -lambdas], axis=1)
    grad_float = grad_mixed.astype(jnp.float32)
    delta = factor[:, :, None] * jnp.sum(grad_float[:, None] * softmax_mixes, axis=-1)
    return (factor, delta)


def score_grads(queries, key_block, value_block, visible, log_total, delta, factor, grad_mixed):
    score_scale = HD ** (-0.5)
    scores = einsum_single("qhcd,khcd->hcqk", queries, key_block) * score_scale
    probability = jnp.exp(jnp.where(visible, scores - log_total[..., None], NEGATIVE_BIG))
    rounded = probability.astype(jnp.bfloat16)
    grad_weights = einsum_single("hqv,khv->hqk", grad_mixed, value_block)
    grad_scores = (
        probability * (factor[:, :, None, None] * grad_weights[:, None] - delta[..., None])
    ).astype(jnp.bfloat16)
    return (rounded, grad_scores)


def attend_backward(
    queries,
    key_rows,
    value_rows,
    segment_rows,
    reach_rows,
    segments,
    query_index,
    lambdas,
    log_total,
    factor,
    delta,
    grad_mixed,
):
    token_row_count, head_count = (queries.shape[0], queries.shape[1])
    score_scale = HD ** (-0.5)
    block_rows = 2 * token_row_count
    total_rows = key_rows.shape[0]
    block_count = total_rows // block_rows

    def one_block(grad_queries, block_index):
        first_row = block_index * block_rows
        key_block = lax.dynamic_slice_in_dim(key_rows, first_row, block_rows, 0).reshape(
            block_rows, head_count, 2, HD
        )
        value_block = lax.dynamic_slice_in_dim(value_rows, first_row, block_rows, 0).reshape(
            block_rows, head_count, VD
        )
        segment_block = lax.dynamic_slice_in_dim(segment_rows, first_row, block_rows, 0)
        visible = key_mask(reach_rows, segments, query_index, segment_block, first_row)
        rounded, grad_scores = score_grads(
            queries, key_block, value_block, visible, log_total, delta, factor, grad_mixed
        )
        grad_queries = grad_queries + score_scale * einsum_single(
            "hcqk,khcd->qhcd", grad_scores, key_block
        )
        grad_values = einsum_single("hqk,hqv->khv", rounded[:, 0], grad_mixed) - lambdas[
            None, :, None
        ] * einsum_single("hqk,hqv->khv", rounded[:, 1], grad_mixed)
        grad_keys = score_scale * einsum_single("hcqk,qhcd->khcd", grad_scores, queries)
        return (
            grad_queries,
            (grad_keys.reshape(block_rows, -1), grad_values.reshape(block_rows, -1)),
        )

    zero_queries = jnp.zeros(queries.shape, jnp.float32)
    grad_queries, key_parts = lax.scan(one_block, zero_queries, jnp.arange(block_count))
    grad_keys, grad_values = key_parts
    key_terms = jnp.concatenate(
        [grad_keys.reshape(total_rows, -1), grad_values.reshape(total_rows, -1)], axis=1
    )
    local_terms = lax.psum_scatter(key_terms, "ctx", scatter_dimension=0, tiled=True)
    return (grad_queries, local_terms)


def place_columns(term, tp_index, col_width, total_width):
    zero_filled = jnp.zeros(term.shape[:-1] + (total_width,), jnp.float32)
    return lax.dynamic_update_slice_in_dim(zero_filled, term, tp_index * col_width, term.ndim - 1)


def shards(
    tokens,
    cotangent,
    segments,
    depths,
    parents,
    tree_adapter_index,
    layer_norm_gains,
    difference_lambda,
    query_key_value_weight,
    output_weight,
    gate_up_weight,
    down_weight,
    adapter_model_factors,
    adapter_hidden_factors,
):
    token_row_count, model_feature_width = tokens.shape
    layer_count = query_key_value_weight.shape[0]
    head_count = difference_lambda.shape[1]
    col_width = head_count * VD
    hidden_local = down_weight.shape[2]
    feedforward_width = adapter_hidden_factors.shape[4]
    adapter_rank = adapter_model_factors.shape[3]
    adapter_number = adapter_model_factors.shape[2]
    tp_index = lax.axis_index("tp")
    tensor_parallel_leader = (tp_index == 0).astype(jnp.float32)
    adapter_slot = tree_adapter_index[0]
    reach_table = ancestors(parents[0])
    query_table = (segments[:, None] == jnp.arange(NSEG)[None, :]).astype(jnp.float32)
    reach_rows = jnp.dot(query_table, reach_table)
    query_index = lax.axis_index("ctx") * token_row_count + jnp.arange(token_row_count)
    angles = angles_of(depths)

    def adapter_slices(current_layer_index):
        model_portion = adapter_model_factors[current_layer_index, :, adapter_slot]
        hidden_portion = adapter_hidden_factors[current_layer_index, :, adapter_slot]
        raise_query_key_value = lax.dynamic_slice_in_dim(
            model_portion[6:9], tp_index * col_width, col_width, 2
        )
        reduce_out = lax.dynamic_slice_in_dim(model_portion[3], tp_index * col_width, col_width, 1)
        raise_gate_up = lax.dynamic_slice_in_dim(
            hidden_portion[0:2], tp_index * hidden_local, hidden_local, 2
        )
        reduce_down = lax.dynamic_slice_in_dim(
            hidden_portion[2], tp_index * hidden_local, hidden_local, 1
        )
        return (model_portion, raise_query_key_value, reduce_out, raise_gate_up, reduce_down)

    residual_stream = tokens.astype(jnp.float32)
    saved = []
    for current_layer_index in range(layer_count):
        gathered = (
            lax.all_gather(
                query_key_value_weight[current_layer_index], ("fsdp", "ctx"), axis=0, tiled=True
            ),
            lax.all_gather(output_weight[current_layer_index], ("fsdp", "ctx"), axis=0, tiled=True),
            lax.all_gather(
                gate_up_weight[current_layer_index], ("fsdp", "ctx"), axis=0, tiled=True
            ),
            lax.all_gather(down_weight[current_layer_index], ("fsdp", "ctx"), axis=0, tiled=True),
        )
        query_key_value_matrix, weight_out, weight_gateup, weight_down = gathered
        model_portion, raise_query_key_value, reduce_out, raise_gate_up, reduce_down = (
            adapter_slices(current_layer_index)
        )
        lambdas = difference_lambda[current_layer_index]
        scale_attn = rms_scale(residual_stream)
        normed_attention_input = (
            residual_stream * scale_attn * layer_norm_gains[current_layer_index, 0]
        ).astype(jnp.bfloat16)
        reduced_query_key_value = (
            multiply_transposed(
                normed_attention_input,
                model_portion[0:3].reshape(3 * adapter_rank, model_feature_width),
            )
            .astype(jnp.bfloat16)
            .reshape(token_row_count, 3, adapter_rank)
        )
        projected_rows = einsum_single(
            "zs,sxw->zxw", normed_attention_input, query_key_value_matrix
        ) + ADAPTER_SCALE * einsum_single(
            "gwy,wyk->gwk", reduced_query_key_value, raise_query_key_value
        )
        queries = rotate(
            projected_rows[:, 0].reshape(token_row_count, head_count, 2, HD), angles, 1.0
        ).astype(jnp.bfloat16)
        key_vectors = (
            rotate(projected_rows[:, 1].reshape(token_row_count, head_count, 2, HD), angles, 1.0)
            .astype(jnp.bfloat16)
            .reshape(token_row_count, col_width)
        )
        value_vectors = projected_rows[:, 2].astype(jnp.bfloat16)
        log_total, softmax_mixes = attend_forward(
            queries, key_vectors, value_vectors, segments, reach_rows, query_index
        )
        mixed_heads = softmax_mixes[:, 0] - lambdas[:, None, None] * softmax_mixes[:, 1]
        scale_heads = rms_scale(mixed_heads)
        per_head_rows = (
            (mixed_heads * scale_heads * keep_factor(current_layer_index))
            .transpose(1, 0, 2)
            .reshape(token_row_count, col_width)
            .astype(jnp.bfloat16)
        )
        attention_portion, side_part = branch_total(
            (
                multiply_transposed(per_head_rows, weight_out),
                multiply_transposed(per_head_rows, reduce_out),
            )
        )
        adapter_attention = side_part.astype(jnp.bfloat16)
        residual_middle = (
            residual_stream
            + attention_portion
            + ADAPTER_SCALE * matrix_product(adapter_attention, model_portion[9])
        )
        scale_ffn = rms_scale(residual_middle)
        normed_feedforward_input = (
            residual_middle * scale_ffn * layer_norm_gains[current_layer_index, 1]
        ).astype(jnp.bfloat16)
        reduced_feedforward = (
            multiply_transposed(
                normed_feedforward_input,
                model_portion[4:6].reshape(2 * adapter_rank, model_feature_width),
            )
            .astype(jnp.bfloat16)
            .reshape(token_row_count, 2, adapter_rank)
        )
        gate_up_values = einsum_single(
            "im,mqg->iqg", normed_feedforward_input, weight_gateup
        ) + ADAPTER_SCALE * einsum_single("jvi,vin->jvn", reduced_feedforward, raise_gate_up)
        gate_value = gate_up_values[:, 0]
        up_value = gate_up_values[:, 1]
        hidden_activation = (jax.nn.silu(gate_value) * up_value).astype(jnp.bfloat16)
        feedforward_portion, side_part_ffn = branch_total(
            (
                multiply_transposed(hidden_activation, weight_down),
                multiply_transposed(hidden_activation, reduce_down),
            )
        )
        adapter_feedforward = side_part_ffn.astype(jnp.bfloat16)
        residual_following = (
            residual_middle
            + feedforward_portion
            + ADAPTER_SCALE * matrix_product(adapter_feedforward, model_portion[10])
        )
        stored_weights = None
        saved.append(
            (
                stored_weights,
                residual_stream,
                scale_attn,
                normed_attention_input,
                reduced_query_key_value,
                queries,
                key_vectors,
                value_vectors,
                log_total,
                softmax_mixes,
                mixed_heads,
                scale_heads,
                per_head_rows,
                adapter_attention,
                residual_middle,
                scale_ffn,
                normed_feedforward_input,
                reduced_feedforward,
                gate_value,
                up_value,
                hidden_activation,
                adapter_feedforward,
            )
        )
        residual_stream = residual_following
    grad = cotangent.astype(jnp.float32)
    model_grads = []
    hidden_grads = []
    for current_layer_index in reversed(range(layer_count)):
        (
            stored_weights,
            residual_in,
            scale_attn,
            normed_attention_input,
            reduced_query_key_value,
            queries,
            key_vectors,
            value_vectors,
            log_total,
            softmax_mixes,
            mixed_heads,
            scale_heads,
            per_head_rows,
            adapter_attention,
            residual_middle,
            scale_ffn,
            normed_feedforward_input,
            reduced_feedforward,
            gate_value,
            up_value,
            hidden_activation,
            adapter_feedforward,
        ) = saved[current_layer_index]
        query_key_value_matrix, weight_out, weight_gateup, weight_down = (
            lax.all_gather(
                query_key_value_weight[current_layer_index], ("fsdp", "ctx"), axis=0, tiled=True
            ),
            lax.all_gather(output_weight[current_layer_index], ("fsdp", "ctx"), axis=0, tiled=True),
            lax.all_gather(
                gate_up_weight[current_layer_index], ("fsdp", "ctx"), axis=0, tiled=True
            ),
            lax.all_gather(down_weight[current_layer_index], ("fsdp", "ctx"), axis=0, tiled=True),
        )
        model_portion, raise_query_key_value, reduce_out, raise_gate_up, reduce_down = (
            adapter_slices(current_layer_index)
        )
        lambdas = difference_lambda[current_layer_index]
        gradient_lowrank = grad.astype(jnp.bfloat16)
        gradient_raise_down = (
            tensor_parallel_leader
            * ADAPTER_SCALE
            * contract_over_rows(adapter_feedforward, gradient_lowrank)
        )
        gradient_adapter_feedforward = (
            ADAPTER_SCALE * multiply_transposed(gradient_lowrank, model_portion[10])
        ).astype(jnp.bfloat16)
        grad_hidden = matrix_product(gradient_lowrank, weight_down) + matrix_product(
            gradient_adapter_feedforward, reduce_down
        )
        grad_reduce_down = contract_over_rows(gradient_adapter_feedforward, hidden_activation)
        sigmoid_gate = jax.nn.sigmoid(gate_value)
        grad_gate = (
            grad_hidden * up_value * sigmoid_gate * (1.0 + gate_value * (1.0 - sigmoid_gate))
        )
        grad_up = grad_hidden * gate_value * sigmoid_gate
        gradient_gate_up = jnp.stack([grad_gate, grad_up], axis=1).astype(jnp.bfloat16)
        gradient_raise_gate_up = ADAPTER_SCALE * einsum_single(
            "ajl,ajw->jlw", reduced_feedforward, gradient_gate_up
        )
        input_part, side_part = grad_total(
            (
                einsum_single("tcf,dcf->td", gradient_gate_up, weight_gateup),
                ADAPTER_SCALE * einsum_single("ihl,hwl->ihw", gradient_gate_up, raise_gate_up),
            )
        )
        gradient_reduced_feedforward = side_part.astype(jnp.bfloat16)
        grad_normed_ffn = input_part + matrix_product(
            gradient_reduced_feedforward.reshape(token_row_count, 2 * adapter_rank),
            model_portion[4:6].reshape(2 * adapter_rank, model_feature_width),
        )
        grad_reduce_gateup = tensor_parallel_leader * einsum_single(
            "tcr,td->crd", gradient_reduced_feedforward, normed_feedforward_input
        )
        grad = grad + norm_back(
            grad_normed_ffn, residual_middle, scale_ffn, layer_norm_gains[current_layer_index, 1]
        )
        gradient_lowrank = grad.astype(jnp.bfloat16)
        gradient_raise_output = (
            tensor_parallel_leader
            * ADAPTER_SCALE
            * contract_over_rows(adapter_attention, gradient_lowrank)
        )
        gradient_adapter_attention = (
            ADAPTER_SCALE * multiply_transposed(gradient_lowrank, model_portion[9])
        ).astype(jnp.bfloat16)
        grad_headed = matrix_product(gradient_lowrank, weight_out) + matrix_product(
            gradient_adapter_attention, reduce_out
        )
        grad_reduce_out = contract_over_rows(gradient_adapter_attention, per_head_rows)
        grad_heads = grad_headed.reshape(token_row_count, head_count, VD).transpose(1, 0, 2)
        grad_mixed = norm_back(
            grad_heads, mixed_heads, scale_heads, keep_factor(current_layer_index)
        ).astype(jnp.bfloat16)
        factor, delta = softmax_terms(lambdas, softmax_mixes, grad_mixed)
        key_rows, value_rows, segment_rows = (
            lax.all_gather(key_vectors, "ctx", axis=0, tiled=True),
            lax.all_gather(value_vectors, "ctx", axis=0, tiled=True),
            lax.all_gather(segments, "ctx", axis=0, tiled=True),
        )
        grad_queries, local_terms = attend_backward(
            queries,
            key_rows,
            value_rows,
            segment_rows,
            reach_rows,
            segments,
            query_index,
            lambdas,
            log_total,
            factor,
            delta,
            grad_mixed,
        )
        grad_keys = local_terms[:, :col_width].reshape(token_row_count, head_count, 2, HD)
        grad_values = local_terms[:, col_width:]
        gradient_projected_rows = jnp.stack(
            [
                rotate(grad_queries, angles, -1.0).reshape(token_row_count, col_width),
                rotate(grad_keys, angles, -1.0).reshape(token_row_count, col_width),
                grad_values,
            ],
            axis=1,
        ).astype(jnp.bfloat16)
        gradient_raise_query_key_value = ADAPTER_SCALE * einsum_single(
            "qok,qoj->okj", reduced_query_key_value, gradient_projected_rows
        )
        input_part, side_part = grad_total(
            (
                einsum_single("tcn,dcn->td", gradient_projected_rows, query_key_value_matrix),
                ADAPTER_SCALE
                * einsum_single("mhu,hzu->mhz", gradient_projected_rows, raise_query_key_value),
            )
        )
        gradient_reduced_query_key_value = side_part.astype(jnp.bfloat16)
        grad_normed = input_part + matrix_product(
            gradient_reduced_query_key_value.reshape(token_row_count, 3 * adapter_rank),
            model_portion[0:3].reshape(3 * adapter_rank, model_feature_width),
        )
        grad_reduce_qkv = tensor_parallel_leader * einsum_single(
            "tcr,td->crd", gradient_reduced_query_key_value, normed_attention_input
        )
        grad = grad + norm_back(
            grad_normed, residual_in, scale_attn, layer_norm_gains[current_layer_index, 0]
        )
        model_grads.insert(
            0,
            jnp.concatenate(
                [
                    grad_reduce_qkv,
                    place_columns(grad_reduce_out[None], tp_index, col_width, model_feature_width),
                    grad_reduce_gateup,
                    place_columns(
                        gradient_raise_query_key_value, tp_index, col_width, model_feature_width
                    ),
                    gradient_raise_output[None],
                    gradient_raise_down[None],
                ],
                axis=0,
            ),
        )
        hidden_grads.insert(
            0,
            jnp.concatenate(
                [
                    place_columns(
                        gradient_raise_gate_up, tp_index, hidden_local, feedforward_width
                    ),
                    place_columns(
                        grad_reduce_down[None], tp_index, hidden_local, feedforward_width
                    ),
                ],
                axis=0,
            ),
        )
    own_model = jnp.stack(model_grads)
    own_hidden = jnp.stack(hidden_grads)
    adapter_table = (jnp.arange(adapter_number) == adapter_slot).astype(jnp.float32)[
        None, None, :, None, None
    ]
    part_model, part_hidden = (
        lax.psum_scatter(
            own_model[:, :, None] * adapter_table, "fsdp", scatter_dimension=2, tiled=True
        ),
        lax.psum_scatter(
            own_hidden[:, :, None] * adapter_table, "fsdp", scatter_dimension=2, tiled=True
        ),
    )
    grad_model, grad_hidden = (
        lax.psum_scatter(part_model, ("ctx", "tp"), scatter_dimension=4, tiled=True),
        lax.psum_scatter(part_hidden, ("ctx", "tp"), scatter_dimension=4, tiled=True),
    )
    return (residual_stream.astype(jnp.bfloat16), grad, grad_model, grad_hidden)


def solution(mesh):
    in_specs = (
        P(("fsdp", "ctx"), None),
        P(("fsdp", "ctx"), None),
        P(("fsdp", "ctx")),
        P(("fsdp", "ctx")),
        P("fsdp", None),
        P("fsdp"),
        P(),
        P(None, "tp"),
        P(None, ("fsdp", "ctx"), None, "tp"),
        P(None, ("fsdp", "ctx"), "tp"),
        P(None, ("fsdp", "ctx"), None, "tp"),
        P(None, ("fsdp", "ctx"), "tp"),
        P(),
        P(),
    )
    out_specs = (
        P(("fsdp", "ctx"), None),
        P(("fsdp", "ctx"), None),
        P(None, None, "fsdp", None, ("ctx", "tp")),
        P(None, None, "fsdp", None, ("ctx", "tp")),
    )
    return jax.shard_map(shards, mesh=mesh, in_specs=in_specs, out_specs=out_specs, check_vma=False)
```

profile of v0, /device:TPU:3, one launch (start us, length us, event | category | flops | bytes accessed | tf_op | source)
XLA Modules:
  0.0 3075.7 jit_solution(10709417264127017868)
XLA Ops:
  14.0 150.1 %all-gather.28.cloned.1.call-done = bf16[1,2048,3,1024]{3,1,2,0:T(8,128)(2,1)} async-done(((bf16[1,128,3,1024]{3,1,2,0:T(8,128)(2,1)}), bf16[1,2048,3,1024]{3,1,2,0:T(8,128)(2,1)}) %all-gather.28.cloned.1.call-update) | async-done | bytes 12582928 | tf_op jit(solution)/shard_map/all_gather | solution.py:285
  164.1 6.5 fusion.72
  184.4 7.9 all-gather.10
  194.4 25.1 all-gather.30.cloned.1.call-done
  223.4 43.5 %all-gather.24.cloned.1.call-done = bf16[1024,1024]{0,1:T(8,128)(2,1)} async-done(((bf16[256,1024]{0,1:T(8,128)(2,1)}), bf16[1024,1024]{0,1:T(8,128)(2,1)}) %all-gather.24.cloned.1.call-update) | async-done | bytes 2097168 | tf_op jit(solution)/shard_map/all_gather | solution.py:103
  266.9 20.5 while.78
  287.4 16.5 while.79
  307.2 35.7 %all-gather.32.cloned.1.call-done = bf16[1,2048,1024]{2,1,0:T(8,128)(2,1)} async-done(((bf16[1,128,1024]{2,1,0:T(8,128)(2,1)}), bf16[1,2048,1024]{2,1,0:T(8,128)(2,1)}) %all-gather.32.cloned.1.call-update) | async-done | bytes 4194320 | tf_op jit(solution)/shard_map/all_gather | solution.py:288
  363.5 6.1 all-reduce.16.cloned.1.call-done
  373.0 250.7 %all-gather.34.cloned.1.call-done = bf16[1,2048,2,2816]{3,1,2,0:T(8,128)(2,1)} async-done(((bf16[1,128,2,2816]{3,1,2,0:T(8,128)(2,1)}), bf16[1,2048,2,2816]{3,1,2,0:T(8,128)(2,1)}) %all-gather.34.cloned.1.call-update) | async-done | bytes 23068688 | tf_op jit(solution)/shard_map/all_gather | solution.py:289
  623.7 10.7 fusion.64
  639.7 128.2 %all-gather.36.cloned.1.call-done = bf16[1,2048,2816]{2,1,0:T(8,128)(2,1)} async-done(((bf16[1,128,2816]{2,1,0:T(8,128)(2,1)}), bf16[1,2048,2816]{2,1,0:T(8,128)(2,1)}) %all-gather.36.cloned.1.call-update) | async-done | bytes 11534352 | tf_op jit(solution)/shard_map/all_gather | solution.py:292
  767.9 8.8 fusion.80
  785.3 12.2 all-reduce.18.cloned.1.call-done
  801.9 150.5 %all-gather.38.cloned.1.call-done = bf16[1,2048,3,1024]{3,1,2,0:T(8,128)(2,1)} async-done(((bf16[1,128,3,1024]{3,1,2,0:T(8,128)(2,1)}), bf16[1,2048,3,1024]{3,1,2,0:T(8,128)(2,1)}) %all-gather.38.cloned.1.call-update) | async-done | bytes 12582928 | tf_op jit(solution)/shard_map/all_gather | solution.py:285
  952.3 6.4 fusion.68
  968.1 37.8 %all-gather.40.cloned.1.call-done = bf16[1024,1,1024]{2,0,1:T(8,128)(2,1)} async-done(((bf16[256,1,1024]{2,0,1:T(8,128)(2,1)}), bf16[1024,1,1024]{2,0,1:T(8,128)(2,1)}) %all-gather.40.cloned.1.call-update) | async-done | bytes 2097168 | tf_op jit(solution)/shard_map/all_gather | solution.py:104
  1009.9 43.4 %all-gather.26.cloned.1.call-done = bf16[1024,1024]{0,1:T(8,128)(2,1)} async-done(((bf16[256,1024]{0,1:T(8,128)(2,1)}), bf16[1024,1024]{0,1:T(8,128)(2,1)}) %all-gather.26.cloned.1.call-update) | async-done | bytes 2097168 | tf_op jit(solution)/shard_map/all_gather | solution.py:103
  1053.3 18.3 while.80
  1071.6 15.5 while.81
  1089.4 39.2 %all-gather.42.cloned.1.call-done = bf16[1,2048,1024]{2,1,0:T(8,128)(2,1)} async-done(((bf16[1,128,1024]{2,1,0:T(8,128)(2,1)}), bf16[1,2048,1024]{2,1,0:T(8,128)(2,1)}) %all-gather.42.cloned.1.call-update) | async-done | bytes 4194320 | tf_op jit(solution)/shard_map/all_gather | solution.py:288
  1137.8 135.5 %all-gather.46.cloned.1.call-done = bf16[1,2048,2816]{2,1,0:T(8,128)(2,1)} async-done(((bf16[1,128,2816]{2,1,0:T(8,128)(2,1)}), bf16[1,2048,2816]{2,1,0:T(8,128)(2,1)}) %all-gather.46.cloned.1.call-update) | async-done | bytes 11534352 | tf_op jit(solution)/shard_map/all_gather | solution.py:292
  1273.3 9.4 fusion.74
  1287.9 8.4 all-reduce.20.cloned.1.call-done
  1300.5 249.8 %all-gather.44.cloned.1.call-done = bf16[1,2048,2,2816]{3,1,2,0:T(8,128)(2,1)} async-done(((bf16[1,128,2,2816]{3,1,2,0:T(8,128)(2,1)}), bf16[1,2048,2,2816]{3,1,2,0:T(8,128)(2,1)}) %all-gather.44.cloned.1.call-update) | async-done | bytes 23068688 | tf_op jit(solution)/shard_map/all_gather | solution.py:289
  1550.3 10.7 fusion.60
  1567.2 12.7 fusion.126
  1588.1 12.9 all-reduce.22.cloned.1.call-done
  1618.4 55.8 %while.82 = (s32[]{:T(128)}, f32[256,4,2,128]{0,3,2,1:T(8,128)}, f32[2,512,1024]{2,1,0:T(8,128)}, f32[2,512,1024]{2,1,0:T(8,128)}, s32[2]{0:T(128)S(1)}, /*index...) while((s32[]{:T(128)}, f32[256,4,2,128]{0,3,2,1:T(8,128)}, ...), condition=%wide.region_32.33_spmd.clone, body=%wide.region_31.32_spmd.clone.sunk | while | flops 1625562368 | bytes 54301520 | solution.py:219
  1674.2 7.8 pad_maximum_fusion
  1682.5 144.4 %reduce-scatter.13.cloned.1.call-done = f32[256,2048]{1,0:T(8,128)} async-done(((f32[1024,2048]{1,0:T(8,128)}), f32[256,2048]{1,0:T(8,128)}) %reduce-scatter.13.cloned.1.call-update) | async-done | bytes 2097168 | tf_op jit(solution)/shard_map/reduce_scatter | solution.py:224
  1831.1 9.7 fusion.120
  1847.1 16.8 all-reduce.24.cloned.1.call-done
  1869.1 6.5 fusion.78
  1878.2 13.1 fusion.123
  1898.7 15.2 all-reduce.26.cloned.1.call-done
  1931.8 56.1 %while.83 = (s32[]{:T(128)}, f32[256,4,2,128]{0,3,2,1:T(8,128)}, f32[2,512,1024]{2,1,0:T(8,128)}, f32[2,512,1024]{2,1,0:T(8,128)}, s32[2]{0:T(128)S(1)}, /*index...) while((s32[]{:T(128)}, f32[256,4,2,128]{0,3,2,1:T(8,128)}, ...), condition=%wide.region_43.44_spmd.clone, body=%wide.region_42.43_spmd.clone.sunk | while | flops 1625562368 | bytes 54301520 | solution.py:219
  1987.9 7.9 pad_maximum_fusion.1
  2012.8 8.2 broadcast_multiply_fusion.1
  2022.6 118.1 %reduce-scatter.15.cloned.1.call-done = f32[256,2048]{1,0:T(8,128)} async-done(((f32[1024,2048]{1,0:T(8,128)}), f32[256,2048]{1,0:T(8,128)}) %reduce-scatter.15.cloned.1.call-update) | async-done | bytes 2097168 | tf_op jit(solution)/shard_map/reduce_scatter | solution.py:224
  2160.7 12.6 broadcast_multiply_fusion
  2173.7 9.3 fusion.76
  2183.0 9.3 fusion.117
  2194.3 668.5 %all-reduce.28.cloned.1.call-done = (f32[2,11,8,16,2048]{4,3,2,1,0:T(8,128)}, f32[2,3,8,16,5632]{4,3,2,1,0:T(8,128)}) async-done(((f32[2,11,8,16,2048]{4,3,2,1,0:T(8,128)}, f32[2,3,8,16,5632]{4,3,2,1,0:T(8,128)}), (f32[2,11,8,16,2048]{4,3,2,1,0:T(8,128)}, f32[2,3,8,16,5632]{4,3,2,1,0:T(8,128)})) %all-reduce.28.cloned.1.call-update) | async-done | bytes 40370192
  2867.3 38.6 %copy.402 = f32[2,3,2,16,5632]{3,2,1,0,4:T(2,128)} copy(f32[2,3,2,16,5632]{4,3,2,1,0:T(8,128)} %constant_dynamic-slice_fusion.14) | data formatting | bytes 8650752
  2905.9 33.6 %reshape.477 = f32[5632,192]{1,0:T(8,128)} reshape(f32[5632,2,3,2,16]{4,3,2,1,0:T(2,128)} %bitcast.803) | data formatting | bytes 8650752
  2953.4 48.9 %reduce-scatter.19.cloned.1.call-done = f32[704,192]{1,0:T(8,128)} async-done(((f32[5632,192]{1,0:T(8,128)}), f32[704,192]{1,0:T(8,128)}) %reduce-scatter.19.cloned.1.call-update) | async-done | bytes 540688
  3013.8 54.6 %reduce-scatter.17.cloned.1.call-done = f32[2,11,2,16,256]{4,3,2,1,0:T(8,128)} async-done(((f32[2,11,2,16,2048]{4,3,2,1,0:T(8,128)}), f32[2,11,2,16,256]{4,3,2,1,0:T(8,128)}) %reduce-scatter.17.cloned.1.call-update) | async-done | bytes 720912 | tf_op jit(solution)/shard_map/reduce_scatter | solution.py:599
  (680 shorter events, 423.9 us)
Async XLA Ops:
  7.2 156.9 %all-gather.28.cloned.1.call-start = ((), (), s32[]{:S(2)}) async-start(), calls=%async_computation.15 | async-start | bytes 13369344 | tf_op jit(solution)/shard_map/all_gather | solution.py:285
  10.0 209.4 %all-gather.30.cloned.1.call-start = ((), (), s32[]{:S(2)}) async-start(), calls=%async_computation.16 | async-start | bytes 2621440 | tf_op jit(solution)/shard_map/all_gather | solution.py:104
  11.1 159.5 %copy-start.110 = (f32[256]{0:T(256)}, f32[256]{0:T(256)S(1)}, u32[]{:S(2)}) copy-start(f32[256]{0:T(256)S(1)} %add_rsqrt_fusion.5) | copy-start | bytes 3076
  13.5 157.1 %copy-start.78 = (f32[1,1,2048]{2,1,0:T(1,128)}, f32[1,1,2048]{2,1,0:T(1,128)S(1)}, u32[]{:S(2)}) copy-start(f32[1,1,2048]{2,1,0:T(1,128)S(1)} %get-tuple-element.1283) | copy-start | bytes 24580
  13.5 358.4 %copy-start.94 = (f32[1,1,2048]{2,1,0:T(1,128)}, f32[1,1,2048]{2,1,0:T(1,128)S(1)}, u32[]{:S(2)}) copy-start(f32[1,1,2048]{2,1,0:T(1,128)S(1)} %get-tuple-element.1282) | copy-start | bytes 24580
  14.0 156.6 %copy-start.112 = (bf16[256,48]{0,1:T(8,128)(2,1)}, bf16[256,48]{0,1:T(8,128)(2,1)S(1)}, u32[]{:S(2)}) copy-start(bf16[256,48]{0,1:T(8,128)(2,1)S(1)} %convolution_convert_fusion.1) | copy-start | bytes 73732
  174.8 92.1 %all-gather.24.cloned.1.call-start = ((), (), s32[]{:S(2)}) async-start(), calls=%async_computation.4 | async-start | bytes 2621440 | tf_op jit(solution)/shard_map/all_gather | solution.py:103
  182.3 160.5 %all-gather.32.cloned.1.call-start = ((), (), s32[]{:S(2)}) async-start(), calls=%async_computation.17 | async-start | bytes 4456448 | tf_op jit(solution)/shard_map/all_gather | solution.py:288
  184.3 185.3 %all-reduce.16.cloned.1.call-start = ((), (), s32[]{:S(2)}) async-start(), calls=%async_computation.5 | async-start | bytes 4194304 | tf_op jit(solution)/shard_map/psum | solution.py:92
  193.3 30.0 copy-start.20
  306.1 41.6 %copy-start.103 = (f32[4,256]{1,0:T(4,128)}, f32[4,256]{1,0:T(4,128)S(1)}, u32[]{:S(2)}) copy-start(f32[4,256]{1,0:T(4,128)S(1)} %add_rsqrt_fusion.1) | copy-start | bytes 12292
  307.2 50.0 %copy-start.40 = (bf16[4,256,256]{1,2,0:T(8,128)(2,1)}, bf16[4,256,256]{1,2,0:T(8,128)(2,1)S(1)}, u32[]{:S(2)}) copy-start(bf16[4,256,256]{1,2,0:T(8,128)(2,1)S(1)} %multiply_convert_fusion.12) | copy-start | bytes 1572868
  347.7 276.0 %all-gather.34.cloned.1.call-start = ((), (), s32[]{:S(2)}) async-start(), calls=%async_computation.18 | async-start | bytes 24510464 | tf_op jit(solution)/shard_map/all_gather | solution.py:289
  353.7 414.2 %all-gather.36.cloned.1.call-start = ((), (), s32[]{:S(2)}) async-start(), calls=%async_computation.19 | async-start | bytes 12255232 | tf_op jit(solution)/shard_map/all_gather | solution.py:292
  355.5 442.0 %all-reduce.18.cloned.1.call-start = ((), (), s32[]{:S(2)}) async-start(), calls=%async_computation.6 | async-start | bytes 4194304 | tf_op jit(solution)/shard_map/psum | solution.py:92
  371.9 425.7 %copy-start.2 = (f32[256,2048]{1,0:T(8,128)}, f32[256,2048]{1,0:T(8,128)S(1)}, u32[]{:S(2)}) copy-start(f32[256,2048]{1,0:T(8,128)S(1)} %get-tuple-element.1295) | copy-start | bytes 6291460
  372.2 262.2 %copy-start.27 = (bf16[256,2048]{1,0:T(8,128)(2,1)}, bf16[256,2048]{1,0:T(8,128)(2,1)S(1)}, u32[]{:S(2)}) copy-start(bf16[256,2048]{1,0:T(8,128)(2,1)S(1)} %multiply_convert_fusion.6) | copy-start | bytes 3145732
  373.0 261.4 %copy-start.99 = (bf16[256,32]{0,1:T(8,128)(2,1)}, bf16[256,32]{0,1:T(8,128)(2,1)S(1)}, u32[]{:S(2)}) copy-start(bf16[256,32]{0,1:T(8,128)(2,1)S(1)} %convolution_convert_fusion.3) | copy-start | bytes 49156
  639.7 137.0 %copy-start.37 = (bf16[256,2816]{1,0:T(8,128)(2,1)}, bf16[256,2816]{1,0:T(8,128)(2,1)S(1)}, u32[]{:S(2)}) copy-start(bf16[256,2816]{1,0:T(8,128)(2,1)S(1)} %fusion.107) | copy-start | bytes 4325380
  776.7 175.6 %all-gather.38.cloned.1.call-start = ((), (), s32[]{:S(2)}) async-start(), calls=%async_computation.20 | async-start | bytes 13369344 | tf_op jit(solution)/shard_map/all_gather | solution.py:285
  777.4 228.5 %all-gather.40.cloned.1.call-start = ((), (), s32[]{:S(2)}) async-start(), calls=%async_computation.21 | async-start | bytes 2621440 | tf_op jit(solution)/shard_map/all_gather | solution.py:104
  801.4 157.4 %copy-start.25 = (bf16[256,2048]{1,0:T(8,128)(2,1)}, bf16[256,2048]{1,0:T(8,128)(2,1)S(1)}, u32[]{:S(2)}) copy-start(bf16[256,2048]{1,0:T(8,128)(2,1)S(1)} %multiply_convert_fusion.5) | copy-start | bytes 3145732
  801.9 156.9 %copy-start.84 = (bf16[256,48]{0,1:T(8,128)(2,1)}, bf16[256,48]{0,1:T(8,128)(2,1)S(1)}, u32[]{:S(2)}) copy-start(bf16[256,48]{0,1:T(8,128)(2,1)S(1)} %convolution_convert_fusion) | copy-start | bytes 73732
  961.2 92.1 %all-gather.26.cloned.1.call-start = ((), (), s32[]{:S(2)}) async-start(), calls=%async_computation.7 | async-start | bytes 2621440 | tf_op jit(solution)/shard_map/all_gather | solution.py:103
  966.4 162.2 %all-gather.42.cloned.1.call-start = ((), (), s32[]{:S(2)}) async-start(), calls=%async_computation.22 | async-start | bytes 4456448 | tf_op jit(solution)/shard_map/all_gather | solution.py:288
  966.9 306.3 %all-gather.46.cloned.1.call-start = ((), (), s32[]{:S(2)}) async-start(), calls=%async_computation.24 | async-start | bytes 12255232 | tf_op jit(solution)/shard_map/all_gather | solution.py:292
  967.7 328.5 %all-reduce.20.cloned.1.call-start = ((), (), s32[]{:S(2)}) async-start(), calls=%async_computation.8 | async-start | bytes 4194304 | tf_op jit(solution)/shard_map/psum | solution.py:92
  967.8 42.0 %copy-start.22 = (bf16[256,4,2,128]{0,3,2,1:T(8,128)(2,1)}, bf16[256,4,2,128]{0,3,2,1:T(8,128)(2,1)S(1)}, u32[]{:S(2)}) copy-start(bf16[256,4,2,128]{0,3,2,1:T(8,128)(2,1)S(1)} %pad_maximum_fusion.17) | copy-start | bytes 1572868
  1005.9 47.4 %copy-start.125 = (bf16[256,13]{0,1:T(8,128)(2,1)S(1)}, bf16[256,13]{0,1:T(8,128)(2,1)}, u32[]{:S(2)}) copy-start(bf16[256,13]{0,1:T(8,128)(2,1)} %copy-done.124) | copy-start | bytes 19972
  1089.4 44.1 %copy-start.42 = (bf16[4,256,256]{1,2,0:T(8,128)(2,1)}, bf16[4,256,256]{1,2,0:T(8,128)(2,1)S(1)}, u32[]{:S(2)}) copy-start(bf16[4,256,256]{1,2,0:T(8,128)(2,1)S(1)} %multiply_convert_fusion.11) | copy-start | bytes 1572868
  1133.5 416.8 %all-gather.44.cloned.1.call-start = ((), (), s32[]{:S(2)}) async-start(), calls=%async_computation.23 | async-start | bytes 24510464 | tf_op jit(solution)/shard_map/all_gather | solution.py:289
  1136.3 464.7 %all-reduce.22.cloned.1.call-start = ((), (), s32[]{:S(2)}) async-start(), calls=%async_computation.9 | async-start | bytes 4194304 | tf_op jit(solution)/shard_map/psum | solution.py:96
  1137.7 425.4 %copy-start.107 = (bf16[16,256]{1,0:T(8,128)(2,1)}, bf16[16,256]{1,0:T(8,128)(2,1)S(1)}, u32[]{:S(2)}) copy-start(bf16[16,256]{1,0:T(8,128)(2,1)S(1)} %fusion.174) | copy-start | bytes 24580
  1137.7 158.5 %copy-start.5 = (f32[256,2048]{1,0:T(8,128)S(1)}, f32[256,2048]{1,0:T(8,128)}, u32[]{:S(2)}) copy-start(f32[256,2048]{1,0:T(8,128)} %copy-done.4) | copy-start | bytes 6291460
  1300.0 261.0 %copy-start.29 = (bf16[256,2048]{1,0:T(8,128)(2,1)}, bf16[256,2048]{1,0:T(8,128)(2,1)S(1)}, u32[]{:S(2)}) copy-start(bf16[256,2048]{1,0:T(8,128)(2,1)S(1)} %multiply_convert_fusion.4) | copy-start | bytes 3145732
  1300.5 260.6 %copy-start.101 = (bf16[256,32]{0,1:T(8,128)(2,1)}, bf16[256,32]{0,1:T(8,128)(2,1)S(1)}, u32[]{:S(2)}) copy-start(bf16[256,32]{0,1:T(8,128)(2,1)S(1)} %convolution_convert_fusion.2) | copy-start | bytes 49156
  1580.0 247.0 %reduce-scatter.13.cloned.1.call-start = ((), (), s32[]{:S(2)}) async-start(), calls=%async_computation.10 | async-start | bytes 10485760 | tf_op jit(solution)/shard_map/reduce_scatter | solution.py:224
  1682.0 146.5 %copy-start.53 = (f32[256,64]{0,1:T(8,128)S(1)}, f32[256,64]{0,1:T(8,128)}, u32[]{:S(2)}) copy-start(f32[256,64]{0,1:T(8,128)} %copy-done.51) | copy-start | bytes 196612
  1682.0 146.5 %copy-start.63 = (f32[256,64]{0,1:T(8,128)S(1)}, f32[256,64]{0,1:T(8,128)}, u32[]{:S(2)}) copy-start(f32[256,64]{0,1:T(8,128)} %get-tuple-element.1285) | copy-start | bytes 196612
  1682.0 146.5 %copy-start.1 = (f32[256,4,2,128]{0,3,2,1:T(8,128)S(1)}, f32[256,4,2,128]{0,3,2,1:T(8,128)}, u32[]{:S(2)}) copy-start(f32[256,4,2,128]{0,3,2,1:T(8,128)} %get-tuple-element.408) | copy-start | bytes 3145732
  1682.1 181.8 %all-reduce.24.cloned.1.call-start = ((), (), s32[]{:S(2)}) async-start(), calls=%async_computation.11 | async-start | bytes 4194304 | tf_op jit(solution)/shard_map/psum | solution.py:96
  1840.9 73.1 %all-reduce.26.cloned.1.call-start = ((), (), s32[]{:S(2)}) async-start(), calls=%async_computation.12 | async-start | bytes 4194304 | tf_op jit(solution)/shard_map/psum | solution.py:96
  1891.4 249.3 %reduce-scatter.15.cloned.1.call-start = ((), (), s32[]{:S(2)}) async-start(), calls=%async_computation.13 | async-start | bytes 10485760 | tf_op jit(solution)/shard_map/reduce_scatter | solution.py:224
  1995.8 867.0 %all-reduce.28.cloned.1.call-start = ((), (), s32[]{:S(2)}) async-start(), calls=%async_computation.26 | async-start | bytes 80740352
  2022.6 119.7 %copy-start = (f32[256,4,2,128]{0,3,2,1:T(8,128)S(1)}, f32[256,4,2,128]{0,3,2,1:T(8,128)}, u32[]{:S(2)}) copy-start(f32[256,4,2,128]{0,3,2,1:T(8,128)} %get-tuple-element.411) | copy-start | bytes 3145732
  2173.4 772.1 %all-reduce.30.cloned.1.call-start = ((), (), s32[]{:S(2)}) async-start(), calls=%async_computation.27 | async-start | bytes 8388608 | tf_op jit(solution)/shard_map/psum | solution.py:92
  2192.4 809.9 %reduce-scatter.19.cloned.1.call-start = ((), (), s32[]{:S(2)}) async-start(), calls=%async_computation.25 | async-start | bytes 6488064
  2939.5 129.0 %reduce-scatter.17.cloned.1.call-start = ((), (), s32[]{:S(2)}) async-start(), calls=%async_computation.14 | async-start | bytes 6488064 | tf_op jit(solution)/shard_map/reduce_scatter | solution.py:599
  (128 other events, 691.6 us)
Sparse Core Ops, SparseCore 0:
  11.4 152.6 all-gather.27
  174.9 44.5 all-gather.29
  221.6 45.2 all-gather.23
  270.1 72.7 all-gather.31
  347.8 21.7 all-reduce.15
  372.6 250.9 all-gather.33
  627.3 140.5 all-gather.35
  776.8 20.7 all-reduce.17
  800.4 151.8 all-gather.37
  961.3 44.5 all-gather.39
  1008.0 45.2 all-gather.25
  1055.9 72.6 all-gather.41
  1131.9 141.3 all-gather.45
  1275.5 20.7 all-reduce.19
  1299.3 251.0 all-gather.43
  1580.1 20.8 all-reduce.21
  1682.2 144.7 reduce-scatter.12
  1841.0 22.8 all-reduce.23
  1891.5 22.4 all-reduce.25
  1995.9 144.7 reduce-scatter.14
  2173.5 689.2 all-reduce.27
  2865.9 29.2 all-reduce.29
  2939.6 62.7 reduce-scatter.18
  3005.2 63.2 reduce-scatter.16
where the time goes:
time: 3090 us; the launch traced here: 3080 us
  waiting for transfers between devices  2400 us (78%)
  matrix products  286 us (9%)
  local copies, waits for them, and re-layouts  253 us (8%)
  other arithmetic  70.7 us (2%)
  blocking collectives  39.1 us (1%)
    unnamed x26, waiting for transfers between devices  720 us
    all_gather x2, waiting for transfers between devices, shards(): lax.all_gather(gate_up_weight[current_layer_index], ('fsdp', 'ctx'), axis...  500 us
    all_gather x2, waiting for transfers between devices, shards(): lax.all_gather(query_key_value_weight[current_layer_index], ('fsdp', 'ctx...  301 us
    all_gather x2, waiting for transfers between devices, shards(): lax.all_gather(down_weight[current_layer_index], ('fsdp', 'ctx'), axis=0,...  264 us
    reduce_scatter x2, waiting for transfers between devices, attend_backward(): lax.psum_scatter(key_terms, 'ctx', scatter_dimension=0, tiled=True)  263 us
    dot_general x56, matrix products, einsum_single(): jnp.einsum(formula, left_side, right_side, preferred_element_type=jnp.flo...  185 us
    unnamed x312, local copies, waits for them, and re-layouts  130 us
    all_gather x2, waiting for transfers between devices, attend_forward(): lax.all_gather(key_vectors, 'ctx', axis=0, tiled=True)  86.9 us
  transfers between devices with their start and end apart: 24, of which 23 were waited for; matrix products, arithmetic and copies ran while one was open for 10% of the time, Pallas kernels for 0%

commit v1 on v0

v1 whole, which is shorter than its diff:
```python
import functools
import math

import jax
import jax.numpy as jnp
from jax import lax
from jax.experimental import pallas as pl
from jax.experimental.pallas import tpu as pltpu
from jax.sharding import PartitionSpec as P

HD = 128
VD = 256
NSEG = 13
EPSILON = 1e-05
ADAPTER_SCALE = 0.5
NEGATIVE_BIG = -1e30
MESH = pl.DeviceIdType.MESH
BF = jnp.bfloat16
F32 = jnp.float32


class Place:
    def __init__(self, n):
        self.n, self.h = n, n // 2
        self.f, self.c, self.t = lax.axis_index("fsdp"), lax.axis_index("ctx"), lax.axis_index("tp")
        self.f_hi, self.f_lo = self.f // 2, self.f % 2
        self.c_hi, self.c_lo = self.c // self.h, self.c % self.h
        self.q = self.f_lo * self.h + self.c_lo
        self.pos = self.f_lo * (n - 1) + (1 - 2 * self.f_lo) * self.c_lo

    def ring(self, k):
        n, h = self.n, self.h
        p = lax.rem(self.pos + k + 2 * n, n)
        low = p // h
        column = (1 - low) * p + low * (n - 1 - p)
        device = {"fsdp": self.f_hi * 2 + low, "ctx": self.c_hi * h + column}
        return low * h + column, device


def enter(place):
    bar = pltpu.get_barrier_semaphore()
    for device in (place.ring(1)[1], place.ring(-1)[1], {"tp": 1 - place.t}):
        pl.semaphore_signal(bar, inc=1, device_id=device, device_id_type=MESH)
    pl.semaphore_wait(bar, 3)


def remote(src, dst, send, recv, device):
    copy = pltpu.make_async_remote_copy(
        src_ref=src, dst_ref=dst, send_sem=send, recv_sem=recv, device_id=device, device_id_type=MESH
    )
    copy.start()
    return copy


class Gather:
    def __init__(self, place, x, send_r, recv_r, send_l, recv_l, core_send, core_recv):
        self.place, self.x = place, x
        self.sems = (send_r, recv_r, send_l, recv_l, core_send, core_recv)
        self.to_right, self.to_left, self.across = [], [], []

    @staticmethod
    def semaphores(n):
        dma = pltpu.SemaphoreType.DMA
        return [dma((n // 2,))] * 4 + [dma((n,))] * 2

    def _pass_on(self, s):
        place, x = self.place, self.x
        send_r, recv_r, send_l, recv_l = self.sems[:4]
        rows, half, t = x.shape[2], place.n // 2, place.t
        top = rows // 2
        part_r = pl.ds(0, top) if s == half - 1 else pl.ds(0, rows)
        part_l = pl.ds(top, top) if s == half - 1 else pl.ds(0, rows)
        right_at = x.at[place.ring(-s)[0], t, part_r]
        left_at = x.at[place.ring(s)[0], t, part_l]
        self.to_right.append(remote(right_at, right_at, send_r.at[s], recv_r.at[s], place.ring(1)[1]))
        self.to_left.append(remote(left_at, left_at, send_l.at[s], recv_l.at[s], place.ring(-1)[1]))

    def _cross(self, q):
        core_send, core_recv = self.sems[4:]
        slot, at = len(self.across), self.x.at[q, self.place.t]
        other = {"tp": 1 - self.place.t}
        self.across.append(remote(at, at, core_send.at[slot], core_recv.at[slot], other))

    def begin(self):
        self._pass_on(0)
        self._cross(self.place.q)

    def chunks(self):
        place, half = self.place, self.place.n // 2
        self.across[0].wait_recv()
        yield place.q
        for s in range(half):
            self.to_right[s].wait_recv()
            self.to_left[s].wait_recv()
            arrived = [place.ring(half)[0]] if s == half - 1 else [place.ring(-s - 1)[0], place.ring(s + 1)[0]]
            if s < half - 1:
                self._pass_on(s + 1)
            first = len(self.across)
            for q in arrived:
                self._cross(q)
            for i, q in enumerate(arrived):
                self.across[first + i].wait_recv()
                yield q

    def finish(self):
        for copy in self.to_right + self.to_left + self.across:
            copy.wait_send()


def by_rows(count, body, step=16):
    def one(i, carry):
        body(pl.ds(pl.multiple_of(i * step, step), step))
        return carry

    lax.fori_loop(0, count // step, one, 0)


class Reduce:
    def __init__(self, place, p, from_core, in_r, in_l, send_r, recv_r, send_l, recv_l, core_send, core_recv):
        self.place, self.p, self.from_core, self.in_r, self.in_l = place, p, from_core, in_r, in_l
        self.sems = (send_r, recv_r, send_l, recv_l, core_send, core_recv)
        half = place.n // 2
        self.order = [half] + [k for j in range(half - 1, 0, -1) for k in (j, -j)] + [0]
        self.chips = {k: place.ring(k)[0] for k in self.order}
        self.across, self.to_right, self.to_left = {}, [], []

    @staticmethod
    def scratch(n, rows, width):
        dma = pltpu.SemaphoreType.DMA
        wide = [pltpu.VMEM((n, rows, width), BF)] + [pltpu.VMEM((n // 2, rows, width), BF)] * 2
        return wide + [dma((n // 2,))] * 4 + [dma((n,))] * 2

    def offer(self, k):
        core_send, core_recv = self.sems[4:]
        slot, q, t = len(self.across), self.chips[k], self.place.t
        self.across[k] = remote(
            self.p.at[q, 1 - t], self.from_core.at[q], core_send.at[slot], core_recv.at[slot], {"tp": 1 - t}
        )

    def _local(self, k, at):
        q = self.chips[k]
        return self.p[q, self.place.t, at].astype(F32) + self.from_core[q, at].astype(F32)

    def _add(self, k, start, count, extra=None):
        def body(at):
            whole = pl.ds(pl.multiple_of(start + at.start, 16), at.size)
            total = self._local(k, whole)
            if extra is not None:
                total = total + extra[whole].astype(F32)
            self.from_core[self.chips[k], whole] = total.astype(BF)

        by_rows(count, body)

    def far(self):
        send_r, recv_r, send_l, recv_l = self.sems[:4]
        place, half = self.place, self.place.n // 2
        rows = self.p.shape[2]
        top = rows // 2
        self.across[half].wait_recv()
        self._add(half, 0, rows)
        low, high = pl.ds(0, top), pl.ds(top, top)
        sums = self.from_core.at[self.chips[half]]
        right, left = place.ring(1)[1], place.ring(-1)[1]
        self.to_right.append(remote(sums.at[low], self.in_r.at[0, low], send_r.at[0], recv_r.at[0], right))
        self.to_left.append(remote(sums.at[high], self.in_l.at[0, high], send_l.at[0], recv_l.at[0], left))

    def near(self, s):
        send_r, recv_r, send_l, recv_l = self.sems[:4]
        place, k = self.place, self.place.n // 2 - s
        rows = self.p.shape[2]
        top = rows // 2
        self.across[k].wait_recv()
        self.across[-k].wait_recv()
        if s == 1:
            self._add(k, top, top)
            self._add(-k, 0, top)
        start = 0 if s == 1 else None
        self.to_right[-1].wait_recv()
        self._add(k, 0, top if s == 1 else rows, self.in_r.at[s - 1])
        self.to_right.append(
            remote(self.from_core.at[self.chips[k]], self.in_r.at[s], send_r.at[s], recv_r.at[s], place.ring(1)[1])
        )
        self.to_left[-1].wait_recv()
        self._add(-k, top if s == 1 else 0, top if s == 1 else rows, self.in_l.at[s - 1])
        self.to_left.append(
            remote(self.from_core.at[self.chips[-k]], self.in_l.at[s], send_l.at[s], recv_l.at[s], place.ring(-1)[1])
        )

    def end(self, use):
        half = self.place.n // 2
        self.across[0].wait_recv()
        self.to_right[-1].wait_recv()
        self.to_left[-1].wait_recv()

        def body(at):
            use(at, self._local(0, at) + self.in_r[half - 1, at].astype(F32) + self.in_l[half - 1, at].astype(F32))

        by_rows(self.p.shape[2], body)

    def finish(self):
        for copy in self.to_right + self.to_left + list(self.across.values()):
            copy.wait_send()

    def run(self, use, before=None):
        for k in self.order:
            self.offer(k)
        self.far()
        for s in range(1, self.place.n // 2):
            self.near(s)
        if before is not None:
            before()
        self.end(use)


def rs_kernel(n, p_ref, out_ref, *scratch):
    place = Place(n)
    reduce = Reduce(place, p_ref, *scratch)
    enter(place)

    def use(at, total):
        out_ref[at] = total

    reduce.run(use)
    reduce.finish()


def group_reduce(p, n, collective):
    vmem = pl.BlockSpec(memory_space=pltpu.VMEM)
    rows, width = p.shape[2:]
    return pl.pallas_call(
        functools.partial(rs_kernel, n),
        out_shape=jax.ShapeDtypeStruct((rows, width), F32),
        in_specs=[vmem],
        out_specs=vmem,
        scratch_shapes=Reduce.scratch(n, rows, width),
        compiler_params=pltpu.CompilerParams(
            collective_id=collective, has_side_effects=True, vmem_limit_bytes=60 << 20
        ),
    )(p)


def mm(a, b):
    return jnp.dot(a, b, preferred_element_type=F32)


def mm_t(a, b):
    return lax.dot_general(a, b, (((1,), (1,)), ((), ())), preferred_element_type=F32)


def t_mm(a, b):
    return lax.dot_general(a, b, (((0,), (0,)), ((), ())), preferred_element_type=F32)


def rms_scale(values):
    return lax.rsqrt(jnp.mean(values * values, axis=-1, keepdims=True) + EPSILON)


def norm_back(grad_normed, inputs, scale_rows, gain):
    unit = inputs * scale_rows
    scaled = grad_normed * gain
    return scale_rows * (scaled - unit * jnp.mean(scaled * unit, axis=-1, keepdims=True))


def tiles(count, width, body):
    def one(j, carry):
        body(pl.ds(pl.multiple_of(j * width, width), width))
        return carry

    lax.fori_loop(0, count // width, one, 0)


def tile_of(count):
    return 256 if count % 256 == 0 else 128


def turn(v, cosine, sine):
    return v * cosine + pltpu.roll(v, HD // 2, 1) * sine


def block_diagonal(out, parts, rank, width):
    out[...] = jnp.zeros(out.shape, out.dtype)
    for i in range(parts[1]):
        out[i * rank : (i + 1) * rank, i * width : (i + 1) * width] = parts[0][i * rank : (i + 1) * rank, :]


def write_norm(x_rows, source, gain):
    def body(at):
        v = source[at]
        x_rows[at] = (v * rms_scale(v) * gain[...]).astype(BF)

    by_rows(source.shape[0], body)


ROW_BLOCK = 128
KEY_STEP = 256


def row_blocks(tree, body):
    for j in range(tree // KEY_STEP):

        def one(i, carry, j=j):
            body(pl.ds(pl.multiple_of(j * KEY_STEP + i * ROW_BLOCK, ROW_BLOCK), ROW_BLOCK), (j + 1) * KEY_STEP)
            return carry

        lax.fori_loop(0, KEY_STEP // ROW_BLOCK, one, 0)


def seen(rows, keys, query_bits, key_bits):
    shared = (query_bits[rows] & key_bits[:, :keys]) != 0
    i = rows.start + lax.broadcasted_iota(jnp.int32, (ROW_BLOCK, keys), 0)
    j = lax.broadcasted_iota(jnp.int32, (ROW_BLOCK, keys), 1)
    return shared & (j <= i)


def attention_forward(
    n, layer, part, rank,
    residual, gain, w_hbm, a_model, a_head, cosine, sine, query_bits, key_bits, lam,
    middle, x_hbm, queries, keys, values, small, log_total, mixed, headed, side,
    x, p, w, raised, copy_sems, *sems,
):
    place = Place(n)
    chip_rows, width = 2 * x_hbm.shape[2], x_hbm.shape[3]
    tree = n * chip_rows
    load = pltpu.make_async_copy(w_hbm, w, copy_sems.at[0])
    load.start()
    gather, reduce = Gather(place, x, *sems[:6]), Reduce(place, p, *sems[6:])
    write_norm(x.at[place.q, place.t], residual, gain)
    block_diagonal(raised, (a_head[rank : 4 * rank], 3), rank, VD)
    enter(place)
    gather.begin()
    load.wait()

    def project(q):
        rows = pl.ds(pl.multiple_of(q * chip_rows, chip_rows), chip_rows)
        v = x[q].reshape(chip_rows, width)
        low = mm_t(v, a_model[: 3 * rank]).astype(BF)
        small[rows] = low
        for i, out in enumerate((queries, keys, values)):
            at = slice(i * VD, (i + 1) * VD)
            made = mm(v, w[:, at]) + ADAPTER_SCALE * mm(low, raised[:, at])
            if i < 2:
                for c in range(2):
                    half = slice(c * HD, (c + 1) * HD)
                    out[rows, half] = turn(made[:, half], cosine[rows], sine[rows]).astype(BF)
            else:
                out[rows] = made.astype(BF)

    for q in gather.chunks():
        project(q)
    keep = pltpu.make_async_copy(x, x_hbm, copy_sems.at[1])
    keep.start()
    score_scale = HD ** (-0.5)
    weight = lam[...]

    def attend(rows, count):
        visible = seen(rows, count, query_bits, key_bits)
        both = []
        for c in range(2):
            at = slice(c * HD, (c + 1) * HD)
            scores = mm_t(queries[rows, at], keys[:count, at]) * score_scale
            scores = jnp.where(visible, scores, NEGATIVE_BIG)
            top = jnp.max(scores, axis=-1, keepdims=True)
            raw = jnp.exp(scores - top)
            total = jnp.sum(raw, axis=-1, keepdims=True)
            log_total[rows, c : c + 1] = top + jnp.log(total)
            both.append(raw * (1.0 / total))
        mix = mm((both[0] - weight * both[1]).astype(BF), values[:count])
        mixed[rows] = mix
        head = (mix * rms_scale(mix) * keep_factor(layer)).astype(BF)
        headed[rows] = head
        side[rows] = mm_t(head, a_head[:rank]).astype(BF)

    row_blocks(tree, attend)

    for k in reduce.order:
        q = reduce.chips[k]
        rows = pl.ds(pl.multiple_of(q * chip_rows, chip_rows), chip_rows)
        head, low = headed[rows], side[rows]

        def out_tile(at):
            made = mm_t(head, w[at, 3 * VD :]) + ADAPTER_SCALE * mm(low, a_model[9 * rank : 10 * rank, at])
            p[q, :, :, at] = (made * part).astype(BF).reshape(2, chip_rows // 2, at.size)

        tiles(width, 512, out_tile)
        reduce.offer(k)
        if k == reduce.order[2]:
            reduce.far()
    for s in range(1, n // 2):
        reduce.near(s)

    def use(at, total):
        middle[at] = residual[at] + total

    reduce.end(use)
    keep.wait()
    gather.finish()
    reduce.finish()


def ffn_forward(
    n, units, rank,
    residual, gain, w_hbm, a_model, e_model,
    following, x_hbm, gates, ups, hidden, small, side,
    x, p, w, raised, copy_sems, *sems,
):
    place = Place(n)
    chip_rows, width = 2 * x_hbm.shape[2], x_hbm.shape[3]
    tree = n * chip_rows
    load = pltpu.make_async_copy(w_hbm, w, copy_sems.at[0])
    load.start()
    gather, reduce = Gather(place, x, *sems[:6]), Reduce(place, p, *sems[6:])
    write_norm(x.at[place.q, place.t], residual, gain)
    block_diagonal(raised, (e_model, 2), rank, units)
    enter(place)
    gather.begin()
    load.wait()
    step = tile_of(units)

    for q in gather.chunks():
        rows = pl.ds(pl.multiple_of(q * chip_rows, chip_rows), chip_rows)
        v = x[q].reshape(chip_rows, width)
        low = mm_t(v, a_model[4 * rank : 6 * rank]).astype(BF)
        small[rows] = low

        def unit_tile(at):
            up_at = pl.ds(pl.multiple_of(units + at.start, step), step)
            gate = mm(v, w[:, at]) + ADAPTER_SCALE * mm(low, raised[:, at])
            up = mm(v, w[:, up_at]) + ADAPTER_SCALE * mm(low, raised[:, up_at])
            gates[rows, at] = gate.astype(BF)
            ups[rows, at] = up.astype(BF)
            hidden[rows, at] = (gate / (1.0 + jnp.exp(-gate)) * up).astype(BF)

        tiles(units, step, unit_tile)
        made_hidden = hidden[rows]
        low_hidden = mm_t(made_hidden, e_model[2 * rank : 3 * rank]).astype(BF)
        side[rows] = low_hidden

        def out_tile(at):
            made = mm_t(made_hidden, w[at, 2 * units :])
            made = made + ADAPTER_SCALE * mm(low_hidden, a_model[10 * rank : 11 * rank, at])
            p[q, :, :, at] = made.astype(BF).reshape(2, chip_rows // 2, at.size)

        tiles(width, 512, out_tile)

    keep = pltpu.make_async_copy(x, x_hbm, copy_sems.at[1])
    keep.start()

    def use(at, total):
        following[at] = residual[at] + total

    reduce.run(use)
    keep.wait()
    gather.finish()
    reduce.finish()


def ffn_backward(
    n, units, rank,
    grad, middle, gain, w_hbm, a_model, e_model, x_hbm, gates, ups, hidden, small, side,
    grad_out, grad_up_down, grad_in, grad_units, grad_e2,
    x, p, w, kept, dgu, dsmall, dside, raised, copy_sems, *sems,
):
    place = Place(n)
    chip_rows, width = 2 * x_hbm.shape[2], x_hbm.shape[3]
    tree = n * chip_rows
    load = pltpu.make_async_copy(w_hbm, w, copy_sems.at[0])
    load.start()
    fetch = pltpu.make_async_copy(x_hbm, kept, copy_sems.at[1])
    fetch.start()
    gather, reduce = Gather(place, x, *sems[:6]), Reduce(place, p, *sems[6:])

    def own(at):
        x[place.q, place.t, at] = grad[at].astype(BF)

    by_rows(grad.shape[0], own)
    block_diagonal(raised, (e_model, 2), rank, units)
    enter(place)
    gather.begin()
    load.wait()
    step = tile_of(units)

    for q in gather.chunks():
        rows = pl.ds(pl.multiple_of(q * chip_rows, chip_rows), chip_rows)
        v = x[q].reshape(chip_rows, width)
        low = (ADAPTER_SCALE * mm_t(v, a_model[10 * rank : 11 * rank])).astype(BF)
        dside[rows] = low

        def unit_tile(at):
            up_at = pl.ds(pl.multiple_of(units + at.start, step), step)
            down_at = pl.ds(pl.multiple_of(2 * units + at.start, step), step)
            dhidden = mm(v, w[:, down_at]) + mm(low, e_model[2 * rank : 3 * rank, at])
            gate, up = gates[rows, at].astype(F32), ups[rows, at].astype(F32)
            sig = 1.0 / (1.0 + jnp.exp(-gate))
            dgu[rows, at] = (dhidden * up * sig * (1.0 + gate * (1.0 - sig))).astype(BF)
            dgu[rows, up_at] = (dhidden * gate * sig).astype(BF)

        tiles(units, step, unit_tile)
        back = dgu[rows]
        low_back = (ADAPTER_SCALE * mm_t(back, raised[...])).astype(BF)
        dsmall[rows] = low_back

        def out_tile(at):
            made = mm_t(back, w[at, : 2 * units]) + mm(low_back, a_model[4 * rank : 6 * rank, at])
            p[q, :, :, at] = made.astype(BF).reshape(2, chip_rows // 2, at.size)

        tiles(width, 512, out_tile)

    def use(at, total):
        inputs = middle[at]
        grad_out[at] = grad[at] + norm_back(total, inputs, rms_scale(inputs), gain[...])

    def adapters():
        fetch.wait()

        def model_tile(at):
            flat = x[:, :, :, at].reshape(tree, at.size)
            grad_up_down[:, at] = (ADAPTER_SCALE * t_mm(side[...], flat)).astype(BF)
            flat = kept[:, :, :, at].reshape(tree, at.size)
            grad_in[:, at] = t_mm(dsmall[...], flat).astype(BF)

        tiles(width, 256, model_tile)

        def unit_tile(at):
            up_at = pl.ds(pl.multiple_of(units + at.start, step), step)
            grad_units[:rank, at] = ADAPTER_SCALE * t_mm(small[...], dgu[:, at])[:rank]
            grad_units[rank:, at] = ADAPTER_SCALE * t_mm(small[...], dgu[:, up_at])[rank:]
            grad_e2[:, at] = t_mm(dside[...], hidden[:, at])

        tiles(units, step, unit_tile)

    reduce.run(use, adapters)
    gather.finish()
    reduce.finish()


def attention_backward(
    n, layer, part, rank,
    grad, residual, gain, w_hbm, a_model, a_head, cosine, sine, query_bits, key_bits, lam,
    x_hbm, queries, keys, values, small, log_total, mixed, headed, side,
    grad_out, grad_a9, grad_in, grad_head,
    x, p, w, dmixed, dq, dk, dv, dprojected, dsmall, dside, raised, copy_sems, *sems,
):
    place = Place(n)
    chip_rows, width = 2 * x_hbm.shape[2], x_hbm.shape[3]
    tree = n * chip_rows
    load = pltpu.make_async_copy(w_hbm, w, copy_sems.at[0])
    load.start()
    gather, reduce = Gather(place, x, *sems[:6]), Reduce(place, p, *sems[6:])

    def own(at):
        x[place.q, place.t, at] = grad[at].astype(BF)

    by_rows(grad.shape[0], own)
    block_diagonal(raised, (a_head[rank : 4 * rank], 3), rank, VD)
    enter(place)
    gather.begin()
    dk[...] = jnp.zeros(dk.shape, F32)
    dv[...] = jnp.zeros(dv.shape, F32)
    load.wait()

    for q in gather.chunks():
        rows = pl.ds(pl.multiple_of(q * chip_rows, chip_rows), chip_rows)
        v = x[q].reshape(chip_rows, width)
        low = (ADAPTER_SCALE * mm_t(v, a_model[9 * rank : 10 * rank])).astype(BF)
        dside[rows] = low
        dheaded = mm(v, w[:, 3 * VD :]) + mm(low, a_head[:rank])
        inputs = mixed[rows]
        dmixed[rows] = norm_back(dheaded, inputs, rms_scale(inputs), keep_factor(layer)).astype(BF)

    def out_gradient(at):
        flat = x[:, :, :, at].reshape(tree, at.size)
        grad_a9[:, at] = (ADAPTER_SCALE * part * t_mm(side[...], flat)).astype(BF)

    tiles(width, 256, out_gradient)
    gather.finish()
    fetch = pltpu.make_async_copy(x_hbm, x, copy_sems.at[1])
    fetch.start()
    score_scale = HD ** (-0.5)
    weight = lam[...]

    def attend(rows, count):
        visible = seen(rows, count, query_bits, key_bits)
        dmix = dmixed[rows]
        dweights = mm_t(dmix, values[:count])
        both = []
        for c in range(2):
            at = slice(c * HD, (c + 1) * HD)
            scores = mm_t(queries[rows, at], keys[:count, at]) * score_scale
            probability = jnp.exp(jnp.where(visible, scores - log_total[rows, c : c + 1], NEGATIVE_BIG))
            both.append(probability)
            weighted = probability * dweights
            dscores = weighted - probability * jnp.sum(weighted, axis=-1, keepdims=True)
            dscores = (dscores * -weight if c else dscores).astype(BF)
            dq[rows, at] = mm(dscores, keys[:count, at])
            dk[:count, at] += t_mm(dscores, queries[rows, at])
        dv[:count] += t_mm((both[0] - weight * both[1]).astype(BF), dmix)

    row_blocks(tree, attend)

    for k in reduce.order:
        q = reduce.chips[k]
        rows = pl.ds(pl.multiple_of(q * chip_rows, chip_rows), chip_rows)
        for i, source in enumerate((dq, dk)):
            for c in range(2):
                half = slice(c * HD, (c + 1) * HD)
                turned = turn(source[rows, half] * score_scale, cosine[rows], -sine[rows])
                dprojected[rows, i * VD + c * HD : i * VD + (c + 1) * HD] = turned.astype(BF)
        dprojected[rows, 2 * VD :] = dv[rows].astype(BF)
        back = dprojected[rows]
        low_back = (ADAPTER_SCALE * mm_t(back, raised[...])).astype(BF)
        dsmall[rows] = low_back

        def out_tile(at):
            made = mm_t(back, w[at, : 3 * VD]) + mm(low_back, a_model[: 3 * rank, at])
            p[q, :, :, at] = (made * part).astype(BF).reshape(2, chip_rows // 2, at.size)

        tiles(width, 512, out_tile)
        reduce.offer(k)
        if k == reduce.order[2]:
            reduce.far()
    for s in range(1, n // 2):
        reduce.near(s)

    fetch.wait()

    def model_tile(at):
        flat = x[:, :, :, at].reshape(tree, at.size)
        grad_in[:, at] = (part * t_mm(dsmall[...], flat)).astype(BF)

    tiles(width, 256, model_tile)
    grad_head[:rank] = part * t_mm(dside[...], headed[...])
    for i in range(3):
        made = t_mm(small[...], dprojected[:, i * VD : (i + 1) * VD])[i * rank : (i + 1) * rank]
        grad_head[(i + 1) * rank : (i + 2) * rank] = ADAPTER_SCALE * part * made

    def use(at, total):
        inputs = residual[at]
        grad_out[at] = grad[at] + norm_back(total, inputs, rms_scale(inputs), gain[...])

    reduce.end(use)
    reduce.finish()


def call(kernel, collective, ins, outs, scratch):
    spec = lambda hbm: pl.BlockSpec(memory_space=pl.ANY if hbm else pltpu.VMEM)
    return pl.pallas_call(
        kernel,
        out_shape=[jax.ShapeDtypeStruct(shape, kind) for shape, kind, _ in outs],
        in_specs=[spec(hbm) for _, hbm in ins],
        out_specs=[spec(hbm) for _, _, hbm in outs],
        scratch_shapes=scratch,
        compiler_params=pltpu.CompilerParams(
            collective_id=collective, has_side_effects=True, vmem_limit_bytes=60 << 20
        ),
    )(*[array for array, _ in ins])


def line_bits(parent_row, seg):
    number = jnp.arange(NSEG)
    one = lambda x: lax.shift_left(jnp.ones_like(x), x)
    grand = jnp.sum(jnp.where(parent_row[:, None] == number[None, :], parent_row[None, :], 0), axis=1)
    line = one(number) | one(parent_row) | one(grand)
    mine = jnp.sum(jnp.where(seg[:, None] == number[None, :], line[None, :], 0), axis=1)
    return mine, one(seg)


def keep_factor(layer):
    return 0.2 + 0.6 * math.exp(-0.3 * layer)


def chips_of(nf, nc):
    h = nc // 2
    for f in range(nf):
        for c in range(nc):
            yield f * nc + c, (f // 2, f % 2, c // h, c % h)


def permute(x, nf, nc, target):
    h = nc // 2
    pairs = []
    for source, spot in chips_of(nf, nc):
        f_hi, f_lo, c_hi, c_lo = target(*spot)
        pairs.append((source, (f_hi * 2 + f_lo) * nc + c_hi * h + c_lo))
    return lax.ppermute(x, ("fsdp", "ctx"), pairs)


def swap_trees(x, nf, nc):
    return permute(x, nf, nc, lambda f_hi, f_lo, c_hi, c_lo: (f_hi, c_hi, f_lo, c_lo))


def spread_weights(blocks, q, g, nf, nc):
    n, h = nc, nc // 2
    rows, width = blocks.shape[1:]
    mine = jnp.zeros((n, rows, width), BF)
    for d in range(n):
        part = lax.dynamic_index_in_dim(blocks, q ^ d, 0, keepdims=False)
        if d:

            def exchange(f_hi, f_lo, c_hi, c_lo, d=d):
                to = (f_lo * h + c_lo) ^ d
                return f_hi, to // h, c_hi, to % h

            part = permute(part, nf, nc, exchange)
        mine = lax.dynamic_update_index_in_dim(mine, part, q ^ d, 0)
    gathered = jnp.zeros((nf, n, rows, width), BF)
    gathered = lax.dynamic_update_index_in_dim(gathered, mine, g, 0)
    partner = permute(mine, nf, nc, lambda a, b, c, d: (a, b, c ^ 1, d))
    gathered = lax.dynamic_update_index_in_dim(gathered, partner, g ^ 1, 0)
    for d in range(1, nf // 2):
        for e, held in ((0, mine), (1, partner)):
            moved = permute(held, nf, nc, lambda a, b, c, k, d=d: (a ^ d, b, c, k))
            gathered = lax.dynamic_update_index_in_dim(gathered, moved, g ^ (2 * d + e), 0)
    return gathered.reshape(nf * n * rows, width)


def shards(
    nf,
    nc,
    tokens,
    cotangent,
    segments,
    depths,
    parents,
    tree_adapter_index,
    layer_norm_gains,
    difference_lambda,
    query_key_value_weight,
    output_weight,
    gate_up_weight,
    down_weight,
    adapter_model_factors,
    adapter_hidden_factors,
):
    n = nc
    place = Place(n)
    q, t, g = place.q, place.t, place.f_hi * 2 + place.c_hi
    tokens_dev, width = tokens.shape
    rows = tokens_dev // 2
    tree = tokens_dev * n
    layers, weight_rows = query_key_value_weight.shape[:2]
    heads_tp = difference_lambda.shape[1]
    share = max(1, n // heads_tp)
    head = q // share
    hidden_tp = down_weight.shape[2]
    units = (hidden_tp + n * 128 - 1) // (n * 128) * 128
    rank, adapters = adapter_model_factors.shape[3], adapter_model_factors.shape[2]
    h = n // 2

    def swap_columns(x):
        lead = x.shape[:-1]
        cut = x.reshape(lead + (nf // 2, 2, 2, h * weight_rows))
        return jnp.swapaxes(cut, -3, -2).reshape(lead + (width,))

    of_tree = lax.all_gather(jnp.stack([segments, depths]), "ctx", axis=1, tiled=True)
    notes = jnp.concatenate([of_tree[0], of_tree[1], parents[0], tree_adapter_index])
    notes = swap_trees(notes, nf, nc)
    seg, dep = notes[:tree], notes[tree : 2 * tree]
    parent_row, slot = notes[2 * tree : 2 * tree + NSEG], notes[2 * tree + NSEG]
    own_tokens = lax.dynamic_slice_in_dim(tokens, t * rows, rows, 0)
    own_cotangent = lax.dynamic_slice_in_dim(cotangent, t * rows, rows, 0)
    residual = swap_columns(swap_trees(own_tokens, nf, nc)).astype(F32)
    own_cotangent = swap_columns(swap_trees(own_cotangent, nf, nc))

    query_bits, key_bits = line_bits(parent_row, seg)
    query_bits, key_bits = query_bits[:, None], key_bits[None, :]
    frequency = 10000.0 ** (-jnp.arange(HD // 2).astype(F32) / (HD // 2))
    angles = dep.astype(F32)[:, None] * frequency[None, :]
    cosine, sine = jnp.cos(angles), jnp.sin(angles)
    cosine = jnp.concatenate([cosine, cosine], axis=1)
    sine = jnp.concatenate([-sine, sine], axis=1)
    gains = swap_columns(layer_norm_gains)

    a_all = lax.dynamic_index_in_dim(adapter_model_factors, slot, 2, keepdims=False)
    e_all = lax.dynamic_index_in_dim(adapter_hidden_factors, slot, 2, keepdims=False)
    a_model = swap_columns(a_all).reshape(layers, 11 * rank, width)
    e_all = e_all.reshape(layers, 3 * rank, -1)
    head_at = (t * heads_tp + head) * VD

    heads_of = lax.dynamic_slice_in_dim(a_all, head_at, VD, 3)
    a_head = jnp.concatenate([heads_of[:, 3:4], heads_of[:, 6:9]], axis=1).reshape(layers, 4 * rank, VD)

    def unit_columns(x):
        x = lax.dynamic_slice_in_dim(x, t * hidden_tp, hidden_tp, x.ndim - 1)
        x = jnp.pad(x, ((0, 0),) * (x.ndim - 1) + ((0, n * units - hidden_tp),))
        return lax.dynamic_slice_in_dim(x, q * units, units, x.ndim - 1)

    e_model = unit_columns(e_all)

    def blocks_of(l):
        def heads(x):
            cut = x.reshape(weight_rows, heads_tp, VD).transpose(1, 0, 2)
            return jnp.repeat(cut, share, axis=0) if share > 1 else cut

        def unit(x):
            x = jnp.pad(x, ((0, 0), (0, n * units - hidden_tp)))
            return x.reshape(weight_rows, n, units).transpose(1, 0, 2)

        w = query_key_value_weight[l]
        v = gate_up_weight[l]
        attention = jnp.concatenate([heads(w[:, i]) for i in range(3)] + [heads(output_weight[l])], axis=2)
        forward = jnp.concatenate([unit(v[:, 0]), unit(v[:, 1]), unit(down_weight[l])], axis=2)
        return attention, forward

    weights = []
    for l in range(layers):
        attention, forward = blocks_of(l)
        weights.append((spread_weights(attention, q, g, nf, nc), spread_weights(forward, q, g, nf, nc)))

    part = 1.0 / share
    calls = [0]
    whole_x = ((n, 2, rows, width), BF)
    sems = Gather.semaphores(n) + Reduce.scratch(n, rows, width)
    pair = pltpu.SemaphoreType.DMA((2,))
    vmem = lambda *spec: pltpu.VMEM(*spec)
    big = [vmem(*whole_x), vmem(*whole_x)]

    def run(kernel, ins, outs, scratch):
        calls[0] += 1
        return call(kernel, calls[0], ins, outs, scratch)

    near = lambda *arrays: [(array, False) for array in arrays]
    far = lambda *arrays: [(array, True) for array in arrays]
    out = lambda shape, kind, hbm=False: (shape, kind, hbm)

    saved = []
    for l in range(layers):
        w_attention, w_forward = weights[l]
        lam = lax.dynamic_slice_in_dim(difference_lambda[l], head, 1).reshape(1, 1)
        gain_a, gain_f = gains[l, 0:1], gains[l, 1:2]
        shared = (a_model[l], a_head[l], cosine, sine, query_bits, key_bits, lam)
        got = run(
            functools.partial(attention_forward, n, l, part, rank),
            near(residual, gain_a) + far(w_attention) + near(*shared),
            [
                out((rows, width), F32),
                out(*whole_x, True),
                out((tree, VD), BF),
                out((tree, VD), BF),
                out((tree, VD), BF),
                out((tree, 3 * rank), BF),
                out((tree, 2), F32),
                out((tree, VD), F32),
                out((tree, VD), BF),
                out((tree, rank), BF),
            ],
            big + [vmem((width, 4 * VD), BF), vmem((3 * rank, 3 * VD), BF), pair] + sems,
        )
        middle, kept = got[0], got[1:]
        ffn = run(
            functools.partial(ffn_forward, n, units, rank),
            near(middle, gain_f) + far(w_forward) + near(a_model[l], e_model[l]),
            [
                out((rows, width), F32),
                out(*whole_x, True),
                out((tree, units), BF),
                out((tree, units), BF),
                out((tree, units), BF),
                out((tree, 2 * rank), BF),
                out((tree, rank), BF),
            ],
            big + [vmem((width, 3 * units), BF), vmem((2 * rank, 2 * units), BF), pair] + sems,
        )
        saved.append((residual, middle, gain_a, gain_f, shared, kept, ffn[1:]))
        residual = ffn[0]

    grad = own_cotangent.astype(F32)
    model_grads, hidden_grads = [], []
    for l in reversed(range(layers)):
        w_attention, w_forward = weights[l]
        residual_in, middle, gain_a, gain_f, shared, kept, ffn = saved[l]
        grad, grad_a10, grad_a45, grad_e01, grad_e2 = run(
            functools.partial(ffn_backward, n, units, rank),
            near(grad, middle, gain_f) + far(w_forward) + near(a_model[l], e_model[l]) + far(ffn[0]) + near(*ffn[1:]),
            [
                out((rows, width), F32),
                out((rank, width), BF),
                out((2 * rank, width), BF),
                out((2 * rank, units), F32),
                out((rank, units), F32),
            ],
            big
            + [
                vmem((width, 3 * units), BF),
                vmem(*whole_x),
                vmem((tree, 2 * units), BF),
                vmem((tree, 2 * rank), BF),
                vmem((tree, rank), BF),
                vmem((2 * rank, 2 * units), BF),
                pair,
            ]
            + sems,
        )
        grad, grad_a9, grad_a012, grad_head = run(
            functools.partial(attention_backward, n, l, part, rank),
            near(grad, residual_in, gain_a) + far(w_attention) + near(*shared) + far(kept[0]) + near(*kept[1:]),
            [
                out((rows, width), F32),
                out((rank, width), BF),
                out((3 * rank, width), BF),
                out((4 * rank, VD), F32),
            ],
            big
            + [
                vmem((width, 4 * VD), BF),
                vmem((tree, VD), BF),
                vmem((tree, VD), F32),
                vmem((tree, VD), F32),
                vmem((tree, VD), F32),
                vmem((tree, 3 * VD), BF),
                vmem((tree, 3 * rank), BF),
                vmem((tree, rank), BF),
                vmem((3 * rank, 3 * VD), BF),
                pair,
            ]
            + sems,
        )

        def placed(x):
            empty = jnp.zeros(x.shape[:-1] + (width,), F32)
            return lax.dynamic_update_slice_in_dim(empty, x, head_at, x.ndim - 1).astype(BF)

        def placed_units(x):
            empty = jnp.zeros(x.shape[:-1] + (2, n * units), F32)
            empty = lax.dynamic_update_slice(
                empty, x[..., None, :], (0,) * (x.ndim - 1) + (t, q * units)
            )
            return empty[..., :hidden_tp].reshape(x.shape[:-1] + (2 * hidden_tp,)).astype(BF)

        headed = placed(grad_head)
        model_grads.insert(
            0,
            jnp.concatenate(
                [
                    swap_columns(grad_a012),
                    headed[:rank],
                    swap_columns(grad_a45),
                    headed[rank:],
                    swap_columns(grad_a9),
                    swap_columns(grad_a10),
                ]
            ),
        )
        hidden_grads.insert(0, placed_units(jnp.concatenate([grad_e01, grad_e2])))

    model_all = jnp.stack(model_grads).reshape(layers * 11 * rank, n, 2, width // (2 * n))
    hidden_all = jnp.stack(hidden_grads).reshape(layers * 3 * rank, n, 2, 2 * hidden_tp // (2 * n))
    lanes = 1024
    flat = jnp.concatenate(
        [x.transpose(1, 2, 0, 3).reshape(n, 2, -1) for x in (model_all, hidden_all)], axis=2
    )
    size = flat.shape[2]
    tall = -(-size // (lanes * 32)) * 32
    flat = jnp.pad(flat, ((0, 0), (0, 0), (0, tall * lanes - size))).reshape(n, 2, tall, lanes).astype(BF)
    calls[0] += 1
    summed = swap_trees(group_reduce(flat, n, calls[0]).astype(BF), nf, nc)
    every = lax.all_gather(summed, "fsdp", axis=0).reshape(nf, -1)[:, :size].astype(F32)
    slots = lax.all_gather(tree_adapter_index, "fsdp", axis=0, tiled=True)
    own_adapters = adapters // nf
    chosen = place.f * own_adapters + jnp.arange(own_adapters)
    pick = (slots[None, :] == chosen[:, None]).astype(F32)
    totals = jnp.sum(pick[:, :, None] * every[None], axis=1)
    cut = layers * 11 * rank * (width // (2 * n))
    grad_model = totals[:, :cut].reshape(own_adapters, layers, 11, rank, -1).transpose(1, 2, 0, 3, 4)
    grad_hidden = totals[:, cut:].reshape(own_adapters, layers, 3, rank, -1).transpose(1, 2, 0, 3, 4)

    def home(x):
        mine = swap_trees(swap_columns(x), nf, nc)
        other = lax.ppermute(mine, "tp", ((0, 1), (1, 0)))
        return jnp.where(t == 0, jnp.concatenate([mine, other]), jnp.concatenate([other, mine]))

    return home(residual.astype(BF)), home(grad), grad_model, grad_hidden


def solution(mesh):
    in_specs = (
        P(("fsdp", "ctx"), None),
        P(("fsdp", "ctx"), None),
        P(("fsdp", "ctx")),
        P(("fsdp", "ctx")),
        P("fsdp", None),
        P("fsdp"),
        P(),
        P(None, "tp"),
        P(None, ("fsdp", "ctx"), None, "tp"),
        P(None, ("fsdp", "ctx"), "tp"),
        P(None, ("fsdp", "ctx"), None, "tp"),
        P(None, ("fsdp", "ctx"), "tp"),
        P(),
        P(),
    )
    out_specs = (
        P(("fsdp", "ctx"), None),
        P(("fsdp", "ctx"), None),
        P(None, None, "fsdp", None, ("ctx", "tp")),
        P(None, None, "fsdp", None, ("ctx", "tp")),
    )
    body = functools.partial(shards, mesh.shape["fsdp"], mesh.shape["ctx"])
    return jax.shard_map(body, mesh=mesh, in_specs=in_specs, out_specs=out_specs, check_vma=False)
```

time: 3090 us -> 1280 us (0.41)
  waiting for transfers between devices: 2400 us -> 338 us
  Pallas kernels: 0 us -> 626 us
  matrix products: 286 us -> 0 us
  local copies, waits for them, and re-layouts: 253 us -> 204 us
  other arithmetic: 70.7 us -> 26 us
  starting transfers between devices: 2.5 us -> 36.7 us
    all_gather x12 -> x1, waiting for transfers between devices: 1290 us -> 0.01 us  [shards(): lax.all_gather(summed, 'fsdp', axis=0).reshape(nf, -1)[:, :size].astype(F32)]
    unnamed x26 -> x1, waiting for transfers between devices: 720 us -> 0.02 us
    pallas_call x0 -> x9, Pallas kernels: none -> 626 us  [the longest x8 584 us: call(): pl.pallas_call(kernel, out_shape=[jax.ShapeDtypeStruct(shape, kind) for s...]
    ppermute x0 -> x32, waiting for transfers between devices: none -> 338 us  [the longest x30 338 us: permute(): return lax.ppermute(x, ('fsdp', 'ctx'), pairs)]
    reduce_scatter x3 -> x0, waiting for transfers between devices: 317 us -> none  [the longest x2 263 us: attend_backward(): lax.psum_scatter(key_terms, 'ctx', scatter_dimension=0, tiled=True)]
    dot_general x109 -> x0, matrix products: 286 us -> none  [the longest x56 185 us: einsum_single(): jnp.einsum(formula, left_side, right_side, preferred_element_type=jnp.flo...]
    unnamed x312 -> x98, local copies, waits for them, and re-layouts: 130 us -> 8.52 us
    psum x7 -> x0, waiting for transfers between devices: 71.6 us -> none  [the longest x3 44.9 us: grad_total(): return lax.psum((pair[0], pair[1]), 'tp')]
  transfers between devices with their start and end apart: 24 -> 33, of which waited for: 23 -> 9; matrix products, arithmetic and copies ran while one was open for 10% -> 13% of each run, Pallas kernels for 0% -> 24%
where the time goes in v1:
time: 1280 us; the launch traced here: 1270 us
  Pallas kernels  626 us (49%)
  waiting for transfers between devices  338 us (26%)
  local copies, waits for them, and re-layouts  204 us (16%)
  starting transfers between devices  36.7 us (3%)
  other arithmetic  26 us (2%)
  blocking collectives  18.6 us (1%)
  between operations  18.2 us (1%)
    pallas_call x8, Pallas kernels, call(): pl.pallas_call(kernel, out_shape=[jax.ShapeDtypeStruct(shape, kind) for s...  584 us
    ppermute x30, waiting for transfers between devices, permute(): return lax.ppermute(x, ('fsdp', 'ctx'), pairs)  338 us
    pallas_call x1, Pallas kernels, group_reduce(): pl.pallas_call(functools.partial(rs_kernel, n), out_shape=jax.ShapeDtypeS...  42 us
    ppermute x30, starting transfers between devices, permute(): return lax.ppermute(x, ('fsdp', 'ctx'), pairs)  35.5 us
    another operation x16, local copies, waits for them, and re-layouts, heads(): cut = x.reshape(weight_rows, heads_tp, VD).transpose(1, 0, 2)  27.5 us
  transfers between devices with their start and end apart: 33, of which 9 were waited for; matrix products, arithmetic and copies ran while one was open for 13% of the time, Pallas kernels for 24%

profile of v1, /device:TPU:3, one launch (start us, length us, event | category | flops | bytes accessed | tf_op | source)
XLA Modules:
  0.0 1267.9 jit_solution(12500622352420440016)
XLA Ops:
  7.3 3.8 fusion.7
  39.6 11.8 all_gather.12
  52.1 2.9 collective-permute-start.7
  90.3 4.9 reshape.235
  95.1 3.6 fusion.8
  108.3 3.1 squeeze.135.a_model
  115.2 3.0 squeeze.151.a_model
  128.0 3.6 collective-permute-start
  131.7 3.7 collective-permute-start.28
  140.6 17.5 %collective-permute-done = bf16[128,2048]{1,0:T(8,128)(2,1)} collective-permute-done((bf16[128,2048]{1,0:T(8,128)(2,1)S(1)}, bf16[128,2048]{1,0:T(8,128)(2,1)}, u32[]{:S(2)}, u32[]{:S(2)}) %collective-permute-start) | collective-permute-done | bytes 524320 | tf_op jit(solution)/shard_map/ppermute | solution.py:684
  160.0 3.0 reshape.276
  165.7 3.0 reshape.274.residual
  168.8 8.9 collective-permute-done.28
  177.7 3.0 reshape.277
  183.5 3.0 reshape.275.grad
  187.7 2.9 collective-permute-start.17
  196.3 2.8 bitcast_dynamic-update-slice_fusion.21
  201.4 12.3 collective-permute-done.10
  214.6 92.7 %collective-permute-done.17 = bf16[4,128,1024]{2,1,0:T(8,128)(2,1)} collective-permute-done((bf16[4,128,1024]{2,1,0:T(8,128)(2,1)S(1)}, bf16[4,128,1024]{2,1,0:T(8,128)(2,1)}, u32[]{:S(2)}, u32[]{:S(2)}) %collective-permute-start.17) | collective-permute-done | bytes 1048608 | tf_op jit(solution)/shard_map/ppermute | solution.py:684
  307.3 4.5 broadcast.82.clone
  311.8 3.3 bitcast_dynamic-update-slice_fusion.7
  315.1 65.1 %collective-permute-done.4 = bf16[4,128,1024]{2,1,0:T(8,128)(2,1)S(1)} collective-permute-done((bf16[4,128,1024]{2,1,0:T(8,128)(2,1)S(1)}, bf16[4,128,1024]{2,1,0:T(8,128)(2,1)S(1)}, u32[]{:S(2)}, u32[]{:S(2)}) %collective-permute-start.4) | collective-permute-done | bytes 1048608 | tf_op jit(solution)/shard_map/ppermute | solution.py:684
  388.3 10.9 collective-permute-done.6
  401.4 140.6 %shard_map.165 = (f32[128,2048]{1,0:T(8,128)}, bf16[4,2,128,2048]{3,2,1,0:T(8,128)(2,1)}, bf16[1024,256]{1,0:T(8,128)(2,1)}, bf16[1024,256]{1,0:T(8,128)(2,1)}, ...) custom-call(f32[128,2048]{1,0:T(8,128)} %reshape.274.residual, ...), custom_call_target="tpu_custom_call" | custom-call | tf_op jit(solution)/shard_map/pallas_call | solution.py:646
  544.5 3.2 bitcast_dynamic-update-slice_fusion.2
  547.7 3.2 bitcast_dynamic-update-slice_fusion.6
  550.9 3.2 bitcast_dynamic-update-slice_fusion.1
  554.2 3.2 bitcast_dynamic-update-slice_fusion.5
  557.4 88.5 %collective-permute-done.13 = bf16[4,128,2304]{2,1,0:T(8,128)(2,1)S(1)} collective-permute-done((bf16[4,128,2304]{2,1,0:T(8,128)(2,1)}, bf16[4,128,2304]{2,1,0:T(8,128)(2,1)S(1)}, u32[]{:S(2)}, u32[]{:S(2)}) %collective-permute-start.13) | collective-permute-done | bytes 2359328 | tf_op jit(solution)/shard_map/ppermute | solution.py:684
  647.5 59.7 %shard_map.166 = (f32[128,2048]{1,0:T(8,128)}, bf16[4,2,128,2048]{3,2,1,0:T(8,128)(2,1)}, bf16[1024,768]{1,0:T(8,128)(2,1)}, bf16[1024,768]{1,0:T(8,128)(2,1)}, ...) custom-call(f32[128,2048]{1,0:T(8,128)} %get-tuple-element.56.residual.middle, ...), custom_call_target="tpu_custom_call" | custom-call | tf_op jit(solution)/shard_map/pallas_call | solution.py:646
  707.2 63.6 %shard_map.167 = (f32[128,2048]{1,0:T(8,128)}, bf16[4,2,128,2048]{3,2,1,0:T(8,128)(2,1)}, bf16[1024,256]{1,0:T(8,128)(2,1)}, bf16[1024,256]{1,0:T(8,128)(2,1)}, ...) custom-call(f32[128,2048]{1,0:T(8,128)} %get-tuple-element.57.residu, ...), custom_call_target="tpu_custom_call" | custom-call | tf_op jit(solution)/shard_map/pallas_call | solution.py:646
  770.9 3.3 bitcast_dynamic-update-slice_fusion
  774.2 59.6 %shard_map.168 = (f32[128,2048]{1,0:T(8,128)}, bf16[4,2,128,2048]{3,2,1,0:T(8,128)(2,1)}, bf16[1024,768]{1,0:T(8,128)(2,1)}, bf16[1024,768]{1,0:T(8,128)(2,1)}, ...) custom-call(f32[128,2048]{1,0:T(8,128)} %get-tuple-element.58.residual.middle, ...), custom_call_target="tpu_custom_call" | custom-call | tf_op jit(solution)/shard_map/pallas_call | solution.py:646
  833.7 59.8 %shard_map.169 = (f32[128,2048]{1,0:T(8,128)}, bf16[16,2048]{1,0:T(8,128)(2,1)}, bf16[32,2048]{1,0:T(8,128)(2,1)}, f32[32,768]{1,0:T(8,128)}, f32[16,768]{1,0:T(8,128)}) custom-call(f32[128,2048]{1,0:T(8,128)} %reshape.275.grad, f32[128,2048]{1,0:T(8,128)} %get-tuple-element.58.residual.middle, f32[1,2048]{1,0:T(1,128)} %get-tuple-element.160.gain, ...), custom_call_target="tpu_custom_call" | custom-call | tf_op jit(solution)/shard_map/pallas_call | solution.py:646
  893.5 68.4 %shard_map.170 = (f32[128,2048]{1,0:T(8,128)}, bf16[16,2048]{1,0:T(8,128)(2,1)}, bf16[48,2048]{1,0:T(8,128)(2,1)}, f32[64,256]{1,0:T(8,128)}) custom-call(f32[128,2048]{1,0:T(8,128)} %get-tuple-element.66.grad, f32[128,2048]{1,0:T(8,128)} %get-tuple-element.57.residual, f32[1,2048]{1,0:T(1,128)} %get-tuple-element.161.gain, ...), custom_call_target="tpu_custom_call" | custom-call | tf_op jit(solution)/shard_map/pallas_call | solution.py:646
  961.9 61.8 %shard_map.171 = (f32[128,2048]{1,0:T(8,128)}, bf16[16,2048]{1,0:T(8,128)(2,1)}, bf16[32,2048]{1,0:T(8,128)(2,1)}, f32[32,768]{1,0:T(8,128)}, f32[16,768]{1,0:T(8,128)}) custom-call(f32[128,2048]{1,0:T(8,128)} %get-tuple-element.76.grad, f32[128,2048]{1,0:T(8,128)} %get-tuple-element.56.residual.middle, f32[1,2048]{1,0:T(1,128)} %get-tuple-element.162.gain, ...), custom_call_target="tpu_custom_call" | custom-call | tf_op jit(solution)/shard_map/pallas_call | solution.py:646
  1023.7 70.7 %shard_map.172 = (f32[128,2048]{1,0:T(8,128)}, bf16[16,2048]{1,0:T(8,128)(2,1)}, bf16[48,2048]{1,0:T(8,128)(2,1)}, f32[64,256]{1,0:T(8,128)}) custom-call(f32[128,2048]{1,0:T(8,128)} %get-tuple-element.83.grad, f32[128,2048]{1,0:T(8,128)} %reshape.274.residual, f32[1,2048]{1,0:T(1,128)} %get-tuple-element.163.gain, bf16[2048,1024]{1,0:T(8,128)(2,1)} %bitcast.18.w_hbm, ...), custom_call_target="tpu_custom_call" | custom-call | tf_op jit(solution)/shard_map/pallas_call | solution.py:646
  1102.8 4.6 dynamic_update_slice.146
  1110.5 5.0 dynamic_update_slice.147
  1119.1 3.2 reshape.268
  1124.9 4.0 reshape.269
  1134.1 8.7 fusion.2
  1142.8 5.1 reshape.270.p_ref
  1147.9 42.0 %shard_map.173 = f32[160,1024]{1,0:T(8,128)} custom-call(bf16[4,2,160,1024]{3,2,1,0:T(8,128)(2,1)} %reshape.270.p_ref), custom_call_target="tpu_custom_call" | custom-call | tf_op jit(solution)/shard_map/pallas_call | solution.py:230
  1193.0 18.2 %collective-permute-done.31 = bf16[160,1024]{1,0:T(8,128)(2,1)S(1)} collective-permute-done((bf16[160,1024]{1,0:T(8,128)(2,1)S(1)}, bf16[160,1024]{1,0:T(8,128)(2,1)S(1)}, u32[]{:S(2)}, u32[]{:S(2)}) %collective-permute-start.31) | collective-permute-done | bytes 327712 | tf_op jit(solution)/shard_map/ppermute | solution.py:684
  1215.8 24.2 %collective-permute-done.26 = bf16[128,2048]{1,0:T(8,128)(2,1)S(1)} collective-permute-done((bf16[128,2048]{1,0:T(8,128)(2,1)S(1)}, bf16[128,2048]{1,0:T(8,128)(2,1)S(1)}, u32[]{:S(2)}, u32[]{:S(2)}) %collective-permute-start.26) | collective-permute-done | bytes 524320 | tf_op jit(solution)/shard_map/ppermute | solution.py:684
  1241.9 6.8 all-reduce.8
  1254.4 4.0 multiply_reduce_fusion
  (319 shorter events, 161.5 us)
Async XLA Ops:
  7.2 67.2 %copy-start = (bf16[256,2048]{1,0:T(8,128)(2,1)S(1)}, bf16[256,2048]{1,0:T(8,128)(2,1)}, u32[]{:S(2)}) copy-start(bf16[256,2048]{1,0:T(8,128)(2,1)} %param.14) | copy-start | bytes 3145732
  7.2 1244.4 %all-gather.3.cloned.1.call-start = ((), (), s32[]{:S(2)}) async-start(), calls=%async_computation | async-start | bytes 1638400 | tf_op jit(solution)/shard_map/all_gather | solution.py:956
  16.7 169.8 %collective-permute-start.20 = (bf16[128,2304]{1,0:T(8,128)(2,1)}, bf16[128,2304]{1,0:T(8,128)(2,1)}, u32[]{:S(2)}, u32[]{:S(2)}) collective-permute-start(bf16[128,2304]{1,0:T(8,128)(2,1)} %get-tuple-element.124), channel_id=1, source_target_pairs={{0,2},{2,0},{4,6},{6,4},{8,10},{10,8},{12,14},{14,12},{16,18},{18,... | collective-permute-start | bytes 1769480 | tf_op jit(solution)/shard_map/ppermute | solution.py:684
  18.0 169.6 %collective-permute-start.21 = (bf16[128,2304]{1,0:T(8,128)(2,1)}, bf16[128,2304]{1,0:T(8,128)(2,1)}, u32[]{:S(2)}, u32[]{:S(2)}) collective-permute-start(bf16[128,2304]{1,0:T(8,128)(2,1)} %get-tuple-element.123), channel_id=1, source_target_pairs={{0,8},{2,10},{4,12},{6,14},{8,0},{10,2},{12,4},{14,6},{16,24},{18,... | collective-permute-start | bytes 1769480 | tf_op jit(solution)/shard_map/ppermute | solution.py:684
  34.9 4.7 copy-start.37
  34.9 4.7 copy-start.38
  34.9 17.1 %copy-start.39 = (s32[1,13]{1,0:T(1,128)S(1)}, s32[1,13]{1,0:T(1,128)}, u32[]{:S(2)}) copy-start(s32[1,13]{1,0:T(1,128)} %param.18) | copy-start | bytes 160
  38.2 80.0 %collective-permute-start.14 = (bf16[128,1024]{1,0:T(8,128)(2,1)}, bf16[128,1024]{1,0:T(8,128)(2,1)}, u32[]{:S(2)}, u32[]{:S(2)}) collective-permute-start(bf16[128,1024]{1,0:T(8,128)(2,1)} %get-tuple-element.142), channel_id=1, source_target_pairs={{0,2},{2,0},{4,6},{6,4},{8,10},{10,8},{12,14},{14,12},{16,18},{18,... | collective-permute-start | bytes 786440 | tf_op jit(solution)/shard_map/ppermute | solution.py:684
  38.7 81.2 %collective-permute-start.15 = (bf16[128,1024]{1,0:T(8,128)(2,1)}, bf16[128,1024]{1,0:T(8,128)(2,1)}, u32[]{:S(2)}, u32[]{:S(2)}) collective-permute-start(bf16[128,1024]{1,0:T(8,128)(2,1)} %get-tuple-element.141), channel_id=1, source_target_pairs={{0,8},{2,10},{4,12},{6,14},{8,0},{10,2},{12,4},{14,6},{16,24},{18,... | collective-permute-start | bytes 786440 | tf_op jit(solution)/shard_map/ppermute | solution.py:684
  52.1 33.0 %collective-permute-start.7 = (s32[2062]{0:T(1024)S(1)}, s32[2062]{0:T(1024)S(1)}, u32[]{:S(2)}, u32[]{:S(2)}) collective-permute-start(s32[2062]{0:T(1024)S(1)} %concatenate.52), channel_id=1, source_target_pairs={{0,0},{2,2},{4,8},{6,10},{8,4},{10,6},{12,12},{14,14},{16,16},{18,... | collective-permute-start | bytes 24752 | tf_op jit(solution)/shard_map/ppermute | solution.py:684
  59.5 14.1 %copy-start.36 = (f32[2,4]{1,0:T(2,128)S(1)}, f32[2,4]{1,0:T(2,128)}, u32[]{:S(2)}) copy-start(f32[2,4]{1,0:T(2,128)} %param.21) | copy-start | bytes 100
  59.5 14.1 %copy-start.35 = (f32[2,2,2048]{2,1,0:T(2,128)S(1)}, f32[2,2,2048]{2,1,0:T(2,128)}, u32[]{:S(2)}) copy-start(f32[2,2,2048]{2,1,0:T(2,128)} %param.20) | copy-start | bytes 98308
  85.1 37.7 %collective-permute-start.16 = (bf16[128,1024]{1,0:T(8,128)(2,1)}, bf16[128,1024]{1,0:T(8,128)(2,1)}, u32[]{:S(2)}, u32[]{:S(2)}) collective-permute-start(bf16[128,1024]{1,0:T(8,128)(2,1)} %get-tuple-element.140), channel_id=1, source_target_pairs={{0,10},{2,8},{4,14},{6,12},{8,2},{10,0},{12,6},{14,4},{16,26},{18,... | collective-permute-start | bytes 786440 | tf_op jit(solution)/shard_map/ppermute | solution.py:684
  108.3 10.5 copy-start.4
  118.2 9.8 collective-permute-start.1
  119.8 11.8 collective-permute-start.2
  122.8 12.5 collective-permute-start.3
  124.3 7.3 copy-start.6
  128.0 30.2 %collective-permute-start = (bf16[128,2048]{1,0:T(8,128)(2,1)S(1)}, bf16[128,2048]{1,0:T(8,128)(2,1)}, u32[]{:S(2)}, u32[]{:S(2)}) collective-permute-start(bf16[128,2048]{1,0:T(8,128)(2,1)S(1)} %copy-done.20), channel_id=1, source_target_pairs={{0,0},{2,2},{4,8},{6,10},{8,4},{10,6},{12,12},{14,14},{16,16},{18,... | collective-permute-start | bytes 1572872 | tf_op jit(solution)/shard_map/ppermute | solution.py:684
  131.7 46.0 %collective-permute-start.28 = (bf16[128,2048]{1,0:T(8,128)(2,1)}, bf16[128,2048]{1,0:T(8,128)(2,1)}, u32[]{:S(2)}, u32[]{:S(2)}) collective-permute-start(bf16[128,2048]{1,0:T(8,128)(2,1)} %constant_dynamic-slice_fusion), channel_id=1, source_target_pairs={{0,0},{2,2},{4,8},{6,10},{8,4},{10,6},{12,12},{14,14},{16,16},{18,... | collective-permute-start | bytes 1572872 | tf_op jit(solution)/shard_map/ppermute | solution.py:684
  135.4 56.4 %collective-permute-start.22 = (bf16[128,2304]{1,0:T(8,128)(2,1)}, bf16[128,2304]{1,0:T(8,128)(2,1)}, u32[]{:S(2)}, u32[]{:S(2)}) collective-permute-start(bf16[128,2304]{1,0:T(8,128)(2,1)} %get-tuple-element.122), channel_id=1, source_target_pairs={{0,10},{2,8},{4,14},{6,12},{8,2},{10,0},{12,6},{14,4},{16,26},{18,... | collective-permute-start | bytes 1769480 | tf_op jit(solution)/shard_map/ppermute | solution.py:684
  158.1 37.2 %collective-permute-start.8 = (bf16[128,2304]{1,0:T(8,128)(2,1)}, bf16[128,2304]{1,0:T(8,128)(2,1)}, u32[]{:S(2)}, u32[]{:S(2)}) collective-permute-start(bf16[128,2304]{1,0:T(8,128)(2,1)} %get-tuple-element.128), channel_id=1, source_target_pairs={{0,2},{2,0},{4,6},{6,4},{8,10},{10,8},{12,14},{14,12},{16,18},{18,... | collective-permute-start | bytes 1769480 | tf_op jit(solution)/shard_map/ppermute | solution.py:684
  177.7 21.4 %collective-permute-start.9 = (bf16[128,2304]{1,0:T(8,128)(2,1)}, bf16[128,2304]{1,0:T(8,128)(2,1)}, u32[]{:S(2)}, u32[]{:S(2)}) collective-permute-start(bf16[128,2304]{1,0:T(8,128)(2,1)} %get-tuple-element.127), channel_id=1, source_target_pairs={{0,8},{2,10},{4,12},{6,14},{8,0},{10,2},{12,4},{14,6},{16,24},{18,... | collective-permute-start | bytes 1769480 | tf_op jit(solution)/shard_map/ppermute | solution.py:684
  186.5 27.2 %collective-permute-start.10 = (bf16[128,2304]{1,0:T(8,128)(2,1)}, bf16[128,2304]{1,0:T(8,128)(2,1)S(1)}, u32[]{:S(2)}, u32[]{:S(2)}) collective-permute-start(bf16[128,2304]{1,0:T(8,128)(2,1)} %get-tuple-element.126), channel_id=1, source_target_pairs={{0,10},{2,8},{4,14},{6,12},{8,2},{10,0},{12,6},{14,4},{16,26},{18,... | collective-permute-start | bytes 1769480 | tf_op jit(solution)/shard_map/ppermute | solution.py:684
  187.7 119.6 %collective-permute-start.17 = (bf16[4,128,1024]{2,1,0:T(8,128)(2,1)S(1)}, bf16[4,128,1024]{2,1,0:T(8,128)(2,1)}, u32[]{:S(2)}, u32[]{:S(2)}) collective-permute-start(bf16[4,128,1024]{2,1,0:T(8,128)(2,1)S(1)} %bitcast_dynamic-update-slice_fusion.22), channel_id=1, source_target_pairs={{0,4},{2,6},{4,0},{6,2},{8,12},{10,14},{12,8},{14,10},{16,20},{18,... | collective-permute-start | bytes 3145736 | tf_op jit(solution)/shard_map/ppermute | solution.py:684
  191.7 191.9 %collective-permute-start.18 = (bf16[4,128,1024]{2,1,0:T(8,128)(2,1)S(1)}, bf16[4,128,1024]{2,1,0:T(8,128)(2,1)S(1)}, u32[]{:S(2)}, u32[]{:S(2)}) collective-permute-start(bf16[4,128,1024]{2,1,0:T(8,128)(2,1)S(1)} %bitcast_dynamic-update-slice_fusion.22), channel_id=1, source_target_pairs={{0,16},{2,18},{4,20},{6,22},{8,24},{10,26},{12,28},{14,30},{16,0},... | collective-permute-start | bytes 3145736 | tf_op jit(solution)/shard_map/ppermute | solution.py:684
  195.3 116.5 %copy-start.2 = (bf16[4,4,128,2304]{3,2,1,0:T(8,128)(2,1)}, bf16[4,4,128,2304]{3,2,1,0:T(8,128)(2,1)S(1)}, u32[]{:S(2)}) copy-start(bf16[4,4,128,2304]{3,2,1,0:T(8,128)(2,1)S(1)} %bitcast_dynamic-update-slice_fusion.3) | copy-start | bytes 28311556
  196.3 183.9 %collective-permute-start.4 = (bf16[4,128,1024]{2,1,0:T(8,128)(2,1)S(1)}, bf16[4,128,1024]{2,1,0:T(8,128)(2,1)S(1)}, u32[]{:S(2)}, u32[]{:S(2)}) collective-permute-start(bf16[4,128,1024]{2,1,0:T(8,128)(2,1)S(1)} %copy-done.8), channel_id=1, source_target_pairs={{0,4},{2,6},{4,0},{6,2},{8,12},{10,14},{12,8},{14,10},{16,20},{18,... | collective-permute-start | bytes 3145736 | tf_op jit(solution)/shard_map/ppermute | solution.py:684
  199.1 187.0 %collective-permute-start.5 = (bf16[4,128,1024]{2,1,0:T(8,128)(2,1)S(1)}, bf16[4,128,1024]{2,1,0:T(8,128)(2,1)S(1)}, u32[]{:S(2)}, u32[]{:S(2)}) collective-permute-start(bf16[4,128,1024]{2,1,0:T(8,128)(2,1)S(1)} %copy-done.8), channel_id=1, source_target_pairs={{0,16},{2,18},{4,20},{6,22},{8,24},{10,26},{12,28},{14,30},{16,0},... | collective-permute-start | bytes 3145736 | tf_op jit(solution)/shard_map/ppermute | solution.py:684
  213.7 329.3 %collective-permute-start.23 = (bf16[4,128,2304]{2,1,0:T(8,128)(2,1)S(1)}, bf16[4,128,2304]{2,1,0:T(8,128)(2,1)}, u32[]{:S(2)}, u32[]{:S(2)}) collective-permute-start(bf16[4,128,2304]{2,1,0:T(8,128)(2,1)S(1)} %bitcast_dynamic-update-slice_fusion.16), channel_id=1, source_target_pairs={{0,4},{2,6},{4,0},{6,2},{8,12},{10,14},{12,8},{14,10},{16,20},{18,... | collective-permute-start | bytes 7077896 | tf_op jit(solution)/shard_map/ppermute | solution.py:684
  307.3 237.0 %collective-permute-start.11 = (bf16[4,128,2304]{2,1,0:T(8,128)(2,1)}, bf16[4,128,2304]{2,1,0:T(8,128)(2,1)}, u32[]{:S(2)}, u32[]{:S(2)}) collective-permute-start(bf16[4,128,2304]{2,1,0:T(8,128)(2,1)} %bitcast_dynamic-update-slice_fusion.19), channel_id=1, source_target_pairs={{0,4},{2,6},{4,0},{6,2},{8,12},{10,14},{12,8},{14,10},{16,20},{18,... | collective-permute-start | bytes 7077896 | tf_op jit(solution)/shard_map/ppermute | solution.py:684
  380.2 19.0 %collective-permute-start.6 = (bf16[4,128,1024]{2,1,0:T(8,128)(2,1)S(1)}, bf16[4,128,1024]{2,1,0:T(8,128)(2,1)S(1)}, u32[]{:S(2)}, u32[]{:S(2)}) collective-permute-start(bf16[4,128,1024]{2,1,0:T(8,128)(2,1)S(1)} %collective-permute-done.4), channel_id=1, source_target_pairs={{0,16},{2,18},{4,20},{6,22},{8,24},{10,26},{12,28},{14,30},{16,0},... | collective-permute-start | bytes 3145736 | tf_op jit(solution)/shard_map/ppermute | solution.py:684
  383.7 158.3 %collective-permute-start.19 = (bf16[4,128,1024]{2,1,0:T(8,128)(2,1)}, bf16[4,128,1024]{2,1,0:T(8,128)(2,1)S(1)}, u32[]{:S(2)}, u32[]{:S(2)}) collective-permute-start(bf16[4,128,1024]{2,1,0:T(8,128)(2,1)} %collective-permute-done.17), channel_id=1, source_target_pairs={{0,16},{2,18},{4,20},{6,22},{8,24},{10,26},{12,28},{14,30},{16,0},... | collective-permute-start | bytes 3145736 | tf_op jit(solution)/shard_map/ppermute | solution.py:684
  386.1 164.9 %collective-permute-start.24 = (bf16[4,128,2304]{2,1,0:T(8,128)(2,1)S(1)}, bf16[4,128,2304]{2,1,0:T(8,128)(2,1)}, u32[]{:S(2)}, u32[]{:S(2)}) collective-permute-start(bf16[4,128,2304]{2,1,0:T(8,128)(2,1)S(1)} %bitcast_dynamic-update-slice_fusion.16), channel_id=1, source_target_pairs={{0,16},{2,18},{4,20},{6,22},{8,24},{10,26},{12,28},{14,30},{16,0},... | collective-permute-start | bytes 7077896 | tf_op jit(solution)/shard_map/ppermute | solution.py:684
  399.2 155.0 %collective-permute-start.12 = (bf16[4,128,2304]{2,1,0:T(8,128)(2,1)}, bf16[4,128,2304]{2,1,0:T(8,128)(2,1)}, u32[]{:S(2)}, u32[]{:S(2)}) collective-permute-start(bf16[4,128,2304]{2,1,0:T(8,128)(2,1)} %bitcast_dynamic-update-slice_fusion.19), channel_id=1, source_target_pairs={{0,16},{2,18},{4,20},{6,22},{8,24},{10,26},{12,28},{14,30},{16,0},... | collective-permute-start | bytes 7077896 | tf_op jit(solution)/shard_map/ppermute | solution.py:684
  543.0 227.8 %collective-permute-start.25 = (bf16[4,128,2304]{2,1,0:T(8,128)(2,1)}, bf16[4,128,2304]{2,1,0:T(8,128)(2,1)}, u32[]{:S(2)}, u32[]{:S(2)}) collective-permute-start(bf16[4,128,2304]{2,1,0:T(8,128)(2,1)} %collective-permute-done.23), channel_id=1, source_target_pairs={{0,16},{2,18},{4,20},{6,22},{8,24},{10,26},{12,28},{14,30},{16,0},... | collective-permute-start | bytes 7077896 | tf_op jit(solution)/shard_map/ppermute | solution.py:684
  544.3 101.7 %collective-permute-start.13 = (bf16[4,128,2304]{2,1,0:T(8,128)(2,1)}, bf16[4,128,2304]{2,1,0:T(8,128)(2,1)S(1)}, u32[]{:S(2)}, u32[]{:S(2)}) collective-permute-start(bf16[4,128,2304]{2,1,0:T(8,128)(2,1)} %collective-permute-done.11), channel_id=1, source_target_pairs={{0,16},{2,18},{4,20},{6,22},{8,24},{10,26},{12,28},{14,30},{16,0},... | collective-permute-start | bytes 7077896 | tf_op jit(solution)/shard_map/ppermute | solution.py:684
  1023.7 72.2 %copy-start.24 = (bf16[32,2048]{1,0:T(8,128)(2,1)S(1)}, bf16[32,2048]{1,0:T(8,128)(2,1)}, u32[]{:S(2)}) copy-start(bf16[32,2048]{1,0:T(8,128)(2,1)} %get-tuple-element.96) | copy-start | bytes 393220
  1102.3 7.6 copy-start.25
  1102.3 7.6 copy-start.33
  1122.3 6.6 copy-start.15
  1132.2 83.1 %collective-permute-start.29 = (f32[128,2048]{1,0:T(8,128)}, f32[128,2048]{1,0:T(8,128)S(1)}, u32[]{:S(2)}, u32[]{:S(2)}) collective-permute-start(f32[128,2048]{1,0:T(8,128)} %reshape.249), channel_id=1, source_target_pairs={{0,0},{2,2},{4,8},{6,10},{8,4},{10,6},{12,12},{14,14},{16,16},{18,... | collective-permute-start | bytes 3145736 | tf_op jit(solution)/shard_map/ppermute | solution.py:684
  1147.9 64.0 %copy-start.14 = (f32[128,2048]{1,0:T(8,128)S(1)}, f32[128,2048]{1,0:T(8,128)}, u32[]{:S(2)}) copy-start(f32[128,2048]{1,0:T(8,128)} %get-tuple-element.59) | copy-start | bytes 3145732
  1191.0 20.1 %collective-permute-start.31 = (bf16[160,1024]{1,0:T(8,128)(2,1)S(1)}, bf16[160,1024]{1,0:T(8,128)(2,1)S(1)}, u32[]{:S(2)}, u32[]{:S(2)}) collective-permute-start(bf16[160,1024]{1,0:T(8,128)(2,1)S(1)} %convert_element_type.99), channel_id=1, source_target_pairs={{0,0},{2,2},{4,8},{6,10},{8,4},{10,6},{12,12},{14,14},{16,16},{18,... | collective-permute-start | bytes 983048 | tf_op jit(solution)/shard_map/ppermute | solution.py:684
  1211.9 28.7 %copy-start.40 = (u32[32]{0:T(128)S(1)}, u32[32]{0:T(128)}, u32[]{:S(2)}) copy-start(u32[32]{0:T(128)} %constant.256) | copy-start | bytes 388
  1213.3 26.7 %collective-permute-start.26 = (bf16[128,2048]{1,0:T(8,128)(2,1)S(1)}, bf16[128,2048]{1,0:T(8,128)(2,1)S(1)}, u32[]{:S(2)}, u32[]{:S(2)}) collective-permute-start(bf16[128,2048]{1,0:T(8,128)(2,1)S(1)} %reshape.247), channel_id=1, source_target_pairs={{0,0},{2,2},{4,8},{6,10},{8,4},{10,6},{12,12},{14,14},{16,16},{18,... | collective-permute-start | bytes 1572872 | tf_op jit(solution)/shard_map/ppermute | solution.py:684
  1215.2 34.8 %collective-permute-start.30 = (f32[128,2048]{1,0:T(8,128)S(1)}, f32[128,2048]{1,0:T(8,128)S(1)}, u32[]{:S(2)}, u32[]{:S(2)}) collective-permute-start(f32[128,2048]{1,0:T(8,128)S(1)} %collective-permute-done.29), channel_id=1, source_target_pairs={{0,1},{1,0},{2,3},{3,2},{4,5},{5,4},{6,7},{7,6},{8,9},{9,8},{10,11... | collective-permute-start | bytes 3145736 | tf_op jit(solution)/shard_map/ppermute | solution.py:968
  1240.0 8.8 collective-permute-start.27
  (26 other events, 51.8 us)
Sparse Core Ops, SparseCore 0:
  1212.0 35.4 all-gather.2

commit v2 on v1

--- a/solution.py
+++ b/solution.py
@@ -37,19 +37,230 @@
         return low * h + column, device
 
 
-def enter(place):
-    bar = pltpu.get_barrier_semaphore()
-    for device in (place.ring(1)[1], place.ring(-1)[1], {"tp": 1 - place.t}):
-        pl.semaphore_signal(bar, inc=1, device_id=device, device_id_type=MESH)
-    pl.semaphore_wait(bar, 3)
-
-
 def remote(src, dst, send, recv, device):
     copy = pltpu.make_async_remote_copy(
         src_ref=src, dst_ref=dst, send_sem=send, recv_sem=recv, device_id=device, device_id_type=MESH
     )
     copy.start()
     return copy
+
+
+def flip(number, bits):
+    b = 1
+    while b <= bits:
+        if bits & b:
+            number = number + b * (1 - 2 * ((number // b) % 2))
+        b *= 2
+    return number
+
+
+class Spread:
+    def __init__(self, place, nf, w, rows):
+        self.place, self.nf, self.w, self.rows = place, nf, w, rows
+        self.g = place.f_hi * 2 + place.c_hi
+        self.links = range(1, nf // 2)
+        self.scattered, self.sent = [], []
+        self.to_partner, self.along, self.onward = {}, {}, {}
+
+    @staticmethod
+    def scatter_semaphores(n):
+        dma = pltpu.SemaphoreType.DMA
+        return [dma((n,)), dma((n,))]
+
+    @staticmethod
+    def spread_semaphores(n, nf):
+        dma = pltpu.SemaphoreType.DMA
+        return [dma((n,))] * 2 + [dma((n, max(1, nf // 2 - 1)))] * 4
+
+    def block(self, g, q):
+        start = pl.multiple_of((g * self.place.n + q) * self.rows, self.rows)
+        return self.w.at[pl.ds(start, self.rows)]
+
+    def chip(self, q):
+        place = self.place
+        return {"fsdp": place.f_hi * 2 + q // place.h, "ctx": place.c_hi * place.h + q % place.h}
+
+    def partner(self):
+        place = self.place
+        return {"ctx": (1 - place.c_hi) * place.h + place.c_lo}
+
+    def line(self, e):
+        return {"fsdp": flip(self.place.f_hi, e) * 2 + self.place.f_lo}
+
+    def scatter(self, blocks, send, recv):
+        q = self.place.q
+        own = self.block(self.g, q)
+        copy = pltpu.make_async_copy(blocks.at[q], own, recv.at[0])
+        copy.start()
+        self.scattered.append(copy)
+        for d in range(1, self.place.n):
+            to = flip(q, d)
+            self.scattered.append(remote(blocks.at[to], own, send.at[d], recv.at[d], self.chip(to)))
+
+    def arrived(self, d):
+        if d:
+            self.scattered[d].wait_recv()
+        else:
+            self.scattered[0].wait()
+
+    def scatter_sent(self):
+        for copy in self.scattered[1:]:
+            copy.wait_send()
+
+    def use(self, *sems):
+        self.sems = sems
+
+    def spread(self, d):
+        send_z, recv_z, send_y, recv_y = self.sems[:4]
+        at = self.block(self.g, flip(self.place.q, d))
+        self.to_partner[d] = remote(at, at, send_z.at[d], recv_z.at[d], self.partner())
+        for e in self.links:
+            self.along[d, e] = remote(at, at, send_y.at[d, e - 1], recv_y.at[d, e - 1], self.line(e))
+
+    def forward(self, d):
+        send, recv = self.sems[4:]
+        self.to_partner[d].wait_recv()
+        at = self.block(flip(self.g, 1), flip(self.place.q, d))
+        for e in self.links:
+            self.onward[d, e] = remote(at, at, send.at[d, e - 1], recv.at[d, e - 1], self.line(e))
+
+    def complete(self):
+        for copy in list(self.along.values()) + list(self.onward.values()):
+            copy.wait_recv()
+
+    def sent_all(self):
+        for copies in (self.to_partner, self.along, self.onward):
+            for copy in copies.values():
+                copy.wait_send()
+
+
+def enter(place, nf=0, scatters=False):
+    bar = pltpu.get_barrier_semaphore()
+    devices = [{"tp": 1 - place.t}]
+    guide = Spread(place, nf, None, 0)
+    if scatters:
+        devices += [guide.chip(flip(place.q, d)) for d in range(1, place.n)]
+    else:
+        devices += [place.ring(1)[1], place.ring(-1)[1]]
+    if nf:
+        devices += [guide.partner()] + [guide.line(e) for e in guide.links]
+    for device in devices:
+        pl.semaphore_signal(bar, inc=1, device_id=device, device_id_type=MESH)
+    pl.semaphore_wait(bar, len(devices))
+
+
+class Work:
+    def __init__(self, place, nf, rows, scatters, spreads):
+        self.n = place.n
+        self.scatters, self.spreads = [], []
+        for blocks, w, sems in scatters:
+            self.scatters.append((Spread(place, nf, w, rows), blocks, sems))
+        for w, sems in spreads:
+            piece = Spread(place, nf, w, rows)
+            piece.use(*sems)
+            self.spreads.append(piece)
+
+    def scatter(self, i):
+        if i < len(self.scatters):
+            piece, blocks, sems = self.scatters[i]
+            piece.scatter(blocks, *sems)
+
+    def spread(self, i, places=None):
+        if i < len(self.spreads):
+            for d in range(self.n) if places is None else places:
+                self.spreads[i].spread(d)
+
+    def forward(self, i, places):
+        if i < len(self.spreads):
+            for d in places:
+                self.spreads[i].forward(d)
+
+    def complete(self, i):
+        if i < len(self.spreads):
+            self.spreads[i].complete()
+
+    def settle(self, done=()):
+        for i in range(len(self.spreads)):
+            if i not in done:
+                self.complete(i)
+            self.spreads[i].sent_all()
+        for piece, _, _ in self.scatters:
+            for d in range(self.n):
+                piece.arrived(d)
+            piece.scatter_sent()
+
+
+def weights_kernel(
+    n, nf, units, share, layers,
+    qkv, output, gate_up, down, *refs,
+):
+    place = Place(n)
+    rows, hidden = down.shape[1:]
+    w_a, w_g = refs[:2]
+    later = refs[2 : 2 + 3 * layers - 2]
+    a_first, g_first, raw_g, raw_d, cut_sems, raw_sems = refs[3 * layers : 3 * layers + 6]
+    sems = refs[3 * layers + 6 :]
+    a_blocks = [a_first] + list(later[: layers - 1])
+    g_blocks = [g_first] + list(later[layers - 1 : 2 * layers - 2])
+    d_blocks = list(later[2 * layers - 2 :])
+    cuts = []
+    for l in range(layers):
+        for q in range(n):
+            columns = pl.ds(q // share * VD, VD)
+            for i in range(4):
+                source = qkv.at[l, i, :, columns] if i < 3 else output.at[l, :, columns]
+                target = a_blocks[l].at[q, :, pl.ds(i * VD, VD)]
+                cuts.append(pltpu.make_async_copy(source, target, cut_sems.at[l, q, i]))
+    for copy in cuts[: 4 * n]:
+        copy.start()
+    raws = []
+    for l in range(layers):
+        raws.append(pltpu.make_async_copy(gate_up.at[l], raw_g.at[l], raw_sems.at[l, 0]))
+        raws.append(pltpu.make_async_copy(down.at[l], raw_d.at[l], raw_sems.at[l, 1]))
+    for copy in raws:
+        copy.start()
+    attention, forward = Spread(place, nf, w_a, rows), Spread(place, nf, w_g, rows)
+    attention.use(*sems[2:8])
+    enter(place, nf, True)
+    for copy in cuts[: 4 * n]:
+        copy.wait()
+    attention.scatter(a_first, *sems[:2])
+    for copy in cuts[4 * n :]:
+        copy.start()
+
+    def fill(target, j, at, value):
+        width = min(units, hidden - j * units)
+        target[j, :, at : at + width] = value(pl.ds(j * units, width))
+        if width < units:
+            target[j, :, at + width : at + units] = jnp.zeros((rows, units - width), BF)
+
+    def cut_gate_up(l):
+        raws[2 * l].wait()
+        for i in range(2):
+            for j in range(n):
+                fill(g_blocks[l], j, i * units, lambda at, i=i: raw_g[l, :, i, at])
+
+    cut_gate_up(0)
+    for d in range(n):
+        attention.arrived(d)
+        attention.spread(d)
+    forward.scatter(g_first, *sems[8:10])
+    for l in range(layers):
+        if l:
+            cut_gate_up(l)
+        raws[2 * l + 1].wait()
+        for j in range(n):
+            fill(d_blocks[l], j, 0, lambda at, l=l: raw_d[l, :, at])
+    for copy in cuts[4 * n :]:
+        copy.wait()
+    for d in range(n):
+        attention.forward(d)
+    attention.complete()
+    attention.scatter_sent()
+    attention.sent_all()
+    for d in range(n):
+        forward.arrived(d)
+    forward.scatter_sent()
 
 
 class Gather:
@@ -313,11 +524,12 @@
 
 
 def attention_forward(
-    n, layer, part, rank,
-    residual, gain, w_hbm, a_model, a_head, cosine, sine, query_bits, key_bits, lam,
-    middle, x_hbm, queries, keys, values, small, log_total, mixed, headed, side,
-    x, p, w, raised, copy_sems, *sems,
+    n, nf, layer, part, rank, plan,
+    residual, gain, w_hbm, a_model, a_head, cosine, sine, query_bits, key_bits, lam, *refs,
 ):
+    jobs, refs = plan.split(refs)
+    (middle, x_hbm, queries, keys, values, small, log_total, mixed, headed, side,
+     x, p, w, raised, copy_sems, *sems) = refs
     place = Place(n)
     chip_rows, width = 2 * x_hbm.shape[2], x_hbm.shape[3]
     tree = n * chip_rows
@@ -326,8 +538,10 @@
     gather, reduce = Gather(place, x, *sems[:6]), Reduce(place, p, *sems[6:])
     write_norm(x.at[place.q, place.t], residual, gain)
     block_diagonal(raised, (a_head[rank : 4 * rank], 3), rank, VD)
-    enter(place)
+    work = plan.work(place, nf, jobs)
+    enter(place, nf, bool(plan.scatters))
     gather.begin()
+    work.spread(0)
     load.wait()
 
     def project(q):
@@ -347,6 +561,8 @@
 
     for q in gather.chunks():
         project(q)
+    work.forward(0, range(1))
+    work.scatter(0)
     keep = pltpu.make_async_copy(x, x_hbm, copy_sems.at[1])
     keep.start()
     score_scale = HD ** (-0.5)
@@ -371,6 +587,8 @@
         side[rows] = mm_t(head, a_head[:rank]).astype(BF)
 
     row_blocks(tree, attend)
+    work.forward(0, range(1, n // 2))
+    work.scatter(1)
 
     for k in reduce.order:
         q = reduce.chips[k]
@@ -392,31 +610,38 @@
         middle[at] = residual[at] + total
 
     reduce.end(use)
+    work.forward(0, range(n // 2, n))
     keep.wait()
     gather.finish()
     reduce.finish()
+    work.settle()
 
 
 def ffn_forward(
-    n, units, rank,
-    residual, gain, w_hbm, a_model, e_model,
-    following, x_hbm, gates, ups, hidden, small, side,
-    x, p, w, raised, copy_sems, *sems,
+    n, nf, units, rank, plan,
+    residual, gain, w_hbm, a_model, e_model, *refs,
 ):
+    jobs, refs = plan.split(refs)
+    (following, x_hbm, gates, ups, hidden, small, side,
+     x, p, w, raised, copy_sems, *sems) = refs
     place = Place(n)
     chip_rows, width = 2 * x_hbm.shape[2], x_hbm.shape[3]
     tree = n * chip_rows
-    load = pltpu.make_async_copy(w_hbm, w, copy_sems.at[0])
+    load = pltpu.make_async_copy(w_hbm, w.at[:, pl.ds(0, 2 * units)], copy_sems.at[0])
     load.start()
     gather, reduce = Gather(place, x, *sems[:6]), Reduce(place, p, *sems[6:])
     write_norm(x.at[place.q, place.t], residual, gain)
     block_diagonal(raised, (e_model, 2), rank, units)
-    enter(place)
+    work = plan.work(place, nf, jobs)
+    enter(place, nf, bool(plan.scatters))
     gather.begin()
+    work.spread(0)
     load.wait()
     step = tile_of(units)
 
-    for q in gather.chunks():
+    for number, q in enumerate(gather.chunks()):
+        if number == n - 1:
+            work.forward(0, range(1))
         rows = pl.ds(pl.multiple_of(q * chip_rows, chip_rows), chip_rows)
         v = x[q].reshape(chip_rows, width)
         low = mm_t(v, a_model[4 * rank : 6 * rank]).astype(BF)
@@ -431,40 +656,61 @@
             hidden[rows, at] = (gate / (1.0 + jnp.exp(-gate)) * up).astype(BF)
 
         tiles(units, step, unit_tile)
+
+    work.forward(0, range(1, n // 2))
+    work.spread(1)
+    work.scatter(0)
+    keep = pltpu.make_async_copy(x, x_hbm, copy_sems.at[1])
+    keep.start()
+
+    work.forward(0, range(n // 2, n))
+    work.complete(0)
+    load = pltpu.make_async_copy(plan.late(jobs), w.at[:, pl.ds(2 * units, units)], copy_sems.at[0])
+    load.start()
+    load.wait()
+    for k in reduce.order:
+        q = reduce.chips[k]
+        rows = pl.ds(pl.multiple_of(q * chip_rows, chip_rows), chip_rows)
         made_hidden = hidden[rows]
-        low_hidden = mm_t(made_hidden, e_model[2 * rank : 3 * rank]).astype(BF)
-        side[rows] = low_hidden
+        low = mm_t(made_hidden, e_model[2 * rank : 3 * rank]).astype(BF)
+        side[rows] = low
 
         def out_tile(at):
             made = mm_t(made_hidden, w[at, 2 * units :])
-            made = made + ADAPTER_SCALE * mm(low_hidden, a_model[10 * rank : 11 * rank, at])
+            made = made + ADAPTER_SCALE * mm(low, a_model[10 * rank : 11 * rank, at])
             p[q, :, :, at] = made.astype(BF).reshape(2, chip_rows // 2, at.size)
 
         tiles(width, 512, out_tile)
-
-    keep = pltpu.make_async_copy(x, x_hbm, copy_sems.at[1])
-    keep.start()
+        reduce.offer(k)
+        if k == reduce.order[2]:
+            reduce.far()
+    for s in range(1, n // 2):
+        reduce.near(s)
 
     def use(at, total):
         following[at] = residual[at] + total
 
-    reduce.run(use)
+    reduce.end(use)
+    work.forward(1, range(n))
     keep.wait()
     gather.finish()
     reduce.finish()
+    work.settle((0,))
 
 
 def ffn_backward(
     n, units, rank,
-    grad, middle, gain, w_hbm, a_model, e_model, x_hbm, gates, ups, hidden, small, side,
+    grad, middle, gain, w_hbm, w_down_hbm, a_model, e_model, x_hbm, gates, ups, hidden, small, side,
     grad_out, grad_up_down, grad_in, grad_units, grad_e2,
     x, p, w, kept, dgu, dsmall, dside, raised, copy_sems, *sems,
 ):
     place = Place(n)
     chip_rows, width = 2 * x_hbm.shape[2], x_hbm.shape[3]
     tree = n * chip_rows
-    load = pltpu.make_async_copy(w_hbm, w, copy_sems.at[0])
+    load = pltpu.make_async_copy(w_hbm, w.at[:, pl.ds(0, 2 * units)], copy_sems.at[0])
     load.start()
+    load_down = pltpu.make_async_copy(w_down_hbm, w.at[:, pl.ds(2 * units, units)], copy_sems.at[2])
+    load_down.start()
     fetch = pltpu.make_async_copy(x_hbm, kept, copy_sems.at[1])
     fetch.start()
     gather, reduce = Gather(place, x, *sems[:6]), Reduce(place, p, *sems[6:])
@@ -477,6 +723,7 @@
     enter(place)
     gather.begin()
     load.wait()
+    load_down.wait()
     step = tile_of(units)
 
     for q in gather.chunks():
@@ -641,18 +888,59 @@
     reduce.finish()
 
 
-def call(kernel, collective, ins, outs, scratch):
+class Plan:
+    def __init__(self, n, nf, rows, scatters, spreads):
+        self.n, self.nf, self.rows = n, nf, rows
+        self.scatters, self.spreads = scatters, spreads
+
+    def ins(self):
+        return [(blocks, True) for blocks, _ in self.scatters] + [(w, True) for w in self.spreads]
+
+    def outs(self):
+        made = [(shape, BF, True) for _, shape in self.scatters]
+        return made + [(w.shape, BF, True) for w in self.spreads]
+
+    def semaphores(self):
+        made = Spread.scatter_semaphores(self.n) * len(self.scatters)
+        return made + Spread.spread_semaphores(self.n, self.nf) * len(self.spreads)
+
+    def split(self, refs):
+        a, b = len(self.scatters), len(self.spreads)
+        count = 2 * a + 6 * b
+        refs = list(refs)
+        taken = refs[: a + b], refs[a + b : 2 * (a + b)], refs[len(refs) - count :]
+        return taken, refs[2 * (a + b) : len(refs) - count]
+
+    def work(self, place, nf, jobs):
+        a, b = len(self.scatters), len(self.spreads)
+        ins, outs, sems = jobs
+        scatters = [(ins[i], outs[i], sems[2 * i : 2 * i + 2]) for i in range(a)]
+        spreads = [(outs[a + i], sems[2 * a + 6 * i : 2 * a + 6 * i + 6]) for i in range(b)]
+        return Work(place, nf, self.rows, scatters, spreads)
+
+    def late(self, jobs):
+        return jobs[1][len(self.scatters)]
+
+
+def call(kernel, collective, ins, outs, scratch, plan=None):
     spec = lambda hbm: pl.BlockSpec(memory_space=pl.ANY if hbm else pltpu.VMEM)
-    return pl.pallas_call(
+    aliases = {}
+    if plan is not None:
+        first_in, count = len(ins), len(plan.scatters)
+        aliases = {first_in + count + i: count + i for i in range(len(plan.spreads))}
+        ins, outs, scratch = ins + plan.ins(), plan.outs() + outs, scratch + plan.semaphores()
+    made = pl.pallas_call(
         kernel,
         out_shape=[jax.ShapeDtypeStruct(shape, kind) for shape, kind, _ in outs],
         in_specs=[spec(hbm) for _, hbm in ins],
         out_specs=[spec(hbm) for _, _, hbm in outs],
         scratch_shapes=scratch,
+        input_output_aliases=aliases,
         compiler_params=pltpu.CompilerParams(
             collective_id=collective, has_side_effects=True, vmem_limit_bytes=60 << 20
         ),
     )(*[array for array, _ in ins])
+    return list(made)
 
 
 def line_bits(parent_row, seg):
@@ -686,31 +974,6 @@
 
 def swap_trees(x, nf, nc):
     return permute(x, nf, nc, lambda f_hi, f_lo, c_hi, c_lo: (f_hi, c_hi, f_lo, c_lo))
-
-
-def spread_weights(blocks, q, g, nf, nc):
-    n, h = nc, nc // 2
-    rows, width = blocks.shape[1:]
-    mine = jnp.zeros((n, rows, width), BF)
-    for d in range(n):
-        part = lax.dynamic_index_in_dim(blocks, q ^ d, 0, keepdims=False)
-        if d:
-
-            def exchange(f_hi, f_lo, c_hi, c_lo, d=d):
-                to = (f_lo * h + c_lo) ^ d
-                return f_hi, to // h, c_hi, to % h
-
-            part = permute(part, nf, nc, exchange)
-        mine = lax.dynamic_update_index_in_dim(mine, part, q ^ d, 0)
-    gathered = jnp.zeros((nf, n, rows, width), BF)
-    gathered = lax.dynamic_update_index_in_dim(gathered, mine, g, 0)
-    partner = permute(mine, nf, nc, lambda a, b, c, d: (a, b, c ^ 1, d))
-    gathered = lax.dynamic_update_index_in_dim(gathered, partner, g ^ 1, 0)
-    for d in range(1, nf // 2):
-        for e, held in ((0, mine), (1, partner)):
-            moved = permute(held, nf, nc, lambda a, b, c, k, d=d: (a ^ d, b, c, k))
-            gathered = lax.dynamic_update_index_in_dim(gathered, moved, g ^ (2 * d + e), 0)
-    return gathered.reshape(nf * n * rows, width)
 
 
 def shards(
@@ -733,7 +996,7 @@
 ):
     n = nc
     place = Place(n)
-    q, t, g = place.q, place.t, place.f_hi * 2 + place.c_hi
+    q, t = place.q, place.t
     tokens_dev, width = tokens.shape
     rows = tokens_dev // 2
     tree = tokens_dev * n
@@ -786,50 +1049,68 @@
 
     e_model = unit_columns(e_all)
 
-    def blocks_of(l):
-        def heads(x):
-            cut = x.reshape(weight_rows, heads_tp, VD).transpose(1, 0, 2)
-            return jnp.repeat(cut, share, axis=0) if share > 1 else cut
-
-        def unit(x):
-            x = jnp.pad(x, ((0, 0), (0, n * units - hidden_tp)))
-            return x.reshape(weight_rows, n, units).transpose(1, 0, 2)
-
-        w = query_key_value_weight[l]
-        v = gate_up_weight[l]
-        attention = jnp.concatenate([heads(w[:, i]) for i in range(3)] + [heads(output_weight[l])], axis=2)
-        forward = jnp.concatenate([unit(v[:, 0]), unit(v[:, 1]), unit(down_weight[l])], axis=2)
-        return attention, forward
-
-    weights = []
-    for l in range(layers):
-        attention, forward = blocks_of(l)
-        weights.append((spread_weights(attention, q, g, nf, nc), spread_weights(forward, q, g, nf, nc)))
-
     part = 1.0 / share
+    vmem = lambda *spec: pltpu.VMEM(*spec)
     calls = [0]
     whole_x = ((n, 2, rows, width), BF)
     sems = Gather.semaphores(n) + Reduce.scratch(n, rows, width)
-    pair = pltpu.SemaphoreType.DMA((2,))
-    vmem = lambda *spec: pltpu.VMEM(*spec)
+    pair = pltpu.SemaphoreType.DMA((3,))
     big = [vmem(*whole_x), vmem(*whole_x)]
 
-    def run(kernel, ins, outs, scratch):
+    def run(kernel, ins, outs, scratch, plan=None):
         calls[0] += 1
-        return call(kernel, calls[0], ins, outs, scratch)
+        return call(kernel, calls[0], ins, outs, scratch, plan)
 
     near = lambda *arrays: [(array, False) for array in arrays]
     far = lambda *arrays: [(array, True) for array in arrays]
     out = lambda shape, kind, hbm=False: (shape, kind, hbm)
 
+    dma = pltpu.SemaphoreType.DMA
+    c_a, c_g, c_d = 4 * VD, 2 * units, units
+    tall = nf * n * weight_rows
+    cut = lambda columns: out((n, weight_rows, columns), BF)
+    calls[0] += 1
+    made = call(
+        functools.partial(weights_kernel, n, nf, units, share, layers),
+        calls[0],
+        far(jnp.transpose(query_key_value_weight, (0, 2, 1, 3)), output_weight, gate_up_weight, down_weight),
+        [out((tall, c_a), BF, True), out((tall, c_g), BF, True)]
+        + [cut(c_a)] * (layers - 1)
+        + [cut(c_g)] * (layers - 1)
+        + [cut(c_d)] * layers,
+        [
+            vmem((n, weight_rows, c_a), BF),
+            vmem((n, weight_rows, c_g), BF),
+            vmem((layers, weight_rows, 2, hidden_tp), BF),
+            vmem((layers, weight_rows, hidden_tp), BF),
+            dma((layers, n, 4)),
+            dma((layers, 2)),
+        ]
+        + Spread.scatter_semaphores(n)
+        + Spread.spread_semaphores(n, nf)
+        + Spread.scatter_semaphores(n),
+    )
+    w_a, w_g = [made[0]], [made[1]]
+    w_d = []
+    a_blocks = [None] + made[2 : 1 + layers]
+    g_blocks = [None] + made[1 + layers : 2 * layers]
+    d_blocks = made[2 * layers :]
+
+    def plan_of(scatters, spreads):
+        return Plan(n, nf, weight_rows, scatters, spreads)
+
     saved = []
     for l in range(layers):
-        w_attention, w_forward = weights[l]
+        last = l == layers - 1
+        w_attention = w_a[l]
         lam = lax.dynamic_slice_in_dim(difference_lambda[l], head, 1).reshape(1, 1)
         gain_a, gain_f = gains[l, 0:1], gains[l, 1:2]
         shared = (a_model[l], a_head[l], cosine, sine, query_bits, key_bits, lam)
+        plan = plan_of(
+            [(d_blocks[l], (tall, c_d))] + ([] if last else [(a_blocks[l + 1], (tall, c_a))]), [w_g[l]]
+        )
         got = run(
-            functools.partial(attention_forward, n, l, part, rank),
+            functools.partial(attention_forward, n, nf, l, part, rank, plan),
             near(residual, gain_a) + far(w_attention) + near(*shared),
             [
                 out((rows, width), F32),
@@ -844,11 +1125,17 @@
                 out((tree, rank), BF),
             ],
             big + [vmem((width, 4 * VD), BF), vmem((3 * rank, 3 * VD), BF), pair] + sems,
+            plan,
         )
-        middle, kept = got[0], got[1:]
+        w_d.append(got[0])
+        if not last:
+            w_a.append(got[1])
+        w_g[l] = got[2 - last]
+        middle, kept = got[3 - last], got[4 - last :]
+        plan = plan_of([] if last else [(g_blocks[l + 1], (tall, c_g))], [w_d[l]] + ([] if last else [w_a[l + 1]]))
         ffn = run(
-            functools.partial(ffn_forward, n, units, rank),
-            near(middle, gain_f) + far(w_forward) + near(a_model[l], e_model[l]),
+            functools.partial(ffn_forward, n, nf, units, rank, plan),
+            near(middle, gain_f) + far(w_g[l]) + near(a_model[l], e_model[l]),
             [
                 out((rows, width), F32),
                 out(*whole_x, True),
@@ -859,18 +1146,23 @@
                 out((tree, rank), BF),
             ],
             big + [vmem((width, 3 * units), BF), vmem((2 * rank, 2 * units), BF), pair] + sems,
+            plan,
         )
+        if not last:
+            w_g.append(ffn[0])
+            w_a[l + 1] = ffn[2]
+        w_d[l] = ffn[1 - last]
+        ffn = ffn[3 - 2 * last :]
         saved.append((residual, middle, gain_a, gain_f, shared, kept, ffn[1:]))
         residual = ffn[0]
 
     grad = own_cotangent.astype(F32)
     model_grads, hidden_grads = [], []
     for l in reversed(range(layers)):
-        w_attention, w_forward = weights[l]
         residual_in, middle, gain_a, gain_f, shared, kept, ffn = saved[l]
         grad, grad_a10, grad_a45, grad_e01, grad_e2 = run(
             functools.partial(ffn_backward, n, units, rank),
-            near(grad, middle, gain_f) + far(w_forward) + near(a_model[l], e_model[l]) + far(ffn[0]) + near(*ffn[1:]),
+            near(grad, middle, gain_f) + far(w_g[l], w_d[l]) + near(a_model[l], e_model[l]) + far(ffn[0]) + near(*ffn[1:]),
             [
                 out((rows, width), F32),
                 out((rank, width), BF),
@@ -892,7 +1184,7 @@
         )
         grad, grad_a9, grad_a012, grad_head = run(
             functools.partial(attention_backward, n, l, part, rank),
-            near(grad, residual_in, gain_a) + far(w_attention) + near(*shared) + far(kept[0]) + near(*kept[1:]),
+            near(grad, residual_in, gain_a) + far(w_a[l]) + near(*shared) + far(kept[0]) + near(*kept[1:]),
             [
                 out((rows, width), F32),
                 out((rank, width), BF),

time: 1280 us -> 1080 us (0.84)
  waiting for transfers between devices: 338 us -> 42.4 us
  Pallas kernels: 626 us -> 890 us
  local copies, waits for them, and re-layouts: 204 us -> 62.4 us
  starting transfers between devices: 36.7 us -> 19.7 us
    ppermute x30 -> x6, waiting for transfers between devices: 338 us -> 42.4 us  [permute(): return lax.ppermute(x, ('fsdp', 'ctx'), pairs)]
    pallas_call x8 -> x9, Pallas kernels: 584 us -> 843 us  [call(): pl.pallas_call(kernel, out_shape=[jax.ShapeDtypeStruct(shape, kind) for s...]
    dynamic_update_slice x28 -> x0, local copies, waits for them, and re-layouts: 42.8 us -> none  [the longest x8 15.4 us: spread_weights(): lax.dynamic_update_index_in_dim(gathered, moved, g ^ 2 * d + e, 0)]
    another operation x28 -> x4, local copies, waits for them, and re-layouts: 40.5 us -> 0.65 us  [the longest x16 27.5 us: heads(): cut = x.reshape(weight_rows, heads_tp, VD).transpose(1, 0, 2)]
    ppermute x30 -> x6, starting transfers between devices: 35.5 us -> 18.5 us  [permute(): return lax.ppermute(x, ('fsdp', 'ctx'), pairs)]
  transfers between devices with their start and end apart: 33 -> 9, of which waited for: 9 -> 2; matrix products, arithmetic and copies ran while one was open for 13% -> 4% of each run, Pallas kernels for 24% -> 11%
where the time goes in v2:
time: 1080 us; the launch traced here: 1070 us
  Pallas kernels  890 us (82%)
  local copies, waits for them, and re-layouts  62.4 us (6%)
  waiting for transfers between devices  42.4 us (4%)
  other arithmetic  24.9 us (2%)
  starting transfers between devices  19.7 us (2%)
  between operations  17.9 us (2%)
  blocking collectives  17.8 us (2%)
    pallas_call x9, Pallas kernels, call(): pl.pallas_call(kernel, out_shape=[jax.ShapeDtypeStruct(shape, kind) for s...  843 us
    pallas_call x1, Pallas kernels, group_reduce(): pl.pallas_call(functools.partial(rs_kernel, n), out_shape=jax.ShapeDtypeS...  46.4 us
    ppermute x6, waiting for transfers between devices, permute(): return lax.ppermute(x, ('fsdp', 'ctx'), pairs)  42.4 us
  transfers between devices with their start and end apart: 9, of which 2 were waited for; matrix products, arithmetic and copies ran while one was open for 4% of the time, Pallas kernels for 11%

profile of v2, /device:TPU:3, one launch (start us, length us, event | category | flops | bytes accessed | tf_op | source)
XLA Modules:
  0.0 1074.8 jit_solution(12780982611080678348)
XLA Ops:
  8.0 9.5 all_gather.12
  18.9 2.2 collective-permute-start.1
  22.0 4.8 collective-permute-start
  26.8 1.9 constant_dynamic-slice_fusion
  28.7 2.2 collective-permute-start.4
  31.8 71.4 %shard_map.165 = (bf16[2048,1024]{1,0:T(8,128)(2,1)}, bf16[2048,1536]{1,0:T(8,128)(2,1)}, bf16[4,128,1024]{2,1,0:T(8,128)(2,1)}, bf16[4,128,1536]{2,1,0:T(8,128)...) custom-call(bf16[2,3,128,1024]{3,2,1,0:T(8,128)(2,1)} %bitcast.79, bf16[2,128,1024]{2,1,0:T(8,128)(2,1)} %output.1, ...), custom_call_target="tpu_custom_call" | custom-call | tf_op jit(solution)/shard_map/pallas_call | solution.py:932
  106.4 1.1 dynamic-slice_bitcast_fusion
  107.5 1.5 constant_dynamic-slice_fusion.5
  109.0 1.4 reshape.204
  111.5 1.3 constant_dynamic-slice_fusion.3
  115.0 1.4 squeeze.59.a_model
  116.4 1.0 copy.86.query_bits
  118.2 1.4 squeeze.64.a_model
  120.3 1.9 fusion.3
  122.2 1.3 pad_maximum_fusion.2
  123.5 2.1 reshape.236
  126.1 1.8 reshape.234.residual
  129.5 1.8 reshape.235.grad
  131.4 162.1 %shard_map.166 = (bf16[2048,768]{1,0:T(8,128)(2,1)}, bf16[2048,1024]{1,0:T(8,128)(2,1)}, bf16[2048,1536]{1,0:T(8,128)(2,1)}, f32[128,2048]{1,0:T(8,128)}, bf16[4...) custom-call(f32[128,2048]{1,0:T(8,128)} %reshape.234.residual, ...), custom_call_target="tpu_custom_call", output_to_operand_aliasing={{2}: (12, {})} | custom-call | tf_op jit(solution)/shard_map/pallas_call | solution.py:932
  293.4 136.7 %shard_map.167 = (bf16[2048,1536]{1,0:T(8,128)(2,1)}, bf16[2048,768]{1,0:T(8,128)(2,1)}, bf16[2048,1024]{1,0:T(8,128)(2,1)}, f32[128,2048]{1,0:T(8,128)}, bf16[4...) custom-call(f32[128,2048]{1,0:T(8,128)} %get-tuple-element.75.residu, ...), custom_call_target="tpu_custom_call", output_to_operand_aliasing={{1}: (6, {}), {2}: (7, {})} | custom-call | tf_op jit(solution)/shard_map/pallas_call | solution.py:932
  430.1 125.4 %shard_map.168 = (bf16[2048,768]{1,0:T(8,128)(2,1)}, bf16[2048,1536]{1,0:T(8,128)(2,1)}, f32[128,2048]{1,0:T(8,128)}, bf16[4,2,128,2048]{3,2,1,0:T(8,128)(2,1)},...) custom-call(f32[128,2048]{1,0:T(8,128)} %get-tuple-element.80.residu, ...), custom_call_target="tpu_custom_call", output_to_operand_aliasing={{1}: (11, {})} | custom-call | tf_op jit(solution)/shard_map/pallas_call | solution.py:932
  555.5 89.0 %shard_map.169 = (bf16[2048,768]{1,0:T(8,128)(2,1)}, f32[128,2048]{1,0:T(8,128)}, bf16[4,2,128,2048]{3,2,1,0:T(8,128)(2,1)}, bf16[1024,768]{1,0:T(8,128)(2,1)}, ...) custom-call(f32[128,2048]{1,0:T(8,128)} %get-tuple-element.84.residu, ...), custom_call_target="tpu_custom_call", output_to_operand_aliasing={{0}: (5, {})} | custom-call | tf_op jit(solution)/shard_map/pallas_call | solution.py:932
  644.5 61.0 %shard_map.170 = (f32[128,2048]{1,0:T(8,128)}, bf16[16,2048]{1,0:T(8,128)(2,1)}, bf16[32,2048]{1,0:T(8,128)(2,1)}, f32[32,768]{1,0:T(8,128)}, f32[16,768]{1,0:T(8,128)}) custom-call(f32[128,2048]{1,0:T(8,128)} %reshape.235.grad, f32[128,2048]{1,0:T(8,128)} %get-tuple-element.84.residual.middle, f32[1,2048]{1,0:T(1,128)} %get-tuple-element.156.gain, ...), custom_call_target="tpu_custom_call" | custom-call | tf_op jit(solution)/shard_map/pallas_call | solution.py:932
  705.5 70.2 %shard_map.171 = (f32[128,2048]{1,0:T(8,128)}, bf16[16,2048]{1,0:T(8,128)(2,1)}, bf16[48,2048]{1,0:T(8,128)(2,1)}, f32[64,256]{1,0:T(8,128)}) custom-call(f32[128,2048]{1,0:T(8,128)} %get-tuple-element.95.grad, f32[128,2048]{1,0:T(8,128)} %get-tuple-element.80.residual, f32[1,2048]{1,0:T(1,128)} %get-tuple-element.157.gain, ...), custom_call_target="tpu_custom_call" | custom-call | tf_op jit(solution)/shard_map/pallas_call | solution.py:932
  775.7 59.8 %shard_map.172 = (f32[128,2048]{1,0:T(8,128)}, bf16[16,2048]{1,0:T(8,128)(2,1)}, bf16[32,2048]{1,0:T(8,128)(2,1)}, f32[32,768]{1,0:T(8,128)}, f32[16,768]{1,0:T(8,128)}) custom-call(f32[128,2048]{1,0:T(8,128)} %get-tuple-element.105.grad, f32[128,2048]{1,0:T(8,128)} %get-tuple-element.75.residual.middle, f32[1,2048]{1,0:T(1,128)} %get-tuple-element.158.gain, ...), custom_call_target="tpu_custom_call" | custom-call | tf_op jit(solution)/shard_map/pallas_call | solution.py:932
  835.5 67.8 %shard_map.173 = (f32[128,2048]{1,0:T(8,128)}, bf16[16,2048]{1,0:T(8,128)(2,1)}, bf16[48,2048]{1,0:T(8,128)(2,1)}, f32[64,256]{1,0:T(8,128)}) custom-call(f32[128,2048]{1,0:T(8,128)} %get-tuple-element.113.grad, f32[128,2048]{1,0:T(8,128)} %reshape.234.residual, f32[1,2048]{1,0:T(1,128)} %get-tuple-element.159.gain, ...), custom_call_target="tpu_custom_call" | custom-call | tf_op jit(solution)/shard_map/pallas_call | solution.py:932
  903.4 1.1 reshape.210
  906.9 1.1 reshape.226
  908.0 2.1 copy.108
  910.6 4.6 dynamic_update_slice.14
  916.4 4.6 dynamic_update_slice.15
  921.8 1.8 reshape.228
  923.8 2.4 reshape.229
  927.7 1.8 reshape.209
  929.5 5.4 collective-permute-start.5
  934.9 8.9 fusion.2
  943.9 3.5 reshape.230.p_ref
  947.4 46.4 %shard_map.174 = f32[160,1024]{1,0:T(8,128)} custom-call(bf16[4,2,160,1024]{3,2,1,0:T(8,128)(2,1)} %reshape.230.p_ref), custom_call_target="tpu_custom_call" | custom-call | tf_op jit(solution)/shard_map/pallas_call | solution.py:441
  993.8 1.1 convert_element_type.92
  994.9 1.9 collective-permute-start.7
  996.9 16.9 %collective-permute-done.7 = bf16[160,1024]{1,0:T(8,128)(2,1)S(1)} collective-permute-done((bf16[160,1024]{1,0:T(8,128)(2,1)S(1)}, bf16[160,1024]{1,0:T(8,128)(2,1)S(1)}, u32[]{:S(2)}, u32[]{:S(2)}) %collective-permute-start.7) | collective-permute-done | bytes 327712 | tf_op jit(solution)/shard_map/ppermute | solution.py:972
  1016.0 1.9 collective-permute-start.2
  1018.5 25.4 %collective-permute-done.2 = bf16[128,2048]{1,0:T(8,128)(2,1)S(1)} collective-permute-done((bf16[128,2048]{1,0:T(8,128)(2,1)S(1)}, bf16[128,2048]{1,0:T(8,128)(2,1)S(1)}, u32[]{:S(2)}, u32[]{:S(2)}) %collective-permute-start.2) | collective-permute-done | bytes 524320 | tf_op jit(solution)/shard_map/ppermute | solution.py:972
  1045.8 8.3 all-reduce.2
  1054.1 1.2 maximum_select_fusion.1
  1055.4 3.1 maximum_select_fusion
  1058.5 2.3 reshape.231
  1061.4 4.0 multiply_reduce_fusion
  (151 shorter events, 24.8 us)
Async XLA Ops:
  7.2 14.0 %copy-start = (bf16[256,2048]{1,0:T(8,128)(2,1)S(1)}, bf16[256,2048]{1,0:T(8,128)(2,1)}, u32[]{:S(2)}) copy-start(bf16[256,2048]{1,0:T(8,128)(2,1)} %param.14) | copy-start | bytes 3145732
  7.2 23.8 %copy-start.19 = (f32[2,4]{1,0:T(2,128)S(1)}, f32[2,4]{1,0:T(2,128)}, u32[]{:S(2)}) copy-start(f32[2,4]{1,0:T(2,128)} %param.21) | copy-start | bytes 100
  7.2 23.8 %copy-start.18 = (f32[2,2,2048]{2,1,0:T(2,128)S(1)}, f32[2,2,2048]{2,1,0:T(2,128)}, u32[]{:S(2)}) copy-start(f32[2,2,2048]{2,1,0:T(2,128)} %param.20) | copy-start | bytes 98308
  7.2 1051.3 %all-gather.3.cloned.1.call-start = ((), (), s32[]{:S(2)}) async-start(), calls=%async_computation | async-start | bytes 1638400 | tf_op jit(solution)/shard_map/all_gather | solution.py:1248
  18.9 84.9 %collective-permute-start.1 = (s32[2062]{0:T(1024)S(1)}, s32[2062]{0:T(1024)S(1)}, u32[]{:S(2)}, u32[]{:S(2)}) collective-permute-start(s32[2062]{0:T(1024)S(1)} %concatenate.39), channel_id=1, source_target_pairs={{0,0},{2,2},{4,8},{6,10},{8,4},{10,6},{12,12},{14,14},{16,16},{18,... | collective-permute-start | bytes 24752 | tf_op jit(solution)/shard_map/ppermute | solution.py:972
  22.0 101.5 %collective-permute-start = (bf16[128,2048]{1,0:T(8,128)(2,1)}, bf16[128,2048]{1,0:T(8,128)(2,1)}, u32[]{:S(2)}, u32[]{:S(2)}) collective-permute-start(bf16[128,2048]{1,0:T(8,128)(2,1)} %constant_dynamic-slice_fusion.6), channel_id=1, source_target_pairs={{0,0},{2,2},{4,8},{6,10},{8,4},{10,6},{12,12},{14,14},{16,16},{18,... | collective-permute-start | bytes 1572872 | tf_op jit(solution)/shard_map/ppermute | solution.py:972
  28.7 99.2 %collective-permute-start.4 = (bf16[128,2048]{1,0:T(8,128)(2,1)}, bf16[128,2048]{1,0:T(8,128)(2,1)S(1)}, u32[]{:S(2)}, u32[]{:S(2)}) collective-permute-start(bf16[128,2048]{1,0:T(8,128)(2,1)} %constant_dynamic-slice_fusion), channel_id=1, source_target_pairs={{0,0},{2,2},{4,8},{6,10},{8,4},{10,6},{12,12},{14,14},{16,16},{18,... | collective-permute-start | bytes 1572872 | tf_op jit(solution)/shard_map/ppermute | solution.py:972
  835.5 69.3 %copy-start.7 = (bf16[32,2048]{1,0:T(8,128)(2,1)S(1)}, bf16[32,2048]{1,0:T(8,128)(2,1)}, u32[]{:S(2)}) copy-start(bf16[32,2048]{1,0:T(8,128)(2,1)} %get-tuple-element.126) | copy-start | bytes 393220
  903.3 1.8 copy-start.15
  903.3 1.9 copy-start.14
  903.3 2.1 copy-start.13
  903.4 2.2 copy-start.5
  904.9 1.1 copy-start.6
  905.2 1.2 copy-start.12
  905.3 1.1 copy-start.11
  905.4 1.1 copy-start.10
  908.0 2.1 copy-start.9
  908.0 2.1 copy-start.17
  910.1 5.8 copy-start.8
  910.1 5.8 copy-start.16
  923.6 2.7 copy-start.3
  929.5 88.4 %collective-permute-start.5 = (f32[128,2048]{1,0:T(8,128)}, f32[128,2048]{1,0:T(8,128)}, u32[]{:S(2)}, u32[]{:S(2)}) collective-permute-start(f32[128,2048]{1,0:T(8,128)} %reshape.209), channel_id=1, source_target_pairs={{0,0},{2,2},{4,8},{6,10},{8,4},{10,6},{12,12},{14,14},{16,16},{18,... | collective-permute-start | bytes 3145736 | tf_op jit(solution)/shard_map/ppermute | solution.py:972
  947.4 67.1 %copy-start.2 = (f32[128,2048]{1,0:T(8,128)S(1)}, f32[128,2048]{1,0:T(8,128)}, u32[]{:S(2)}) copy-start(f32[128,2048]{1,0:T(8,128)} %get-tuple-element.87) | copy-start | bytes 3145732
  994.9 18.9 %collective-permute-start.7 = (bf16[160,1024]{1,0:T(8,128)(2,1)S(1)}, bf16[160,1024]{1,0:T(8,128)(2,1)S(1)}, u32[]{:S(2)}, u32[]{:S(2)}) collective-permute-start(bf16[160,1024]{1,0:T(8,128)(2,1)S(1)} %convert_element_type.92), channel_id=1, source_target_pairs={{0,0},{2,2},{4,8},{6,10},{8,4},{10,6},{12,12},{14,14},{16,16},{18,... | collective-permute-start | bytes 983048 | tf_op jit(solution)/shard_map/ppermute | solution.py:972
  1013.8 0.7 copy-start.4
  1014.6 29.9 %copy-start.20 = (u32[32]{0:T(128)S(1)}, u32[32]{0:T(128)}, u32[]{:S(2)}) copy-start(u32[32]{0:T(128)} %constant.114) | copy-start | bytes 388
  1016.0 27.9 %collective-permute-start.2 = (bf16[128,2048]{1,0:T(8,128)(2,1)S(1)}, bf16[128,2048]{1,0:T(8,128)(2,1)S(1)}, u32[]{:S(2)}, u32[]{:S(2)}) collective-permute-start(bf16[128,2048]{1,0:T(8,128)(2,1)S(1)} %reshape.207), channel_id=1, source_target_pairs={{0,0},{2,2},{4,8},{6,10},{8,4},{10,6},{12,12},{14,14},{16,16},{18,... | collective-permute-start | bytes 1572872 | tf_op jit(solution)/shard_map/ppermute | solution.py:972
  1017.9 37.5 %collective-permute-start.6 = (f32[128,2048]{1,0:T(8,128)}, f32[128,2048]{1,0:T(8,128)S(1)}, u32[]{:S(2)}, u32[]{:S(2)}) collective-permute-start(f32[128,2048]{1,0:T(8,128)} %collective-permute-done.5), channel_id=1, source_target_pairs={{0,1},{1,0},{2,3},{3,2},{4,5},{5,4},{6,7},{7,6},{8,9},{9,8},{10,11... | collective-permute-start | bytes 3145736 | tf_op jit(solution)/shard_map/ppermute | solution.py:1260
  1043.9 10.2 collective-permute-start.3
  1065.4 2.3 copy-start.1
Sparse Core Ops, SparseCore 0:
  1014.7 36.9 all-gather.2

commit v3 on v2

--- a/solution.py
+++ b/solution.py
@@ -26,6 +26,8 @@
         self.f_hi, self.f_lo = self.f // 2, self.f % 2
         self.c_hi, self.c_lo = self.c // self.h, self.c % self.h
         self.q = self.f_lo * self.h + self.c_lo
+        self.away = self.f_lo + self.c_hi - 2 * self.f_lo * self.c_hi
+        self.home = {"fsdp": self.f_hi * 2 + self.c_hi, "ctx": self.f_lo * self.h + self.c_lo}
         self.pos = self.f_lo * (n - 1) + (1 - 2 * self.f_lo) * self.c_lo
 
     def ring(self, k):
@@ -60,7 +62,7 @@
         self.g = place.f_hi * 2 + place.c_hi
         self.links = range(1, nf // 2)
         self.scattered, self.sent = [], []
-        self.to_partner, self.along, self.onward = {}, {}, {}
+        self.to_partner, self.along, self.onward, self.got = {}, {}, {}, []
 
     @staticmethod
     def scatter_semaphores(n):
@@ -117,14 +119,21 @@
         for e in self.links:
             self.along[d, e] = remote(at, at, send_y.at[d, e - 1], recv_y.at[d, e - 1], self.line(e))
 
+    def landed(self, d):
+        if d in self.to_partner and d not in self.got:
+            self.to_partner[d].wait_recv()
+            self.got.append(d)
+
     def forward(self, d):
         send, recv = self.sems[4:]
-        self.to_partner[d].wait_recv()
+        self.landed(d)
         at = self.block(flip(self.g, 1), flip(self.place.q, d))
         for e in self.links:
             self.onward[d, e] = remote(at, at, send.at[d, e - 1], recv.at[d, e - 1], self.line(e))
 
     def complete(self):
+        for d in list(self.to_partner):
+            self.landed(d)
         for copy in list(self.along.values()) + list(self.onward.values()):
             copy.wait_recv()
 
@@ -134,24 +143,87 @@
                 copy.wait_send()
 
 
-def enter(place, nf=0, scatters=False):
+def enter(place, nf=0, scatters=False, home=False, ring=True, trees=0):
     bar = pltpu.get_barrier_semaphore()
     devices = [{"tp": 1 - place.t}]
     guide = Spread(place, nf, None, 0)
     if scatters:
         devices += [guide.chip(flip(place.q, d)) for d in range(1, place.n)]
-    else:
+    elif ring:
         devices += [place.ring(1)[1], place.ring(-1)[1]]
     if nf:
         devices += [guide.partner()] + [guide.line(e) for e in guide.links]
+    devices += [{"fsdp": flip(place.f, e)} for e in range(1, trees)]
     for device in devices:
         pl.semaphore_signal(bar, inc=1, device_id=device, device_id_type=MESH)
-    pl.semaphore_wait(bar, len(devices))
+    count = len(devices)
+    if home:
+
+        @pl.when(place.away == 1)
+        def greet():
+            pl.semaphore_signal(bar, inc=1, device_id=place.home, device_id_type=MESH)
+
+        count = count + place.away
+    pl.semaphore_wait(bar, count)
+
+
+class Home:
+    def __init__(self, place, out, send, recv):
+        self.place, self.out = place, out
+        self.send, self.recv = send, recv
+
+    @staticmethod
+    def semaphores():
+        dma = pltpu.SemaphoreType.DMA
+        return [dma((2,)), dma((2,))]
+
+    def start(self, rows):
+        place, slot = self.place, self.out.at[self.place.t]
+        far = pltpu.make_async_remote_copy(
+            src_ref=rows, dst_ref=slot, send_sem=self.send.at[0], recv_sem=self.recv.at[0],
+            device_id=place.home, device_id_type=MESH,
+        )
+        near = pltpu.make_async_copy(rows, slot, self.recv.at[0])
+        self.far = far
+        pl.when(place.away == 1)(far.start)
+        pl.when(place.away == 0)(near.start)
+        self.near = near
+
+    def land(self, share=True):
+        pl.when(self.place.away == 1)(self.far.wait)
+        pl.when(self.place.away == 0)(self.near.wait)
+        if share:
+            slot = self.out.at[self.place.t]
+            self.across = remote(slot, slot, self.send.at[1], self.recv.at[1], {"tp": 1 - self.place.t})
+
+    def finish(self):
+        self.across.wait()
+
+
+class TreeMove(Home):
+    def __init__(self, place, rows, out, send, recv):
+        super().__init__(place, out, send, recv)
+        self.rows = rows
+        self.slot = out.at[place.f]
+
+    def start(self):
+        place = self.place
+        target = self.out.at[place.f_hi * 2 + place.c_hi]
+        self.far = pltpu.make_async_remote_copy(
+            src_ref=self.rows, dst_ref=target, send_sem=self.send.at[0], recv_sem=self.recv.at[0],
+            device_id=place.home, device_id_type=MESH,
+        )
+        self.near = pltpu.make_async_copy(self.rows, target, self.recv.at[0])
+        pl.when(place.away == 1)(self.far.start)
+        pl.when(place.away == 0)(self.near.start)
+
+    def land(self):
+        super().land(False)
 
 
 class Work:
-    def __init__(self, place, nf, rows, scatters, spreads):
-        self.n = place.n
+    def __init__(self, place, nf, rows, scatters, spreads, schedule):
+        self.n, self.schedule = place.n, schedule
         self.scatters, self.spreads = [], []
         for blocks, w, sems in scatters:
             self.scatters.append((Spread(place, nf, w, rows), blocks, sems))
@@ -160,34 +232,36 @@
             piece.use(*sems)
             self.spreads.append(piece)
 
-    def scatter(self, i):
-        if i < len(self.scatters):
-            piece, blocks, sems = self.scatters[i]
-            piece.scatter(blocks, *sems)
-
-    def spread(self, i, places=None):
-        if i < len(self.spreads):
-            for d in range(self.n) if places is None else places:
-                self.spreads[i].spread(d)
-
-    def forward(self, i, places):
-        if i < len(self.spreads):
-            for d in places:
-                self.spreads[i].forward(d)
+    def at(self, point):
+        for what, i, *d in self.schedule[point] if point < len(self.schedule) else ():
+            if what == "scatter":
+                piece, blocks, sems = self.scatters[i]
+                piece.scatter(blocks, *sems)
+            elif what == "spread":
+                self.spreads[i].spread(*d)
+            else:
+                self.spreads[i].forward(*d)
 
     def complete(self, i):
-        if i < len(self.spreads):
-            self.spreads[i].complete()
+        self.spreads[i].complete()
 
     def settle(self, done=()):
-        for i in range(len(self.spreads)):
+        for i, piece in enumerate(self.spreads):
             if i not in done:
-                self.complete(i)
-            self.spreads[i].sent_all()
+                piece.complete()
+            piece.sent_all()
         for piece, _, _ in self.scatters:
             for d in range(self.n):
                 piece.arrived(d)
             piece.scatter_sent()
+
+
+def parts(n, first, last):
+    return range(first * n // 4, last * n // 4)
+
+
+def moves(what, piece, places):
+    return [(what, piece, d) for d in places]
 
 
 def weights_kernel(
@@ -196,13 +270,13 @@
 ):
     place = Place(n)
     rows, hidden = down.shape[1:]
-    w_a, w_g = refs[:2]
-    later = refs[2 : 2 + 3 * layers - 2]
-    a_first, g_first, raw_g, raw_d, cut_sems, raw_sems = refs[3 * layers : 3 * layers + 6]
-    sems = refs[3 * layers + 6 :]
+    w_a, w_g, w_d = refs[:3]
+    later = refs[3 : 3 * layers]
+    a_first, g_first, d_first, raw_g, raw_d, cut_sems, raw_sems = refs[3 * layers : 3 * layers + 7]
+    sems = refs[3 * layers + 7 :]
     a_blocks = [a_first] + list(later[: layers - 1])
     g_blocks = [g_first] + list(later[layers - 1 : 2 * layers - 2])
-    d_blocks = list(later[2 * layers - 2 :])
+    d_blocks = [d_first] + list(later[2 * layers - 2 :])
     cuts = []
     for l in range(layers):
         for q in range(n):
@@ -219,8 +293,9 @@
         raws.append(pltpu.make_async_copy(down.at[l], raw_d.at[l], raw_sems.at[l, 1]))
     for copy in raws:
         copy.start()
-    attention, forward = Spread(place, nf, w_a, rows), Spread(place, nf, w_g, rows)
+    attention, forward, back = (Spread(place, nf, w, rows) for w in (w_a, w_g, w_d))
     attention.use(*sems[2:8])
+    forward.use(*sems[10:16])
     enter(place, nf, True)
     for copy in cuts[: 4 * n]:
         copy.wait()
@@ -240,27 +315,42 @@
             for j in range(n):
                 fill(g_blocks[l], j, i * units, lambda at, i=i: raw_g[l, :, i, at])
 
+    def cut_down(l):
+        raws[2 * l + 1].wait()
+        for j in range(n):
+            fill(d_blocks[l], j, 0, lambda at: raw_d[l, :, at])
+
     cut_gate_up(0)
     for d in range(n):
         attention.arrived(d)
         attention.spread(d)
     forward.scatter(g_first, *sems[8:10])
-    for l in range(layers):
-        if l:
-            cut_gate_up(l)
-        raws[2 * l + 1].wait()
-        for j in range(n):
-            fill(d_blocks[l], j, 0, lambda at, l=l: raw_d[l, :, at])
+    cut_down(0)
+    back.scatter(d_first, *sems[16:18])
+    for d in parts(n, 0, 1):
+        attention.forward(d)
+    for l in range(1, layers):
+        cut_gate_up(l)
+        cut_down(l)
     for copy in cuts[4 * n :]:
         copy.wait()
+    for d in parts(n, 1, 3):
+        attention.forward(d)
     for d in range(n):
+        forward.arrived(d)
+    for d in parts(n, 0, 1):
+        forward.spread(d)
+    for d in parts(n, 3, 4):
         attention.forward(d)
     attention.complete()
+    forward.complete()
     attention.scatter_sent()
     attention.sent_all()
+    forward.scatter_sent()
+    forward.sent_all()
     for d in range(n):
-        forward.arrived(d)
-    forward.scatter_sent()
+        back.arrived(d)
+    back.scatter_sent()
 
 
 class Gather:
@@ -423,33 +513,6 @@
         self.end(use)
 
 
-def rs_kernel(n, p_ref, out_ref, *scratch):
-    place = Place(n)
-    reduce = Reduce(place, p_ref, *scratch)
-    enter(place)
-
-    def use(at, total):
-        out_ref[at] = total
-
-    reduce.run(use)
-    reduce.finish()
-
-
-def group_reduce(p, n, collective):
-    vmem = pl.BlockSpec(memory_space=pltpu.VMEM)
-    rows, width = p.shape[2:]
-    return pl.pallas_call(
-        functools.partial(rs_kernel, n),
-        out_shape=jax.ShapeDtypeStruct((rows, width), F32),
-        in_specs=[vmem],
-        out_specs=vmem,
-        scratch_shapes=Reduce.scratch(n, rows, width),
-        compiler_params=pltpu.CompilerParams(
-            collective_id=collective, has_side_effects=True, vmem_limit_bytes=60 << 20
-        ),
-    )(p)
-
-
 def mm(a, b):
     return jnp.dot(a, b, preferred_element_type=F32)
 
@@ -541,7 +604,7 @@
     work = plan.work(place, nf, jobs)
     enter(place, nf, bool(plan.scatters))
     gather.begin()
-    work.spread(0)
+    work.at(0)
     load.wait()
 
     def project(q):
@@ -561,8 +624,7 @@
 
     for q in gather.chunks():
         project(q)
-    work.forward(0, range(1))
-    work.scatter(0)
+    work.at(1)
     keep = pltpu.make_async_copy(x, x_hbm, copy_sems.at[1])
     keep.start()
     score_scale = HD ** (-0.5)
@@ -581,14 +643,13 @@
             log_total[rows, c : c + 1] = top + jnp.log(total)
             both.append(raw * (1.0 / total))
         mix = mm((both[0] - weight * both[1]).astype(BF), values[:count])
-        mixed[rows] = mix
+        mixed[rows] = mix.astype(BF)
         head = (mix * rms_scale(mix) * keep_factor(layer)).astype(BF)
         headed[rows] = head
         side[rows] = mm_t(head, a_head[:rank]).astype(BF)
 
     row_blocks(tree, attend)
-    work.forward(0, range(1, n // 2))
-    work.scatter(1)
+    work.at(2)
 
     for k in reduce.order:
         q = reduce.chips[k]
@@ -603,14 +664,16 @@
         reduce.offer(k)
         if k == reduce.order[2]:
             reduce.far()
+    work.at(3)
     for s in range(1, n // 2):
         reduce.near(s)
+    work.at(4)
 
     def use(at, total):
         middle[at] = residual[at] + total
 
     reduce.end(use)
-    work.forward(0, range(n // 2, n))
+    work.at(5)
     keep.wait()
     gather.finish()
     reduce.finish()
@@ -635,13 +698,13 @@
     work = plan.work(place, nf, jobs)
     enter(place, nf, bool(plan.scatters))
     gather.begin()
-    work.spread(0)
+    work.at(0)
     load.wait()
     step = tile_of(units)
 
     for number, q in enumerate(gather.chunks()):
         if number == n - 1:
-            work.forward(0, range(1))
+            work.at(1)
         rows = pl.ds(pl.multiple_of(q * chip_rows, chip_rows), chip_rows)
         v = x[q].reshape(chip_rows, width)
         low = mm_t(v, a_model[4 * rank : 6 * rank]).astype(BF)
@@ -657,13 +720,10 @@
 
         tiles(units, step, unit_tile)
 
-    work.forward(0, range(1, n // 2))
-    work.spread(1)
-    work.scatter(0)
+    work.at(2)
     keep = pltpu.make_async_copy(x, x_hbm, copy_sems.at[1])
     keep.start()
 
-    work.forward(0, range(n // 2, n))
     work.complete(0)
     load = pltpu.make_async_copy(plan.late(jobs), w.at[:, pl.ds(2 * units, units)], copy_sems.at[0])
     load.start()
@@ -684,14 +744,16 @@
         reduce.offer(k)
         if k == reduce.order[2]:
             reduce.far()
+    work.at(3)
     for s in range(1, n // 2):
         reduce.near(s)
+    work.at(4)
 
     def use(at, total):
         following[at] = residual[at] + total
 
     reduce.end(use)
-    work.forward(1, range(n))
+    work.at(5)
     keep.wait()
     gather.finish()
     reduce.finish()
@@ -699,11 +761,14 @@
 
 
 def ffn_backward(
-    n, units, rank,
-    grad, middle, gain, w_hbm, w_down_hbm, a_model, e_model, x_hbm, gates, ups, hidden, small, side,
-    grad_out, grad_up_down, grad_in, grad_units, grad_e2,
-    x, p, w, kept, dgu, dsmall, dside, raised, copy_sems, *sems,
+    n, units, rank, carry,
+    grad, middle, gain, w_hbm, w_down_hbm, a_model, e_model, x_hbm, gates, ups, hidden, small, side, *refs,
 ):
+    if carry:
+        final, final_out, *refs = refs
+        *refs, final_rows, home_send, home_recv = refs
+    (grad_out, grad_up_down, grad_in, grad_units,
+     x, p, w, kept, dgu, dsmall, dside, raised, copy_sems, *sems) = refs
     place = Place(n)
     chip_rows, width = 2 * x_hbm.shape[2], x_hbm.shape[3]
     tree = n * chip_rows
@@ -720,8 +785,17 @@
 
     by_rows(grad.shape[0], own)
     block_diagonal(raised, (e_model, 2), rank, units)
-    enter(place)
+    if carry:
+
+        def last_rows(at):
+            final_rows[at] = final[at].astype(BF)
+
+        by_rows(final.shape[0], last_rows)
+    enter(place, home=carry)
     gather.begin()
+    if carry:
+        home = Home(place, final_out, home_send, home_recv)
+        home.start(final_rows)
     load.wait()
     load_down.wait()
     step = tile_of(units)
@@ -769,38 +843,47 @@
 
         def unit_tile(at):
             up_at = pl.ds(pl.multiple_of(units + at.start, step), step)
-            grad_units[:rank, at] = ADAPTER_SCALE * t_mm(small[...], dgu[:, at])[:rank]
-            grad_units[rank:, at] = ADAPTER_SCALE * t_mm(small[...], dgu[:, up_at])[rank:]
-            grad_e2[:, at] = t_mm(dside[...], hidden[:, at])
+            grad_units[:rank, at] = (ADAPTER_SCALE * t_mm(small[...], dgu[:, at])[:rank]).astype(BF)
+            grad_units[rank : 2 * rank, at] = (ADAPTER_SCALE * t_mm(small[...], dgu[:, up_at])[rank:]).astype(BF)
+            grad_units[2 * rank : 3 * rank, at] = t_mm(dside[...], hidden[:, at]).astype(BF)
+            grad_units[3 * rank :, at] = jnp.zeros((rank, at.size), BF)
 
         tiles(units, step, unit_tile)
 
     reduce.run(use, adapters)
     gather.finish()
     reduce.finish()
+    if carry:
+        home.land()
+        home.finish()
 
 
 def attention_backward(
-    n, layer, part, rank,
+    n, layer, share, heads_tp, rank,
     grad, residual, gain, w_hbm, a_model, a_head, cosine, sine, query_bits, key_bits, lam,
     x_hbm, queries, keys, values, small, log_total, mixed, headed, side,
-    grad_out, grad_a9, grad_in, grad_head,
-    x, p, w, dmixed, dq, dk, dv, dprojected, dsmall, dside, raised, copy_sems, *sems,
+    grad_up_down, grad_ffn_in, grad_units,
+    grad_out, own_sum, all_units,
+    x, p, w, dmixed, dq, dk, dv, dprojected, dsmall, dside, raised, grad_a9, p_own, copy_sems, *sems,
 ):
     place = Place(n)
+    part = 1.0 / share
     chip_rows, width = 2 * x_hbm.shape[2], x_hbm.shape[3]
     tree = n * chip_rows
     load = pltpu.make_async_copy(w_hbm, w, copy_sems.at[0])
     load.start()
-    gather, reduce = Gather(place, x, *sems[:6]), Reduce(place, p, *sems[6:])
+    gather, reduce = Gather(place, x, *sems[:6]), Reduce(place, p, *sems[6:15])
+    gather_units, reduce_own = Gather(place, all_units, *sems[15:21]), Reduce(place, p_own, *sems[21:])
 
     def own(at):
         x[place.q, place.t, at] = grad[at].astype(BF)
 
     by_rows(grad.shape[0], own)
     block_diagonal(raised, (a_head[rank : 4 * rank], 3), rank, VD)
+    all_units[place.q, place.t] = grad_units[...]
     enter(place)
     gather.begin()
+    gather_units.begin()
     dk[...] = jnp.zeros(dk.shape, F32)
     dv[...] = jnp.zeros(dv.shape, F32)
     load.wait()
@@ -811,7 +894,7 @@
         low = (ADAPTER_SCALE * mm_t(v, a_model[9 * rank : 10 * rank])).astype(BF)
         dside[rows] = low
         dheaded = mm(v, w[:, 3 * VD :]) + mm(low, a_head[:rank])
-        inputs = mixed[rows]
+        inputs = mixed[rows].astype(F32)
         dmixed[rows] = norm_back(dheaded, inputs, rms_scale(inputs), keep_factor(layer)).astype(BF)
 
     def out_gradient(at):
@@ -844,18 +927,27 @@
 
     row_blocks(tree, attend)
 
-    for k in reduce.order:
-        q = reduce.chips[k]
-        rows = pl.ds(pl.multiple_of(q * chip_rows, chip_rows), chip_rows)
-        for i, source in enumerate((dq, dk)):
+    fetch.wait()
+    for _ in gather_units.chunks():
+        pass
+
+    def project(i, carry):
+        rows = pl.ds(pl.multiple_of(i * chip_rows, chip_rows), chip_rows)
+        for j, source in enumerate((dq, dk)):
             for c in range(2):
                 half = slice(c * HD, (c + 1) * HD)
                 turned = turn(source[rows, half] * score_scale, cosine[rows], -sine[rows])
-                dprojected[rows, i * VD + c * HD : i * VD + (c + 1) * HD] = turned.astype(BF)
+                dprojected[rows, j * VD + c * HD : j * VD + (c + 1) * HD] = turned.astype(BF)
         dprojected[rows, 2 * VD :] = dv[rows].astype(BF)
-        back = dprojected[rows]
-        low_back = (ADAPTER_SCALE * mm_t(back, raised[...])).astype(BF)
-        dsmall[rows] = low_back
+        dsmall[rows] = (ADAPTER_SCALE * mm_t(dprojected[rows], raised[...])).astype(BF)
+        return carry
+
+    lax.fori_loop(0, n, project, 0)
+
+    def send_part(k):
+        q = reduce.chips[k]
+        rows = pl.ds(pl.multiple_of(q * chip_rows, chip_rows), chip_rows)
+        back, low_back = dprojected[rows], dsmall[rows]
 
         def out_tile(at):
             made = mm_t(back, w[at, : 3 * VD]) + mm(low_back, a_model[: 3 * rank, at])
@@ -863,34 +955,124 @@
 
         tiles(width, 512, out_tile)
         reduce.offer(k)
-        if k == reduce.order[2]:
-            reduce.far()
+
+    for k in reduce.order[:3]:
+        send_part(k)
+    reduce.far()
+
+    block = width // (2 * n)
+
+    def full_tile(jp, carry):
+        at = pl.ds(pl.multiple_of(jp * block, block), block)
+        j = jp // 4 * 4 + jp % 2 * 2 + jp // 2 % 2
+        q, t = j // 2, j % 2
+        flat = x[:, :, :, at].reshape(tree, block)
+        p_own[q, t, : 3 * rank] = (part * t_mm(dsmall[...], flat)).astype(BF)
+        p_own[q, t, 4 * rank : 6 * rank] = grad_ffn_in[:, at]
+        p_own[q, t, 9 * rank : 10 * rank] = grad_a9[:, at]
+        p_own[q, t, 10 * rank : 11 * rank] = grad_up_down[:, at]
+        p_own[q, t, 11 * rank :] = jnp.zeros((rank, block), BF)
+        return carry
+
+    lax.fori_loop(0, 2 * n, full_tile, 0)
+    of_head = [part * t_mm(dside[...], headed[...])]
+    for i in range(3):
+        made = t_mm(small[...], dprojected[:, i * VD : (i + 1) * VD])[i * rank : (i + 1) * rank]
+        of_head.append(ADAPTER_SCALE * part * made)
+    head = place.t * heads_tp + place.q // share
+    for j in range(2 * n):
+        start = j * block % VD
+        own = (head == j * block // VD).astype(F32)
+        for i, k in enumerate((3, 6, 7, 8)):
+            made = of_head[i][:, start : start + block] * own
+            p_own[j // 2, j % 2, k * rank : (k + 1) * rank] = made.astype(BF)
+
+    for k in reduce.order[3:]:
+        send_part(k)
+    for k in reduce.order:
+        reduce_own.offer(k)
+    reduce_own.far()
     for s in range(1, n // 2):
         reduce.near(s)
-
-    fetch.wait()
-
-    def model_tile(at):
-        flat = x[:, :, :, at].reshape(tree, at.size)
-        grad_in[:, at] = (part * t_mm(dsmall[...], flat)).astype(BF)
-
-    tiles(width, 256, model_tile)
-    grad_head[:rank] = part * t_mm(dside[...], headed[...])
-    for i in range(3):
-        made = t_mm(small[...], dprojected[:, i * VD : (i + 1) * VD])[i * rank : (i + 1) * rank]
-        grad_head[(i + 1) * rank : (i + 2) * rank] = ADAPTER_SCALE * part * made
+        reduce_own.near(s)
+
+    def use_own(at, total):
+        own_sum[at] = total.astype(BF)
 
     def use(at, total):
         inputs = residual[at]
         grad_out[at] = grad[at] + norm_back(total, inputs, rms_scale(inputs), gain[...])
 
     reduce.end(use)
+    reduce_own.end(use_own)
+    gather_units.finish()
     reduce.finish()
+    reduce_own.finish()
+
+
+def finish_kernel(
+    n, nf, layers, rank,
+    grad, own_sums, own_units, slot,
+    tokens_grad, model_grad, hidden_grad,
+    rows_out, landed, sent_sums, all_sums, all_units, home_send, home_recv, tree_send, tree_recv,
+):
+    place = Place(n)
+    own = model_grad.shape[2]
+    tall = own_sums.shape[0]
+
+    def cut(at):
+        rows_out[at] = grad[at].astype(BF)
+
+    by_rows(grad.shape[0], cut)
+    sent_sums[...] = own_sums[...]
+    sent_sums[tall - rank :] = jnp.broadcast_to(slot[...], (rank, own_sums.shape[1])).astype(BF)
+    enter(place, home=True, ring=False, trees=nf)
+    moves = [Home(place, landed, home_send.at[0], home_recv.at[0])]
+    moves[0].start(rows_out)
+    away = {}
+    for i, (source, target) in enumerate(((sent_sums, all_sums), (own_units, all_units))):
+        away[i] = TreeMove(place, source, target, home_send.at[i + 1], home_recv.at[i + 1])
+        away[i].start()
+    copies = []
+    for i in range(2):
+        away[i].land()
+        slot_of = away[i].slot
+        for e in range(1, nf):
+            copies.append(
+                remote(slot_of, slot_of, tree_send.at[i, e], tree_recv.at[i, e], {"fsdp": flip(place.f, e)})
+            )
+    moves[0].land()
+    for copy in copies:
+        copy.wait_recv()
+    block, units = all_sums.shape[2], all_units.shape[2]
+    per_layer = tall // layers
+    for b in range(own):
+        number = (place.f * own + b).astype(F32)
+        keeps = [
+            (all_sums[f, tall - rank : tall - rank + 1, :1].astype(F32) == number).astype(F32) for f in range(nf)
+        ]
+        for l in range(layers):
+            for k in range(11):
+                at = slice(l * per_layer + k * rank, l * per_layer + (k + 1) * rank)
+                model_grad[l, k, b] = sum(keeps[f] * all_sums[f, at].astype(F32) for f in range(nf))
+            for k in range(3):
+                at = slice((l * 3 + k) * rank, (l * 3 + k + 1) * rank)
+                hidden_grad[l, k, b] = sum(keeps[f] * all_units[f, at].astype(F32) for f in range(nf))
+    moves[0].finish()
+    for core in range(2):
+
+        def widen(at, core=core):
+            rows = landed.shape[1]
+            tokens_grad[pl.ds(pl.multiple_of(core * rows + at.start, 16), at.size)] = landed[core, at].astype(F32)
+
+        by_rows(landed.shape[1], widen)
+    for copy in copies:
+        copy.wait_send()
 
 
 class Plan:
-    def __init__(self, n, nf, rows, scatters, spreads):
-        self.n, self.nf, self.rows = n, nf, rows
+    def __init__(self, n, nf, rows, scatters, spreads, schedule):
+        self.n, self.nf, self.rows, self.schedule = n, nf, rows, schedule
         self.scatters, self.spreads = scatters, spreads
 
     def ins(self):
@@ -916,7 +1098,7 @@
         ins, outs, sems = jobs
         scatters = [(ins[i], outs[i], sems[2 * i : 2 * i + 2]) for i in range(a)]
         spreads = [(outs[a + i], sems[2 * a + 6 * i : 2 * a + 6 * i + 6]) for i in range(b)]
-        return Work(place, nf, self.rows, scatters, spreads)
+        return Work(place, nf, self.rows, scatters, spreads, self.schedule)
 
     def late(self, jobs):
         return jobs[1][len(self.scatters)]
@@ -937,7 +1119,7 @@
         scratch_shapes=scratch,
         input_output_aliases=aliases,
         compiler_params=pltpu.CompilerParams(
-            collective_id=collective, has_side_effects=True, vmem_limit_bytes=60 << 20
+            collective_id=collective, has_side_effects=True, vmem_limit_bytes=62 << 20
         ),
     )(*[array for array, _ in ins])
     return list(made)
@@ -1074,30 +1256,27 @@
         functools.partial(weights_kernel, n, nf, units, share, layers),
         calls[0],
         far(jnp.transpose(query_key_value_weight, (0, 2, 1, 3)), output_weight, gate_up_weight, down_weight),
-        [out((tall, c_a), BF, True), out((tall, c_g), BF, True)]
-        + [cut(c_a)] * (layers - 1)
-        + [cut(c_g)] * (layers - 1)
-        + [cut(c_d)] * layers,
+        [out((tall, c_a), BF, True), out((tall, c_g), BF, True), out((tall, c_d), BF, True)]
+        + ([cut(c_a)] + [cut(c_g)] + [cut(c_d)]) * (layers - 1),
         [
             vmem((n, weight_rows, c_a), BF),
             vmem((n, weight_rows, c_g), BF),
+            vmem((n, weight_rows, c_d), BF),
             vmem((layers, weight_rows, 2, hidden_tp), BF),
             vmem((layers, weight_rows, hidden_tp), BF),
             dma((layers, n, 4)),
             dma((layers, 2)),
         ]
-        + Spread.scatter_semaphores(n)
-        + Spread.spread_semaphores(n, nf)
+        + (Spread.scatter_semaphores(n) + Spread.spread_semaphores(n, nf)) * 2
         + Spread.scatter_semaphores(n),
     )
-    w_a, w_g = [made[0]], [made[1]]
-    w_d = []
-    a_blocks = [None] + made[2 : 1 + layers]
-    g_blocks = [None] + made[1 + layers : 2 * layers]
-    d_blocks = made[2 * layers :]
-
-    def plan_of(scatters, spreads):
-        return Plan(n, nf, weight_rows, scatters, spreads)
+    w_a, w_g, w_d = [made[0]], [made[1]], [made[2]]
+    a_blocks = [None] + made[3 : 2 + layers]
+    g_blocks = [None] + made[2 + layers : 1 + 2 * layers]
+    d_blocks = [None] + made[1 + 2 * layers :]
+
+    def plan_of(scatters, spreads, *schedule):
+        return Plan(n, nf, weight_rows, scatters, spreads, schedule)
 
     saved = []
     for l in range(layers):
@@ -1107,7 +1286,12 @@
         gain_a, gain_f = gains[l, 0:1], gains[l, 1:2]
         shared = (a_model[l], a_head[l], cosine, sine, query_bits, key_bits, lam)
         plan = plan_of(
-            [(d_blocks[l], (tall, c_d))] + ([] if last else [(a_blocks[l + 1], (tall, c_a))]), [w_g[l]]
+            [] if last else [(a_blocks[l + 1], (tall, c_a)), (g_blocks[l + 1], (tall, c_g))],
+            [w_g[l], w_d[l]],
+            moves("forward", 0, parts(n, 0, 1)) + moves("spread", 0, parts(n, 1, 4)),
+            moves("forward", 0, parts(n, 1, 2)) + ([] if last else [("scatter", 0)]),
+            moves("spread", 1, parts(n, 0, 2)) + moves("forward", 0, parts(n, 2, 3)),
+            moves("forward", 0, parts(n, 3, 4)) + ([] if last else [("scatter", 1)]),
         )
         got = run(
             functools.partial(attention_forward, n, nf, l, part, rank, plan),
@@ -1120,19 +1304,28 @@
                 out((tree, VD), BF),
                 out((tree, 3 * rank), BF),
                 out((tree, 2), F32),
-                out((tree, VD), F32),
+                out((tree, VD), BF),
                 out((tree, VD), BF),
                 out((tree, rank), BF),
             ],
             big + [vmem((width, 4 * VD), BF), vmem((3 * rank, 3 * VD), BF), pair] + sems,
             plan,
         )
-        w_d.append(got[0])
         if not last:
-            w_a.append(got[1])
-        w_g[l] = got[2 - last]
-        middle, kept = got[3 - last], got[4 - last :]
-        plan = plan_of([] if last else [(g_blocks[l + 1], (tall, c_g))], [w_d[l]] + ([] if last else [w_a[l + 1]]))
+            w_a.append(got[0])
+            w_g.append(got[1])
+            got = got[2:]
+        w_g[l], w_d[l], middle, *kept = got
+        plan = plan_of(
+            [] if last else [(d_blocks[l + 1], (tall, c_d))],
+            [w_d[l]] + ([] if last else [w_a[l + 1], w_g[l + 1]]),
+            moves("forward", 0, parts(n, 0, 2)) + moves("spread", 0, parts(n, 2, 4)),
+            moves("forward", 0, parts(n, 2, 3)),
+            moves("forward", 0, parts(n, 3, 4)) + ([] if last else moves("spread", 1, parts(n, 0, 4)) + [("scatter", 0)]),
+            [] if last else moves("forward", 1, parts(n, 0, 1)),
+            [] if last else moves("forward", 1, parts(n, 1, 2)) + moves("spread", 2, parts(n, 0, 1)),
+            [] if last else moves("forward", 1, parts(n, 2, 4)),
+        )
         ffn = run(
             functools.partial(ffn_forward, n, nf, units, rank, plan),
             near(middle, gain_f) + far(w_g[l]) + near(a_model[l], e_model[l]),
@@ -1149,26 +1342,28 @@
             plan,
         )
         if not last:
-            w_g.append(ffn[0])
-            w_a[l + 1] = ffn[2]
-        w_d[l] = ffn[1 - last]
-        ffn = ffn[3 - 2 * last :]
+            w_d.append(ffn[0])
+            w_d[l], w_a[l + 1], w_g[l + 1], *ffn = ffn[1:]
+        else:
+            w_d[l], *ffn = ffn
         saved.append((residual, middle, gain_a, gain_f, shared, kept, ffn[1:]))
         residual = ffn[0]
 
     grad = own_cotangent.astype(F32)
-    model_grads, hidden_grads = [], []
+    units_here, sums_here, block = [], [], width // (2 * n)
     for l in reversed(range(layers)):
         residual_in, middle, gain_a, gain_f, shared, kept, ffn = saved[l]
-        grad, grad_a10, grad_a45, grad_e01, grad_e2 = run(
-            functools.partial(ffn_backward, n, units, rank),
-            near(grad, middle, gain_f) + far(w_g[l], w_d[l]) + near(a_model[l], e_model[l]) + far(ffn[0]) + near(*ffn[1:]),
-            [
+        carry = l == layers - 1
+        made = run(
+            functools.partial(ffn_backward, n, units, rank, carry),
+            near(grad, middle, gain_f) + far(w_g[l], w_d[l]) + near(a_model[l], e_model[l]) + far(ffn[0]) + near(*ffn[1:])
+            + (near(residual) if carry else []),
+            ([out((2, rows, width), BF)] if carry else [])
+            + [
                 out((rows, width), F32),
                 out((rank, width), BF),
                 out((2 * rank, width), BF),
-                out((2 * rank, units), F32),
-                out((rank, units), F32),
+                out((4 * rank, units), BF),
             ],
             big
             + [
@@ -1180,16 +1375,19 @@
                 vmem((2 * rank, 2 * units), BF),
                 pair,
             ]
-            + sems,
+            + sems
+            + ([vmem((rows, width), BF)] + Home.semaphores() if carry else []),
         )
-        grad, grad_a9, grad_a012, grad_head = run(
-            functools.partial(attention_backward, n, l, part, rank),
-            near(grad, residual_in, gain_a) + far(w_a[l]) + near(*shared) + far(kept[0]) + near(*kept[1:]),
+        if carry:
+            outputs, *made = made
+        grad, *ffn_grads = made
+        grad, own_sum, all_units = run(
+            functools.partial(attention_backward, n, l, share, heads_tp, rank),
+            near(grad, residual_in, gain_a) + far(w_a[l]) + near(*shared) + far(kept[0]) + near(*kept[1:], *ffn_grads),
             [
                 out((rows, width), F32),
-                out((rank, width), BF),
-                out((3 * rank, width), BF),
-                out((4 * rank, VD), F32),
+                out((12 * rank, block), BF),
+                out((n, 2, 4 * rank, units), BF),
             ],
             big
             + [
@@ -1202,65 +1400,50 @@
                 vmem((tree, 3 * rank), BF),
                 vmem((tree, rank), BF),
                 vmem((3 * rank, 3 * VD), BF),
+                vmem((rank, width), BF),
+                vmem((n, 2, 12 * rank, block), BF),
                 pair,
             ]
-            + sems,
+            + sems
+            + Gather.semaphores(n)
+            + Reduce.scratch(n, 12 * rank, block),
         )
 
-        def placed(x):
-            empty = jnp.zeros(x.shape[:-1] + (width,), F32)
-            return lax.dynamic_update_slice_in_dim(empty, x, head_at, x.ndim - 1).astype(BF)
-
-        def placed_units(x):
-            empty = jnp.zeros(x.shape[:-1] + (2, n * units), F32)
-            empty = lax.dynamic_update_slice(
-                empty, x[..., None, :], (0,) * (x.ndim - 1) + (t, q * units)
-            )
-            return empty[..., :hidden_tp].reshape(x.shape[:-1] + (2 * hidden_tp,)).astype(BF)
-
-        headed = placed(grad_head)
-        model_grads.insert(
-            0,
-            jnp.concatenate(
-                [
-                    swap_columns(grad_a012),
-                    headed[:rank],
-                    swap_columns(grad_a45),
-                    headed[rank:],
-                    swap_columns(grad_a9),
-                    swap_columns(grad_a10),
-                ]
-            ),
-        )
-        hidden_grads.insert(0, placed_units(jnp.concatenate([grad_e01, grad_e2])))
-
-    model_all = jnp.stack(model_grads).reshape(layers * 11 * rank, n, 2, width // (2 * n))
-    hidden_all = jnp.stack(hidden_grads).reshape(layers * 3 * rank, n, 2, 2 * hidden_tp // (2 * n))
-    lanes = 1024
-    flat = jnp.concatenate(
-        [x.transpose(1, 2, 0, 3).reshape(n, 2, -1) for x in (model_all, hidden_all)], axis=2
+        number = (q * 2 + t) * (hidden_tp // n)
+        half = lax.dynamic_index_in_dim(all_units, number // hidden_tp, 1, keepdims=False)
+        flat = half[:, : 3 * rank].transpose(1, 0, 2).reshape(3 * rank, n * units)
+        units_here.insert(0, lax.dynamic_slice_in_dim(flat, number % hidden_tp, hidden_tp // n, 1))
+        sums_here.insert(0, own_sum)
+
+    own = adapters // nf
+    dma = pltpu.SemaphoreType.DMA
+    wide = hidden_tp // n
+    tokens_grad, grad_model, grad_hidden = run(
+        functools.partial(finish_kernel, n, nf, layers, rank),
+        near(grad, jnp.concatenate(sums_here), jnp.concatenate(units_here), slot.astype(F32).reshape(1, 1)),
+        [
+            out((2 * rows, width), F32),
+            out((layers, 11, own, rank, block), F32),
+            out((layers, 3, own, rank, wide), F32),
+        ],
+        [
+            vmem((rows, width), BF),
+            vmem((2, rows, width), BF),
+            vmem((layers * 12 * rank, block), BF),
+            vmem((nf, layers * 12 * rank, block), BF),
+            vmem((nf, layers * 3 * rank, wide), BF),
+            dma((3, 2)),
+            dma((3, 2)),
+            dma((2, nf)),
+            dma((2, nf)),
+        ],
     )
-    size = flat.shape[2]
-    tall = -(-size // (lanes * 32)) * 32
-    flat = jnp.pad(flat, ((0, 0), (0, 0), (0, tall * lanes - size))).reshape(n, 2, tall, lanes).astype(BF)
-    calls[0] += 1
-    summed = swap_trees(group_reduce(flat, n, calls[0]).astype(BF), nf, nc)
-    every = lax.all_gather(summed, "fsdp", axis=0).reshape(nf, -1)[:, :size].astype(F32)
-    slots = lax.all_gather(tree_adapter_index, "fsdp", axis=0, tiled=True)
-    own_adapters = adapters // nf
-    chosen = place.f * own_adapters + jnp.arange(own_adapters)
-    pick = (slots[None, :] == chosen[:, None]).astype(F32)
-    totals = jnp.sum(pick[:, :, None] * every[None], axis=1)
-    cut = layers * 11 * rank * (width // (2 * n))
-    grad_model = totals[:, :cut].reshape(own_adapters, layers, 11, rank, -1).transpose(1, 2, 0, 3, 4)
-    grad_hidden = totals[:, cut:].reshape(own_adapters, layers, 3, rank, -1).transpose(1, 2, 0, 3, 4)
-
-    def home(x):
-        mine = swap_trees(swap_columns(x), nf, nc)
-        other = lax.ppermute(mine, "tp", ((0, 1), (1, 0)))
-        return jnp.where(t == 0, jnp.concatenate([mine, other]), jnp.concatenate([other, mine]))
-
-    return home(residual.astype(BF)), home(grad), grad_model, grad_hidden
+    return (
+        swap_columns(outputs.reshape(2 * rows, width)),
+        swap_columns(tokens_grad),
+        grad_model,
+        grad_hidden,
+    )
 
 
 def solution(mesh):

time: 1080 us -> 955 us (0.88)
  waiting for transfers between devices: 42.4 us -> 0.01 us
  Pallas kernels: 890 us -> 859 us
  other arithmetic: 24.9 us -> 8.06 us
  between operations: 17.9 us -> 4.89 us
  local copies, waits for them, and re-layouts: 62.4 us -> 50.4 us
    pallas_call x1 -> x0, Pallas kernels: 46.4 us -> none  [group_reduce(): pl.pallas_call(functools.partial(rs_kernel, n), out_shape=jax.ShapeDtypeS...]
    ppermute x6 -> x3, waiting for transfers between devices: 42.4 us -> 0.01 us  [permute(): return lax.ppermute(x, ('fsdp', 'ctx'), pairs)]
    pallas_call x9 -> x10, Pallas kernels: 843 us -> 859 us  [call(): pl.pallas_call(kernel, out_shape=[jax.ShapeDtypeStruct(shape, kind) for s...]
    reshape x7 -> x2, local copies, waits for them, and re-layouts: 13.7 us -> 0.04 us  [shards(): flat = half[:, :3 * rank].transpose(1, 0, 2).reshape(3 * rank, n * units)]
  transfers between devices with their start and end apart: 9 -> 3, of which waited for: 2 -> 0; matrix products, arithmetic and copies ran while one was open for 4% -> 4% of each run, Pallas kernels for 11% -> 9%
where the time goes in v3:
time: 955 us; the launch traced here: 941 us
  Pallas kernels  859 us (90%)
  local copies, waits for them, and re-layouts  50.4 us (5%)
    pallas_call x10, Pallas kernels, call(): pl.pallas_call(kernel, out_shape=[jax.ShapeDtypeStruct(shape, kind) for s...  859 us
  transfers between devices with their start and end apart: 3, of which 0 were waited for; matrix products, arithmetic and copies ran while one was open for 4% of the time, Pallas kernels for 9%

profile of v3, /device:TPU:3, one launch (start us, length us, event | category | flops | bytes accessed | tf_op | source)
XLA Modules:
  0.0 940.8 jit_solution(15568101181134504135)
XLA Ops:
  0.6 0.8 pad_add_fusion
  1.4 9.5 %all_gather.3 = s32[2,1024]{1,0:T(2,128)S(1)} all-gather(s32[2,256]{1,0:T(2,128)S(1)} %pad_add_fusion), channel_id=1, replica_groups=mesh['fsdp'=4,'ctx'=4,'tp'=2] {'ctx'}, dimensions={1}, use_global_device_ids=true | all-gather | bytes 10240 | tf_op jit(solution)/shard_map/all_gather | solution.py:1199
  11.6 0.7 concatenate.18
  12.3 2.2 collective-permute-start.2
  14.6 0.8 constant_dynamic-slice_fusion.7
  15.4 4.8 collective-permute-start.1
  20.3 1.9 constant_dynamic-slice_fusion.8
  22.2 2.2 collective-permute-start
  24.4 0.8 fusion.6
  25.1 0.8 reshape.80
  27.1 85.4 %shard_map.165 = (bf16[2048,1024]{1,0:T(8,128)(2,1)}, bf16[2048,1536]{1,0:T(8,128)(2,1)}, bf16[2048,768]{1,0:T(8,128)(2,1)}, bf16[4,128,1024]{2,1,0:T(8,128)(2,1...) custom-call(bf16[2,3,128,1024]{3,2,1,0:T(8,128)(2,1)} %bitcast.59, bf16[2,128,1024]{2,1,0:T(8,128)(2,1)} %output.1, ...), custom_call_target="tpu_custom_call" | custom-call | tf_op jit(solution)/shard_map/pallas_call | solution.py:1114
  116.0 1.1 dynamic-slice_bitcast_fusion.2
  117.1 2.7 constant_dynamic-slice_fusion.6
  119.8 4.0 reshape.82
  123.8 2.0 fusion.4
  126.0 1.4 constant_dynamic-slice_fusion.4
  129.5 0.7 copy.46
  130.2 1.4 squeeze.66.a_model
  131.6 1.0 copy.47.query_bits
  132.7 0.7 copy.48
  133.4 1.4 squeeze.71.a_model
  134.8 0.7 fusion.2
  135.5 2.6 fusion
  138.1 1.3 pad_maximum_fusion
  139.4 2.1 reshape.93
  142.1 1.8 reshape.91.residual
  143.9 1.0 reshape.92
  145.5 1.8 reshape.90.grad
  147.3 137.9 %shard_map.166 = (bf16[2048,1024]{1,0:T(8,128)(2,1)}, bf16[2048,1536]{1,0:T(8,128)(2,1)}, bf16[2048,1536]{1,0:T(8,128)(2,1)}, bf16[2048,768]{1,0:T(8,128)(2,1)},...) custom-call(f32[128,2048]{1,0:T(8,128)} %reshape.91.residual, ...), custom_call_target="tpu_custom_call", output_to_operand_aliasing={{2}: (12, {}), {3}: (13, {})} | custom-call | tf_op jit(solution)/shard_map/pallas_call | solution.py:1114
  285.2 113.4 %shard_map.167 = (bf16[2048,768]{1,0:T(8,128)(2,1)}, bf16[2048,768]{1,0:T(8,128)(2,1)}, bf16[2048,1024]{1,0:T(8,128)(2,1)}, bf16[2048,1536]{1,0:T(8,128)(2,1)}, ...) custom-call(f32[128,2048]{1,0:T(8,128)} %get-tuple-element.78.residu, ...), custom_call_target="tpu_custom_call", output_to_operand_aliasing={{1}: (6, {}), {2}: (7, {}), {3}: (8, {})} | custom-call | tf_op jit(solution)/shard_map/pallas_call | solution.py:1114
  398.5 103.9 %shard_map.168 = (bf16[2048,1536]{1,0:T(8,128)(2,1)}, bf16[2048,768]{1,0:T(8,128)(2,1)}, f32[128,2048]{1,0:T(8,128)}, bf16[4,2,128,2048]{3,2,1,0:T(8,128)(2,1)},...) custom-call(f32[128,2048]{1,0:T(8,128)} %get-tuple-element.84.residu, ...), custom_call_target="tpu_custom_call", output_to_operand_aliasing={{0}: (10, {}), {1}: (11, {})} | custom-call | tf_op jit(solution)/shard_map/pallas_call | solution.py:1114
  502.4 76.0 %shard_map.169 = (bf16[2048,768]{1,0:T(8,128)(2,1)}, f32[128,2048]{1,0:T(8,128)}, bf16[4,2,128,2048]{3,2,1,0:T(8,128)(2,1)}, bf16[1024,768]{1,0:T(8,128)(2,1)}, ...) custom-call(f32[128,2048]{1,0:T(8,128)} %get-tuple-element.88.residu, ...), custom_call_target="tpu_custom_call", output_to_operand_aliasing={{0}: (5, {})} | custom-call | tf_op jit(solution)/shard_map/pallas_call | solution.py:1114
  578.4 72.6 %shard_map.170 = (bf16[2,128,2048]{2,1,0:T(8,128)(2,1)}, f32[128,2048]{1,0:T(8,128)}, bf16[16,2048]{1,0:T(8,128)(2,1)}, bf16[32,2048]{1,0:T(8,128)(2,1)}, bf16[64,768]{1,0:T(8,128)(2,1)}) custom-call(f32[128,2048]{1,0:T(8,128)} %reshape.90.grad, f32[128,2048]{1,0:T(8,128)} %get-tuple-element.88.residual.middle, f32[1,2048]{1,0:T(1,128)} %get-tuple-element.148.gain, ...), custom_call_target="tpu_custom_call" | custom-call | tf_op jit(solution)/shard_map/pallas_call | solution.py:1114
  651.0 77.1 %shard_map.171 = (f32[128,2048]{1,0:T(8,128)}, bf16[192,256]{1,0:T(8,128)(2,1)}, bf16[4,2,64,768]{3,2,1,0:T(8,128)(2,1)}) custom-call(f32[128,2048]{1,0:T(8,128)} %get-tuple-element.100.grad, f32[128,2048]{1,0:T(8,128)} %get-tuple-element.84.residual, f32[1,2048]{1,0:T(1,128)} %get-tuple-element.149.gain, bf16[2048,1024]{1,0:T(8,128)(2,1)} %get-tuple-element.85.w_hbm, ...), custom_call_target="tpu_custom_call" | custom-call | tf_op jit(solution)/shard_map/pallas_call | solution.py:1114
  728.2 59.6 %shard_map.172 = (f32[128,2048]{1,0:T(8,128)}, bf16[16,2048]{1,0:T(8,128)(2,1)}, bf16[32,2048]{1,0:T(8,128)(2,1)}, bf16[64,768]{1,0:T(8,128)(2,1)}) custom-call(f32[128,2048]{1,0:T(8,128)} %get-tuple-element.113.grad, f32[128,2048]{1,0:T(8,128)} %get-tuple-element.78.residual.middle, f32[1,2048]{1,0:T(1,128)} %get-tuple-element.150.gain, ...), custom_call_target="tpu_custom_call" | custom-call | tf_op jit(solution)/shard_map/pallas_call | solution.py:1114
  787.8 77.5 %shard_map.173 = (f32[128,2048]{1,0:T(8,128)}, bf16[192,256]{1,0:T(8,128)(2,1)}, bf16[4,2,64,768]{3,2,1,0:T(8,128)(2,1)}) custom-call(f32[128,2048]{1,0:T(8,128)} %get-tuple-element.121.grad, f32[128,2048]{1,0:T(8,128)} %reshape.91.residual, f32[1,2048]{1,0:T(1,128)} %get-tuple-element.151.gain, bf16[2048,1024]{1,0:T(8,128)(2,1)} %get-tuple-element.73.w_hbm, ...), custom_call_target="tpu_custom_call" | custom-call | tf_op jit(solution)/shard_map/pallas_call | solution.py:1114
  865.3 1.1 dynamic-slice_bitcast_fusion.1
  866.8 0.7 pad_maximum_fusion.3.own_units
  867.5 0.7 pad_maximum_fusion.2.own_sums
  868.2 55.3 %shard_map.174 = (f32[256,2048]{1,0:T(8,128)}, f32[2,11,2,16,256]{4,3,2,1,0:T(8,128)}, f32[2,3,2,16,704]{4,3,2,1,0:T(8,128)}) custom-call(f32[128,2048]{1,0:T(8,128)} %get-tuple-element.134.grad, bf16[384,256]{1,0:T(8,128)(2,1)} %pad_maximum_fusion.2.own_sums, bf16[96,704]{1,0:T(8,128)(2,1)} %pad_maximum_fusion.3.own_units, f32[1,1]{1,0:T(1,128)} %bitcast.28.slot), custom_call_target="tpu_custom_call" | custom-call | tf_op jit(solution)/shard_map/pallas_call | solution.py:1114
  923.4 3.0 reshape.88
  926.5 2.4 copy.55
  928.9 4.0 reshape.89
  932.9 0.8 reshape_reshape.4
  933.7 1.1 copy.50
  934.8 1.6 reshape.84
  936.4 2.0 copy.75
  938.4 1.9 copy.76
  (46 shorter events, 5.5 us)
Async XLA Ops:
  0.6 13.9 %copy-start = (bf16[256,2048]{1,0:T(8,128)(2,1)S(1)}, bf16[256,2048]{1,0:T(8,128)(2,1)}, u32[]{:S(2)}) copy-start(bf16[256,2048]{1,0:T(8,128)(2,1)} %param.14) | copy-start | bytes 3145732
  12.3 100.9 %collective-permute-start.2 = (s32[2062]{0:T(1024)S(1)}, s32[2062]{0:T(1024)S(1)}, u32[]{:S(2)}, u32[]{:S(2)}) collective-permute-start(s32[2062]{0:T(1024)S(1)} %concatenate.18), channel_id=1, source_target_pairs={{0,0},{2,2},{4,8},{6,10},{8,4},{10,6},{12,12},{14,14},{16,16},{18,... | collective-permute-start | bytes 24752 | tf_op jit(solution)/shard_map/ppermute | solution.py:1154
  15.4 124.0 %collective-permute-start.1 = (bf16[128,2048]{1,0:T(8,128)(2,1)}, bf16[128,2048]{1,0:T(8,128)(2,1)}, u32[]{:S(2)}, u32[]{:S(2)}) collective-permute-start(bf16[128,2048]{1,0:T(8,128)(2,1)} %constant_dynamic-slice_fusion.7), channel_id=1, source_target_pairs={{0,0},{2,2},{4,8},{6,10},{8,4},{10,6},{12,12},{14,14},{16,16},{18,... | collective-permute-start | bytes 1572872 | tf_op jit(solution)/shard_map/ppermute | solution.py:1154
  22.2 121.7 %collective-permute-start = (bf16[128,2048]{1,0:T(8,128)(2,1)}, bf16[128,2048]{1,0:T(8,128)(2,1)S(1)}, u32[]{:S(2)}, u32[]{:S(2)}) collective-permute-start(bf16[128,2048]{1,0:T(8,128)(2,1)} %constant_dynamic-slice_fusion.8), channel_id=1, source_target_pairs={{0,0},{2,2},{4,8},{6,10},{8,4},{10,6},{12,12},{14,14},{16,16},{18,... | collective-permute-start | bytes 1572872 | tf_op jit(solution)/shard_map/ppermute | solution.py:1154
  117.1 8.8 copy-start.4
  125.8 3.6 copy-start.2
  125.8 2.3 slice-start
  125.8 2.3 slice-start.1
  787.8 78.7 %copy-start.5 = (bf16[4,2,64,768]{3,2,1,0:T(8,128)(2,1)S(1)}, bf16[4,2,64,768]{3,2,1,0:T(8,128)(2,1)}, u32[]{:S(2)}) copy-start(bf16[4,2,64,768]{3,2,1,0:T(8,128)(2,1)} %get-tuple-element.138) | copy-start | bytes 2359300
  865.3 2.2 copy-start.6
  865.3 2.1 copy-start.7
  928.9 4.0 copy-start.3
  933.7 6.7 copy-start.1

commit v4 on v3

--- a/solution.py
+++ b/solution.py
@@ -47,6 +47,12 @@
     return copy
 
 
+def when_even(place, body):
+    even = place.pos % 2 == 0
+    pl.when(even)(lambda: body(True))
+    pl.when(jnp.logical_not(even))(lambda: body(False))
+
+
 def flip(number, bits):
     b = 1
     while b <= bits:
@@ -75,7 +81,9 @@
         return [dma((n,))] * 2 + [dma((n, max(1, nf // 2 - 1)))] * 4
 
     def block(self, g, q):
-        start = pl.multiple_of((g * self.place.n + q) * self.rows, self.rows)
+        n, h = self.place.n, self.place.h
+        source = (g // 2 * 2 + q // h) * n + g % 2 * h + q % h
+        start = pl.multiple_of(source * self.rows, self.rows)
         return self.w.at[pl.ds(start, self.rows)]
 
     def chip(self, q):
@@ -354,27 +362,30 @@
 
 
 class Gather:
-    def __init__(self, place, x, send_r, recv_r, send_l, recv_l, core_send, core_recv):
+    def __init__(self, place, x, send_r, recv_r, send_l, recv_l, core_send, core_recv, lean=False):
         self.place, self.x = place, x
         self.sems = (send_r, recv_r, send_l, recv_l, core_send, core_recv)
-        self.to_right, self.to_left, self.across = [], [], []
+        self.lean = lean and place.n == 4
+        self.right, self.left, self.across = {}, {}, []
 
     @staticmethod
     def semaphores(n):
         dma = pltpu.SemaphoreType.DMA
-        return [dma((n // 2,))] * 4 + [dma((n,))] * 2
-
-    def _pass_on(self, s):
+        return [dma((n,))] * 4 + [dma((n,))] * 2
+
+    def _make(self, s):
         place, x = self.place, self.x
         send_r, recv_r, send_l, recv_l = self.sems[:4]
-        rows, half, t = x.shape[2], place.n // 2, place.t
-        top = rows // 2
-        part_r = pl.ds(0, top) if s == half - 1 else pl.ds(0, rows)
-        part_l = pl.ds(top, top) if s == half - 1 else pl.ds(0, rows)
-        right_at = x.at[place.ring(-s)[0], t, part_r]
-        left_at = x.at[place.ring(s)[0], t, part_l]
-        self.to_right.append(remote(right_at, right_at, send_r.at[s], recv_r.at[s], place.ring(1)[1]))
-        self.to_left.append(remote(left_at, left_at, send_l.at[s], recv_l.at[s], place.ring(-1)[1]))
+        top = x.shape[2] // 2
+        last = s == place.n // 2 - 1
+        for i in range(1 if last and not self.lean else 2):
+            for made, sign, send, recv in ((self.right, 1, send_r, recv_r), (self.left, -1, send_l, recv_l)):
+                piece = i if sign > 0 else 1 - i
+                at = x.at[place.ring(-sign * s)[0], place.t, pl.ds(piece * top, top)]
+                made[s, i] = pltpu.make_async_remote_copy(
+                    src_ref=at, dst_ref=at, send_sem=send.at[2 * s + i], recv_sem=recv.at[2 * s + i],
+                    device_id=place.ring(sign)[1], device_id_type=MESH,
+                )
 
     def _cross(self, q):
         core_send, core_recv = self.sems[4:]
@@ -383,19 +394,42 @@
         self.across.append(remote(at, at, core_send.at[slot], core_recv.at[slot], other))
 
     def begin(self):
-        self._pass_on(0)
+        for s in range(self.place.n // 2):
+            self._make(s)
+        for i in range(2):
+            self.right[0, i].start()
+            self.left[0, i].start()
         self._cross(self.place.q)
+
+    def _hop(self, s):
+        last = self.place.n // 2 - 1
+        if not self.lean:
+            for i in range(1 if s == last else 2):
+                for stream in (self.right, self.left):
+                    stream[s, i].wait_recv()
+                    if s < last - 1 or (s == last - 1 and i == 0):
+                        stream[s + 1, i].start()
+            return
+
+        def body(even):
+            along_ctx, along_fsdp = (self.left, self.right) if even else (self.right, self.left)
+            for i in range(2):
+                if s == 0:
+                    along_ctx[0, i].wait_recv()
+                    along_ctx[1, i].start()
+                    along_fsdp[0, i].wait_recv()
+                else:
+                    along_fsdp[1, i].wait_recv()
+
+        when_even(self.place, body)
 
     def chunks(self):
         place, half = self.place, self.place.n // 2
         self.across[0].wait_recv()
         yield place.q
         for s in range(half):
-            self.to_right[s].wait_recv()
-            self.to_left[s].wait_recv()
+            self._hop(s)
             arrived = [place.ring(half)[0]] if s == half - 1 else [place.ring(-s - 1)[0], place.ring(s + 1)[0]]
-            if s < half - 1:
-                self._pass_on(s + 1)
             first = len(self.across)
             for q in arrived:
                 self._cross(q)
@@ -404,7 +438,23 @@
                 yield q
 
     def finish(self):
-        for copy in self.to_right + self.to_left + self.across:
+        last = self.place.n // 2 - 1
+        for s in range(last + 1):
+            for i in range(2):
+                if s < last:
+                    self.right[s, i].wait_send()
+                    self.left[s, i].wait_send()
+                elif not self.lean and i == 0:
+                    self.right[s, 0].wait_send()
+                    self.left[s, 0].wait_send()
+        if self.lean:
+
+            def body(even):
+                for i in range(2):
+                    (self.left if even else self.right)[1, i].wait_send()
+
+            when_even(self.place, body)
+        for copy in self.across:
             copy.wait_send()
 
 
@@ -417,19 +467,25 @@
 
 
 class Reduce:
-    def __init__(self, place, p, from_core, in_r, in_l, send_r, recv_r, send_l, recv_l, core_send, core_recv):
+    def __init__(self, place, p, from_core, in_r, in_l, send_r, recv_r, send_l, recv_l, core_send, core_recv, lean=False):
         self.place, self.p, self.from_core, self.in_r, self.in_l = place, p, from_core, in_r, in_l
         self.sems = (send_r, recv_r, send_l, recv_l, core_send, core_recv)
+        self.lean = lean and place.n == 4
         half = place.n // 2
         self.order = [half] + [k for j in range(half - 1, 0, -1) for k in (j, -j)] + [0]
         self.chips = {k: place.ring(k)[0] for k in self.order}
-        self.across, self.to_right, self.to_left = {}, [], []
+        self.across, self.copies = {}, {}
+        for sign in (1, -1):
+            for s in range(half):
+                for piece in range(2):
+                    if s or self.lean or piece == (sign < 0):
+                        self._copy(sign, s, piece)
 
     @staticmethod
     def scratch(n, rows, width):
         dma = pltpu.SemaphoreType.DMA
         wide = [pltpu.VMEM((n, rows, width), BF)] + [pltpu.VMEM((n // 2, rows, width), BF)] * 2
-        return wide + [dma((n // 2,))] * 4 + [dma((n,))] * 2
+        return wide + [dma((n // 2, 2))] * 4 + [dma((n,))] * 2
 
     def offer(self, k):
         core_send, core_recv = self.sems[4:]
@@ -442,56 +498,89 @@
         q = self.chips[k]
         return self.p[q, self.place.t, at].astype(F32) + self.from_core[q, at].astype(F32)
 
-    def _add(self, k, start, count, extra=None):
+    def _add(self, k, piece, extra=None):
+        top = self.p.shape[2] // 2
+
         def body(at):
-            whole = pl.ds(pl.multiple_of(start + at.start, 16), at.size)
+            whole = pl.ds(pl.multiple_of(piece * top + at.start, 16), at.size)
             total = self._local(k, whole)
             if extra is not None:
                 total = total + extra[whole].astype(F32)
             self.from_core[self.chips[k], whole] = total.astype(BF)
 
-        by_rows(count, body)
+        by_rows(top, body)
+
+    def _copy(self, sign, s, piece):
+        if (sign, s, piece) not in self.copies:
+            place, top = self.place, self.p.shape[2] // 2
+            send, recv = self.sems[:2] if sign > 0 else self.sems[2:4]
+            target = self.in_r if sign > 0 else self.in_l
+            k = place.n // 2 - s
+            rows = pl.ds(piece * top, top)
+            self.copies[sign, s, piece] = pltpu.make_async_remote_copy(
+                src_ref=self.from_core.at[self.chips[sign * k if s else k], rows], dst_ref=target.at[s, rows],
+                send_sem=send.at[s, piece], recv_sem=recv.at[s, piece],
+                device_id=place.ring(sign)[1], device_id_type=MESH,
+            )
+        return self.copies[sign, s, piece]
 
     def far(self):
-        send_r, recv_r, send_l, recv_l = self.sems[:4]
-        place, half = self.place, self.place.n // 2
-        rows = self.p.shape[2]
-        top = rows // 2
+        half = self.place.n // 2
         self.across[half].wait_recv()
-        self._add(half, 0, rows)
-        low, high = pl.ds(0, top), pl.ds(top, top)
-        sums = self.from_core.at[self.chips[half]]
-        right, left = place.ring(1)[1], place.ring(-1)[1]
-        self.to_right.append(remote(sums.at[low], self.in_r.at[0, low], send_r.at[0], recv_r.at[0], right))
-        self.to_left.append(remote(sums.at[high], self.in_l.at[0, high], send_l.at[0], recv_l.at[0], left))
+        self._add(half, 0)
+        self._add(half, 1)
+        if self.lean:
+            self.across[1].wait_recv()
+            self.across[-1].wait_recv()
+
+            def body(even):
+                sign = -1 if even else 1
+                for piece in range(2):
+                    self._copy(sign, 0, piece).start()
+                for piece in range(2):
+                    self._add(sign, piece)
+                    self._copy(sign, 1, piece).start()
+
+            when_even(self.place, body)
+            return
+        self._copy(1, 0, 0).start()
+        self._copy(-1, 0, 1).start()
+        if half > 1:
+            k = half - 1
+            for sign, piece in ((1, 1), (-1, 0)):
+                self.across[sign * k].wait_recv()
+                self._add(sign * k, piece)
+                self._copy(sign, 1, piece).start()
 
     def near(self, s):
-        send_r, recv_r, send_l, recv_l = self.sems[:4]
-        place, k = self.place, self.place.n // 2 - s
-        rows = self.p.shape[2]
-        top = rows // 2
-        self.across[k].wait_recv()
-        self.across[-k].wait_recv()
-        if s == 1:
-            self._add(k, top, top)
-            self._add(-k, 0, top)
-        start = 0 if s == 1 else None
-        self.to_right[-1].wait_recv()
-        self._add(k, 0, top if s == 1 else rows, self.in_r.at[s - 1])
-        self.to_right.append(
-            remote(self.from_core.at[self.chips[k]], self.in_r.at[s], send_r.at[s], recv_r.at[s], place.ring(1)[1])
-        )
-        self.to_left[-1].wait_recv()
-        self._add(-k, top if s == 1 else 0, top if s == 1 else rows, self.in_l.at[s - 1])
-        self.to_left.append(
-            remote(self.from_core.at[self.chips[-k]], self.in_l.at[s], send_l.at[s], recv_l.at[s], place.ring(-1)[1])
-        )
+        half = self.place.n // 2
+        k = half - s
+        if self.lean:
+
+            def body(even):
+                sign = 1 if even else -1
+                for piece in range(2):
+                    self._copy(sign, 0, piece).wait_recv()
+                    self._add(sign, piece, (self.in_r if even else self.in_l).at[0])
+                    self._copy(sign, 1, piece).start()
+
+            when_even(self.place, body)
+            return
+        if s > 1:
+            self.across[k].wait_recv()
+            self.across[-k].wait_recv()
+        for sign, first, held in ((1, 0, self.in_r), (-1, 1, self.in_l)):
+            for piece in (first,) if s == 1 else (first, 1 - first):
+                self._copy(sign, s - 1, piece).wait_recv()
+                self._add(sign * k, piece, held.at[s - 1])
+                self._copy(sign, s, piece).start()
 
     def end(self, use):
         half = self.place.n // 2
         self.across[0].wait_recv()
-        self.to_right[-1].wait_recv()
-        self.to_left[-1].wait_recv()
+        for sign in (1, -1):
+            for piece in range(2):
+                self._copy(sign, half - 1, piece).wait_recv()
 
         def body(at):
             use(at, self._local(0, at) + self.in_r[half - 1, at].astype(F32) + self.in_l[half - 1, at].astype(F32))
@@ -499,7 +588,22 @@
         by_rows(self.p.shape[2], body)
 
     def finish(self):
-        for copy in self.to_right + self.to_left + list(self.across.values()):
+        half = self.place.n // 2
+        if self.lean:
+
+            def body(even):
+                for piece in range(2):
+                    self._copy(-1 if even else 1, 0, piece).wait_send()
+
+            when_even(self.place, body)
+        else:
+            self._copy(1, 0, 0).wait_send()
+            self._copy(-1, 0, 1).wait_send()
+        for s in range(1, half):
+            for sign in (1, -1):
+                for piece in range(2):
+                    self._copy(sign, s, piece).wait_send()
+        for copy in self.across.values():
             copy.wait_send()
 
     def run(self, use, before=None):
@@ -559,7 +663,7 @@
 
 def write_norm(x_rows, source, gain):
     def body(at):
-        v = source[at]
+        v = source[at].astype(F32)
         x_rows[at] = (v * rms_scale(v) * gain[...]).astype(BF)
 
     by_rows(source.shape[0], body)
@@ -587,7 +691,7 @@
 
 
 def attention_forward(
-    n, nf, layer, part, rank, plan,
+    n, nf, layer, part, rank, lean, plan,
     residual, gain, w_hbm, a_model, a_head, cosine, sine, query_bits, key_bits, lam, *refs,
 ):
     jobs, refs = plan.split(refs)
@@ -598,7 +702,7 @@
     tree = n * chip_rows
     load = pltpu.make_async_copy(w_hbm, w, copy_sems.at[0])
     load.start()
-    gather, reduce = Gather(place, x, *sems[:6]), Reduce(place, p, *sems[6:])
+    gather, reduce = Gather(place, x, *sems[:6], lean=lean), Reduce(place, p, *sems[6:], lean=lean)
     write_norm(x.at[place.q, place.t], residual, gain)
     block_diagonal(raised, (a_head[rank : 4 * rank], 3), rank, VD)
     work = plan.work(place, nf, jobs)
@@ -670,7 +774,7 @@
     work.at(4)
 
     def use(at, total):
-        middle[at] = residual[at] + total
+        middle[at] = residual[at].astype(F32) + total
 
     reduce.end(use)
     work.at(5)
@@ -681,7 +785,7 @@
 
 
 def ffn_forward(
-    n, nf, units, rank, plan,
+    n, nf, units, rank, lean, plan,
     residual, gain, w_hbm, a_model, e_model, *refs,
 ):
     jobs, refs = plan.split(refs)
@@ -692,7 +796,7 @@
     tree = n * chip_rows
     load = pltpu.make_async_copy(w_hbm, w.at[:, pl.ds(0, 2 * units)], copy_sems.at[0])
     load.start()
-    gather, reduce = Gather(place, x, *sems[:6]), Reduce(place, p, *sems[6:])
+    gather, reduce = Gather(place, x, *sems[:6], lean=lean), Reduce(place, p, *sems[6:], lean=lean)
     write_norm(x.at[place.q, place.t], residual, gain)
     block_diagonal(raised, (e_model, 2), rank, units)
     work = plan.work(place, nf, jobs)
@@ -828,7 +932,7 @@
 
     def use(at, total):
         inputs = middle[at]
-        grad_out[at] = grad[at] + norm_back(total, inputs, rms_scale(inputs), gain[...])
+        grad_out[at] = grad[at].astype(F32) + norm_back(total, inputs, rms_scale(inputs), gain[...])
 
     def adapters():
         fetch.wait()
@@ -964,8 +1068,7 @@
 
     def full_tile(jp, carry):
         at = pl.ds(pl.multiple_of(jp * block, block), block)
-        j = jp // 4 * 4 + jp % 2 * 2 + jp // 2 % 2
-        q, t = j // 2, j % 2
+        q, t = jp // 2, jp % 2
         flat = x[:, :, :, at].reshape(tree, block)
         p_own[q, t, : 3 * rank] = (part * t_mm(dsmall[...], flat)).astype(BF)
         p_own[q, t, 4 * rank : 6 * rank] = grad_ffn_in[:, at]
@@ -1000,8 +1103,8 @@
         own_sum[at] = total.astype(BF)
 
     def use(at, total):
-        inputs = residual[at]
-        grad_out[at] = grad[at] + norm_back(total, inputs, rms_scale(inputs), gain[...])
+        inputs = residual[at].astype(F32)
+        grad_out[at] = grad[at].astype(F32) + norm_back(total, inputs, rms_scale(inputs), gain[...])
 
     reduce.end(use)
     reduce_own.end(use_own)
@@ -1191,20 +1294,23 @@
     rank, adapters = adapter_model_factors.shape[3], adapter_model_factors.shape[2]
     h = n // 2
 
-    def swap_columns(x):
-        lead = x.shape[:-1]
-        cut = x.reshape(lead + (nf // 2, 2, 2, h * weight_rows))
-        return jnp.swapaxes(cut, -3, -2).reshape(lead + (width,))
-
-    of_tree = lax.all_gather(jnp.stack([segments, depths]), "ctx", axis=1, tiled=True)
-    notes = jnp.concatenate([of_tree[0], of_tree[1], parents[0], tree_adapter_index])
-    notes = swap_trees(notes, nf, nc)
-    seg, dep = notes[:tree], notes[tree : 2 * tree]
-    parent_row, slot = notes[2 * tree : 2 * tree + NSEG], notes[2 * tree + NSEG]
+    notes = jnp.concatenate([segments, depths, parents[0], tree_adapter_index])
+    order = jnp.arange(n)
+    of_tree = jnp.zeros((n, notes.shape[0]), jnp.int32)
+    for d in range(n):
+
+        def hand_out(f_hi, f_lo, c_hi, c_lo, d=d):
+            to = (c_hi * (n // 2) + c_lo) ^ d
+            return f_hi, to // (n // 2), f_lo, to % (n // 2)
+
+        part_of_tree = permute(notes, nf, nc, hand_out)
+        of_tree = of_tree + jnp.where(order[:, None] == flip(q, d), part_of_tree[None], 0)
+    seg, dep = of_tree[:, :tokens_dev].reshape(tree), of_tree[:, tokens_dev : 2 * tokens_dev].reshape(tree)
+    parent_row, slot = of_tree[0, 2 * tokens_dev : 2 * tokens_dev + NSEG], of_tree[0, 2 * tokens_dev + NSEG]
     own_tokens = lax.dynamic_slice_in_dim(tokens, t * rows, rows, 0)
     own_cotangent = lax.dynamic_slice_in_dim(cotangent, t * rows, rows, 0)
-    residual = swap_columns(swap_trees(own_tokens, nf, nc)).astype(F32)
-    own_cotangent = swap_columns(swap_trees(own_cotangent, nf, nc))
+    residual = swap_trees(own_tokens, nf, nc)
+    own_cotangent = swap_trees(own_cotangent, nf, nc)
 
     query_bits, key_bits = line_bits(parent_row, seg)
     query_bits, key_bits = query_bits[:, None], key_bits[None, :]
@@ -1213,11 +1319,11 @@
     cosine, sine = jnp.cos(angles), jnp.sin(angles)
     cosine = jnp.concatenate([cosine, cosine], axis=1)
     sine = jnp.concatenate([-sine, sine], axis=1)
-    gains = swap_columns(layer_norm_gains)
+    gains = layer_norm_gains
 
     a_all = lax.dynamic_index_in_dim(adapter_model_factors, slot, 2, keepdims=False)
     e_all = lax.dynamic_index_in_dim(adapter_hidden_factors, slot, 2, keepdims=False)
-    a_model = swap_columns(a_all).reshape(layers, 11 * rank, width)
+    a_model = a_all.reshape(layers, 11 * rank, width)
     e_all = e_all.reshape(layers, 3 * rank, -1)
     head_at = (t * heads_tp + head) * VD
 
@@ -1294,7 +1400,7 @@
             moves("forward", 0, parts(n, 3, 4)) + ([] if last else [("scatter", 1)]),
         )
         got = run(
-            functools.partial(attention_forward, n, nf, l, part, rank, plan),
+            functools.partial(attention_forward, n, nf, l, part, rank, not last, plan),
             near(residual, gain_a) + far(w_attention) + near(*shared),
             [
                 out((rows, width), F32),
@@ -1327,7 +1433,7 @@
             [] if last else moves("forward", 1, parts(n, 2, 4)),
         )
         ffn = run(
-            functools.partial(ffn_forward, n, nf, units, rank, plan),
+            functools.partial(ffn_forward, n, nf, units, rank, not last, plan),
             near(middle, gain_f) + far(w_g[l]) + near(a_model[l], e_model[l]),
             [
                 out((rows, width), F32),
@@ -1349,7 +1455,7 @@
         saved.append((residual, middle, gain_a, gain_f, shared, kept, ffn[1:]))
         residual = ffn[0]
 
-    grad = own_cotangent.astype(F32)
+    grad = own_cotangent
     units_here, sums_here, block = [], [], width // (2 * n)
     for l in reversed(range(layers)):
         residual_in, middle, gain_a, gain_f, shared, kept, ffn = saved[l]
@@ -1439,8 +1545,8 @@
         ],
     )
     return (
-        swap_columns(outputs.reshape(2 * rows, width)),
-        swap_columns(tokens_grad),
+        outputs.reshape(2 * rows, width),
+        tokens_grad,
         grad_model,
         grad_hidden,
     )

time: 955 us -> 865 us (0.906)
  Pallas kernels: 859 us -> 802 us
  local copies, waits for them, and re-layouts: 50.4 us -> 22.5 us
    pallas_call x10, Pallas kernels: 859 us -> 802 us  [call(): pl.pallas_call(kernel, out_shape=[jax.ShapeDtypeStruct(shape, kind) for s...]
    reshape x7 -> x0, local copies, waits for them, and re-layouts: 13.5 us -> none  [the longest x4 7.85 us: swap_columns(): cut = x.reshape(lead + (nf // 2, 2, 2, h * weight_rows))]
  transfers between devices with their start and end apart: 3 -> 6, of which waited for: 0 -> 0; matrix products, arithmetic and copies ran while one was open for 4% -> 2% of each run, Pallas kernels for 9% -> 54%
where the time goes in v4:
time: 865 us; the launch traced here: 853 us
  Pallas kernels  802 us (93%)
  local copies, waits for them, and re-layouts  22.5 us (3%)
  starting transfers between devices  16.7 us (2%)
    pallas_call x10, Pallas kernels, call(): pl.pallas_call(kernel, out_shape=[jax.ShapeDtypeStruct(shape, kind) for s...  802 us
  transfers between devices with their start and end apart: 6, of which 0 were waited for; matrix products, arithmetic and copies ran while one was open for 2% of the time, Pallas kernels for 54%

profile of v4, /device:TPU:3, one launch (start us, length us, event | category | flops | bytes accessed | tf_op | source)
XLA Modules:
  0.0 852.8 jit_solution(247509677128018120)
XLA Ops:
  0.6 0.0 copy-start
  1.4 0.8 pad_add_fusion
  2.2 4.2 collective-permute-start.2
  6.4 2.1 collective-permute-start.3
  8.4 2.4 collective-permute-start.5
  10.9 0.8 constant_dynamic-slice_fusion.8
  11.7 1.9 collective-permute-start.1
  13.8 0.8 fusion.6
  14.6 1.4 slice_bitcast_fusion.2
  16.0 1.9 constant_dynamic-slice_fusion.9
  17.9 0.6 constant_dynamic-slice_fusion.6.lam
  18.5 0.6 constant_dynamic-slice_fusion.3.lam
  19.1 81.1 %shard_map.165 = (bf16[2048,1024]{1,0:T(8,128)(2,1)}, bf16[2048,1536]{1,0:T(8,128)(2,1)}, bf16[2048,768]{1,0:T(8,128)(2,1)}, bf16[4,128,1024]{2,1,0:T(8,128)(2,1...) custom-call(bf16[2,3,128,1024]{3,2,1,0:T(8,128)(2,1)} %bitcast.64, bf16[2,128,1024]{2,1,0:T(8,128)(2,1)} %output.1, ...), custom_call_target="tpu_custom_call" | custom-call | tf_op jit(solution)/shard_map/pallas_call | solution.py:1217
  100.3 6.1 collective-permute-start
  106.4 0.1 select_add_fusion
  106.5 0.6 slice.90
  109.0 1.1 dynamic-slice_bitcast_fusion.2
  110.1 0.2 select_reduce_fusion.1
  110.3 1.3 constant_dynamic-slice_fusion.5
  111.7 0.1 select_reduce_fusion
  111.8 1.9 fusion
  113.7 0.7 fusion.2
  114.4 0.6 pad_maximum_fusion.4
  115.7 1.0 copy.32.query_bits
  116.7 0.6 copy.42
  117.3 1.0 pad_maximum_fusion.cosine
  118.3 1.0 pad_maximum_fusion.1.sine
  119.3 2.6 constant_dynamic-slice_fusion.7
  121.9 0.8 copy-done.2
  122.7 104.0 %shard_map.166 = (bf16[2048,1024]{1,0:T(8,128)(2,1)}, bf16[2048,1536]{1,0:T(8,128)(2,1)}, bf16[2048,1536]{1,0:T(8,128)(2,1)}, bf16[2048,768]{1,0:T(8,128)(2,1)},...) custom-call(bf16[128,2048]{1,0:T(8,128)(2,1)} %copy-done.2, ...), custom_call_target="tpu_custom_call", output_to_operand_aliasing={{2}: (12, {}), {3}: (13, {})} | custom-call | tf_op jit(solution)/shard_map/pallas_call | solution.py:1217
  226.7 107.4 %shard_map.167 = (bf16[2048,768]{1,0:T(8,128)(2,1)}, bf16[2048,768]{1,0:T(8,128)(2,1)}, bf16[2048,1024]{1,0:T(8,128)(2,1)}, bf16[2048,1536]{1,0:T(8,128)(2,1)}, ...) custom-call(f32[128,2048]{1,0:T(8,128)} %get-tuple-element.78.residu, ...), custom_call_target="tpu_custom_call", output_to_operand_aliasing={{1}: (6, {}), {2}: (7, {}), {3}: (8, {})} | custom-call | tf_op jit(solution)/shard_map/pallas_call | solution.py:1217
  334.1 95.3 %shard_map.168 = (bf16[2048,1536]{1,0:T(8,128)(2,1)}, bf16[2048,768]{1,0:T(8,128)(2,1)}, f32[128,2048]{1,0:T(8,128)}, bf16[4,2,128,2048]{3,2,1,0:T(8,128)(2,1)},...) custom-call(f32[128,2048]{1,0:T(8,128)} %get-tuple-element.84.residu, ...), custom_call_target="tpu_custom_call", output_to_operand_aliasing={{0}: (10, {}), {1}: (11, {})} | custom-call | tf_op jit(solution)/shard_map/pallas_call | solution.py:1217
  429.5 72.1 %shard_map.169 = (bf16[2048,768]{1,0:T(8,128)(2,1)}, f32[128,2048]{1,0:T(8,128)}, bf16[4,2,128,2048]{3,2,1,0:T(8,128)(2,1)}, bf16[1024,768]{1,0:T(8,128)(2,1)}, ...) custom-call(f32[128,2048]{1,0:T(8,128)} %get-tuple-element.88.residu, ...), custom_call_target="tpu_custom_call", output_to_operand_aliasing={{0}: (5, {})} | custom-call | tf_op jit(solution)/shard_map/pallas_call | solution.py:1217
  501.6 0.8 copy-done.6
  502.4 72.3 %shard_map.170 = (bf16[2,128,2048]{2,1,0:T(8,128)(2,1)}, f32[128,2048]{1,0:T(8,128)}, bf16[16,2048]{1,0:T(8,128)(2,1)}, bf16[32,2048]{1,0:T(8,128)(2,1)}, bf16[64,768]{1,0:T(8,128)(2,1)}) custom-call(bf16[128,2048]{1,0:T(8,128)(2,1)} %copy-done.6, f32[128,2048]{1,0:T(8,128)} %get-tuple-element.88.residual.middle, f32[1,2048]{1,0:T(1,128)} %get-tuple-element.148.gain, ...), custom_call_target="tpu_custom_call" | custom-call | tf_op jit(solution)/shard_map/pallas_call | solution.py:1217
  574.7 75.8 %shard_map.171 = (f32[128,2048]{1,0:T(8,128)}, bf16[192,256]{1,0:T(8,128)(2,1)}, bf16[4,2,64,768]{3,2,1,0:T(8,128)(2,1)}) custom-call(f32[128,2048]{1,0:T(8,128)} %get-tuple-element.100.grad, f32[128,2048]{1,0:T(8,128)} %get-tuple-element.84.residual, f32[1,2048]{1,0:T(1,128)} %get-tuple-element.151.gain, bf16[2048,1024]{1,0:T(8,128)(2,1)} %get-tuple-element.85.w_hbm, ...), custom_call_target="tpu_custom_call" | custom-call | tf_op jit(solution)/shard_map/pallas_call | solution.py:1217
  650.6 59.5 %shard_map.172 = (f32[128,2048]{1,0:T(8,128)}, bf16[16,2048]{1,0:T(8,128)(2,1)}, bf16[32,2048]{1,0:T(8,128)(2,1)}, bf16[64,768]{1,0:T(8,128)(2,1)}) custom-call(f32[128,2048]{1,0:T(8,128)} %get-tuple-element.113.grad, f32[128,2048]{1,0:T(8,128)} %get-tuple-element.78.residual.middle, f32[1,2048]{1,0:T(1,128)} %get-tuple-element.149.gain, ...), custom_call_target="tpu_custom_call" | custom-call | tf_op jit(solution)/shard_map/pallas_call | solution.py:1217
  710.1 76.3 %shard_map.173 = (f32[128,2048]{1,0:T(8,128)}, bf16[192,256]{1,0:T(8,128)(2,1)}, bf16[4,2,64,768]{3,2,1,0:T(8,128)(2,1)}) custom-call(f32[128,2048]{1,0:T(8,128)} %get-tuple-element.121.grad, bf16[128,2048]{1,0:T(8,128)(2,1)} %copy-done.2, f32[1,2048]{1,0:T(1,128)} %get-tuple-element.150.gain, bf16[2048,1024]{1,0:T(8,128)(2,1)} %get-tuple-element.73.w_hbm, ...), custom_call_target="tpu_custom_call" | custom-call | tf_op jit(solution)/shard_map/pallas_call | solution.py:1217
  786.4 1.1 dynamic-slice_bitcast_fusion.1
  787.7 0.1 constant_dynamic-slice_fusion.2
  787.8 0.1 constant_dynamic-slice_fusion.1
  787.9 0.7 pad_maximum_fusion.3.own_units
  788.6 0.7 pad_maximum_fusion.2.own_sums
  789.2 57.8 %shard_map.174 = (f32[256,2048]{1,0:T(8,128)}, f32[2,11,2,16,256]{4,3,2,1,0:T(8,128)}, f32[2,3,2,16,704]{4,3,2,1,0:T(8,128)}) custom-call(f32[128,2048]{1,0:T(8,128)} %get-tuple-element.134.grad, bf16[384,256]{1,0:T(8,128)(2,1)} %pad_maximum_fusion.2.own_sums, bf16[96,704]{1,0:T(8,128)(2,1)} %pad_maximum_fusion.3.own_units, f32[1,1]{1,0:T(1,128)} %bitcast.24.slot), custom_call_target="tpu_custom_call" | custom-call | tf_op jit(solution)/shard_map/pallas_call | solution.py:1217
  847.1 2.5 copy.56
  849.5 1.3 copy.57
  850.9 0.9 copy.58
  851.7 0.8 copy.59
  (40 shorter events, 0.3 us)
Async XLA Ops:
  0.6 10.2 %copy-start = (bf16[256,2048]{1,0:T(8,128)(2,1)S(1)}, bf16[256,2048]{1,0:T(8,128)(2,1)}, u32[]{:S(2)}) copy-start(bf16[256,2048]{1,0:T(8,128)(2,1)} %param.14) | copy-start | bytes 3145732
  2.2 98.1 %collective-permute-start.2 = (s32[526]{0:T(1024)S(1)}, s32[526]{0:T(1024)S(1)}, u32[]{:S(2)}, u32[]{:S(2)}) collective-permute-start(s32[526]{0:T(1024)S(1)} %pad_add_fusion), channel_id=1, source_target_pairs={{0,0},{2,2},{4,8},{6,10},{8,4},{10,6},{12,12},{14,14},{16,16},{18,... | collective-permute-start | bytes 6320 | tf_op jit(solution)/shard_map/ppermute | solution.py:1257
  6.4 100.0 %collective-permute-start.3 = (s32[526]{0:T(1024)S(1)}, s32[526]{0:T(1024)S(1)}, u32[]{:S(2)}, u32[]{:S(2)}) collective-permute-start(s32[526]{0:T(1024)S(1)} %pad_add_fusion), channel_id=1, source_target_pairs={{0,2},{2,0},{4,10},{6,8},{8,6},{10,4},{12,14},{14,12},{16,18},{18,... | collective-permute-start | bytes 6320 | tf_op jit(solution)/shard_map/ppermute | solution.py:1257
  8.4 97.9 %collective-permute-start.4 = (s32[526]{0:T(1024)S(1)}, s32[526]{0:T(1024)S(1)}, u32[]{:S(2)}, u32[]{:S(2)}) collective-permute-start(s32[526]{0:T(1024)S(1)} %pad_add_fusion), channel_id=1, source_target_pairs={{0,8},{2,10},{4,0},{6,2},{8,12},{10,14},{12,4},{14,6},{16,24},{18,... | collective-permute-start | bytes 6320 | tf_op jit(solution)/shard_map/ppermute | solution.py:1257
  8.4 98.0 %collective-permute-start.5 = (s32[526]{0:T(1024)S(1)}, s32[526]{0:T(1024)S(1)}, u32[]{:S(2)}, u32[]{:S(2)}) collective-permute-start(s32[526]{0:T(1024)S(1)} %pad_add_fusion), channel_id=1, source_target_pairs={{0,10},{2,8},{4,2},{6,0},{8,14},{10,12},{12,6},{14,4},{16,26},{18,... | collective-permute-start | bytes 6320 | tf_op jit(solution)/shard_map/ppermute | solution.py:1257
  11.7 110.2 %collective-permute-start.1 = (bf16[128,2048]{1,0:T(8,128)(2,1)}, bf16[128,2048]{1,0:T(8,128)(2,1)S(1)}, u32[]{:S(2)}, u32[]{:S(2)}) collective-permute-start(bf16[128,2048]{1,0:T(8,128)(2,1)} %constant_dynamic-slice_fusion.8), channel_id=1, source_target_pairs={{0,0},{2,2},{4,8},{6,10},{8,4},{10,6},{12,12},{14,14},{16,16},{18,... | collective-permute-start | bytes 1572872 | tf_op jit(solution)/shard_map/ppermute | solution.py:1257
  100.3 401.3 %collective-permute-start = (bf16[128,2048]{1,0:T(8,128)(2,1)}, bf16[128,2048]{1,0:T(8,128)(2,1)S(1)}, u32[]{:S(2)}, u32[]{:S(2)}) collective-permute-start(bf16[128,2048]{1,0:T(8,128)(2,1)} %constant_dynamic-slice_fusion.9), channel_id=1, source_target_pairs={{0,0},{2,2},{4,8},{6,10},{8,4},{10,6},{12,12},{14,14},{16,16},{18,... | collective-permute-start | bytes 1572872 | tf_op jit(solution)/shard_map/ppermute | solution.py:1257
  121.9 0.8 copy-start.2
  501.6 0.8 copy-start.6
  710.1 77.4 %copy-start.7 = (bf16[4,2,64,768]{3,2,1,0:T(8,128)(2,1)S(1)}, bf16[4,2,64,768]{3,2,1,0:T(8,128)(2,1)}, u32[]{:S(2)}) copy-start(bf16[4,2,64,768]{3,2,1,0:T(8,128)(2,1)} %get-tuple-element.138) | copy-start | bytes 2359300
  786.4 2.2 copy-start.8
  786.4 2.1 copy-start.9
  847.1 2.5 copy-start.3
  847.1 3.8 copy-start.4
  847.1 5.5 copy-start.1
  849.5 2.2 copy-start.5

commit v5 on v4

--- a/solution.py
+++ b/solution.py
@@ -606,10 +606,11 @@
         for copy in self.across.values():
             copy.wait_send()
 
-    def run(self, use, before=None):
-        for k in self.order:
-            self.offer(k)
-        self.far()
+    def run(self, use, before=None, offered=False):
+        if not offered:
+            for k in self.order:
+                self.offer(k)
+            self.far()
         for s in range(1, self.place.n // 2):
             self.near(s)
         if before is not None:
@@ -692,7 +693,7 @@
 
 def attention_forward(
     n, nf, layer, part, rank, lean, plan,
-    residual, gain, w_hbm, a_model, a_head, cosine, sine, query_bits, key_bits, lam, *refs,
+    residual, gain, w_hbm, a_model, a_head, cosine, sine, query_bits, key_bits, lam, *refs, pace,
 ):
     jobs, refs = plan.split(refs)
     (middle, x_hbm, queries, keys, values, small, log_total, mixed, headed, side,
@@ -709,6 +710,7 @@
     enter(place, nf, bool(plan.scatters))
     gather.begin()
     work.at(0)
+    pace.ready()
     load.wait()
 
     def project(q):
@@ -753,6 +755,7 @@
         side[rows] = mm_t(head, a_head[:rank]).astype(BF)
 
     row_blocks(tree, attend)
+    pace.flush()
     work.at(2)
 
     for k in reduce.order:
@@ -785,24 +788,31 @@
 
 
 def ffn_forward(
-    n, nf, units, rank, lean, plan,
-    residual, gain, w_hbm, a_model, e_model, *refs,
+    n, nf, units, rank, last, plan,
+    residual, gain, w_hbm, a_model, e_model, *refs, pace,
 ):
+    place = Place(n)
+    if last:
+        cotangent, *refs = refs
     jobs, refs = plan.split(refs)
+    if last:
+        all_refs = refs
+        next_hbm, *refs, next_x = refs[:-6]
+        next_gather = Gather(place, next_x, *all_refs[-6:])
     (following, x_hbm, gates, ups, hidden, small, side,
      x, p, w, raised, copy_sems, *sems) = refs
-    place = Place(n)
     chip_rows, width = 2 * x_hbm.shape[2], x_hbm.shape[3]
     tree = n * chip_rows
     load = pltpu.make_async_copy(w_hbm, w.at[:, pl.ds(0, 2 * units)], copy_sems.at[0])
     load.start()
-    gather, reduce = Gather(place, x, *sems[:6], lean=lean), Reduce(place, p, *sems[6:], lean=lean)
+    gather, reduce = Gather(place, x, *sems[:6], lean=not last), Reduce(place, p, *sems[6:], lean=not last)
     write_norm(x.at[place.q, place.t], residual, gain)
     block_diagonal(raised, (e_model, 2), rank, units)
     work = plan.work(place, nf, jobs)
     enter(place, nf, bool(plan.scatters))
     gather.begin()
     work.at(0)
+    pace.ready()
     load.wait()
     step = tile_of(units)
 
@@ -824,10 +834,19 @@
 
         tiles(units, step, unit_tile)
 
+    pace.flush()
+    if last:
+        next_x[place.q, place.t] = cotangent[...]
+        next_gather.begin()
     work.at(2)
     keep = pltpu.make_async_copy(x, x_hbm, copy_sems.at[1])
     keep.start()
 
+    if last:
+        for _ in next_gather.chunks():
+            pass
+        keep_next = pltpu.make_async_copy(next_x, next_hbm, copy_sems.at[2])
+        keep_next.start()
     work.complete(0)
     load = pltpu.make_async_copy(plan.late(jobs), w.at[:, pl.ds(2 * units, units)], copy_sems.at[0])
     load.start()
@@ -859,6 +878,9 @@
     reduce.end(use)
     work.at(5)
     keep.wait()
+    if last:
+        keep_next.wait()
+        next_gather.finish()
     gather.finish()
     reduce.finish()
     work.settle((0,))
@@ -866,10 +888,10 @@
 
 def ffn_backward(
     n, units, rank, carry,
-    grad, middle, gain, w_hbm, w_down_hbm, a_model, e_model, x_hbm, gates, ups, hidden, small, side, *refs,
+    grad, middle, gain, w_hbm, w_down_hbm, a_model, e_model, x_hbm, gates, ups, hidden, small, side, *refs, pace,
 ):
     if carry:
-        final, final_out, *refs = refs
+        final, gathered, final_out, *refs = refs
         *refs, final_rows, home_send, home_recv = refs
     (grad_out, grad_up_down, grad_in, grad_units,
      x, p, w, kept, dgu, dsmall, dside, raised, copy_sems, *sems) = refs
@@ -884,10 +906,15 @@
     fetch.start()
     gather, reduce = Gather(place, x, *sems[:6]), Reduce(place, p, *sems[6:])
 
-    def own(at):
-        x[place.q, place.t, at] = grad[at].astype(BF)
-
-    by_rows(grad.shape[0], own)
+    if carry:
+        come = pltpu.make_async_copy(gathered, x, copy_sems.at[3])
+        come.start()
+    else:
+
+        def own(at):
+            x[place.q, place.t, at] = grad[at].astype(BF)
+
+        by_rows(grad.shape[0], own)
     block_diagonal(raised, (e_model, 2), rank, units)
     if carry:
 
@@ -896,15 +923,19 @@
 
         by_rows(final.shape[0], last_rows)
     enter(place, home=carry)
-    gather.begin()
-    if carry:
+    if not carry:
+        gather.begin()
+    else:
         home = Home(place, final_out, home_send, home_recv)
         home.start(final_rows)
+    pace.ready()
     load.wait()
     load_down.wait()
     step = tile_of(units)
 
-    for q in gather.chunks():
+    if carry:
+        come.wait()
+    for q in list(reduce.chips.values()) if carry else gather.chunks():
         rows = pl.ds(pl.multiple_of(q * chip_rows, chip_rows), chip_rows)
         v = x[q].reshape(chip_rows, width)
         low = (ADAPTER_SCALE * mm_t(v, a_model[10 * rank : 11 * rank])).astype(BF)
@@ -929,6 +960,11 @@
             p[q, :, :, at] = made.astype(BF).reshape(2, chip_rows // 2, at.size)
 
         tiles(width, 512, out_tile)
+        if carry:
+            k = reduce.order[len(reduce.across)]
+            reduce.offer(k)
+            if k == reduce.order[2]:
+                reduce.far()
 
     def use(at, total):
         inputs = middle[at]
@@ -954,8 +990,9 @@
 
         tiles(units, step, unit_tile)
 
-    reduce.run(use, adapters)
-    gather.finish()
+    reduce.run(use, adapters, carry)
+    if not carry:
+        gather.finish()
     reduce.finish()
     if carry:
         home.land()
@@ -968,7 +1005,7 @@
     x_hbm, queries, keys, values, small, log_total, mixed, headed, side,
     grad_up_down, grad_ffn_in, grad_units,
     grad_out, own_sum, all_units,
-    x, p, w, dmixed, dq, dk, dv, dprojected, dsmall, dside, raised, grad_a9, p_own, copy_sems, *sems,
+    x, p, w, dmixed, dq, dk, dv, dprojected, dsmall, dside, raised, grad_a9, p_own, copy_sems, *sems, pace,
 ):
     place = Place(n)
     part = 1.0 / share
@@ -990,25 +1027,9 @@
     gather_units.begin()
     dk[...] = jnp.zeros(dk.shape, F32)
     dv[...] = jnp.zeros(dv.shape, F32)
+    pace.ready()
     load.wait()
 
-    for q in gather.chunks():
-        rows = pl.ds(pl.multiple_of(q * chip_rows, chip_rows), chip_rows)
-        v = x[q].reshape(chip_rows, width)
-        low = (ADAPTER_SCALE * mm_t(v, a_model[9 * rank : 10 * rank])).astype(BF)
-        dside[rows] = low
-        dheaded = mm(v, w[:, 3 * VD :]) + mm(low, a_head[:rank])
-        inputs = mixed[rows].astype(F32)
-        dmixed[rows] = norm_back(dheaded, inputs, rms_scale(inputs), keep_factor(layer)).astype(BF)
-
-    def out_gradient(at):
-        flat = x[:, :, :, at].reshape(tree, at.size)
-        grad_a9[:, at] = (ADAPTER_SCALE * part * t_mm(side[...], flat)).astype(BF)
-
-    tiles(width, 256, out_gradient)
-    gather.finish()
-    fetch = pltpu.make_async_copy(x_hbm, x, copy_sems.at[1])
-    fetch.start()
     score_scale = HD ** (-0.5)
     weight = lam[...]
 
@@ -1029,7 +1050,29 @@
             dk[:count, at] += t_mm(dscores, queries[rows, at])
         dv[:count] += t_mm((both[0] - weight * both[1]).astype(BF), dmix)
 
-    row_blocks(tree, attend)
+    for q in gather.chunks():
+        rows = pl.ds(pl.multiple_of(q * chip_rows, chip_rows), chip_rows)
+        v = x[q].reshape(chip_rows, width)
+        low = (ADAPTER_SCALE * mm_t(v, a_model[9 * rank : 10 * rank])).astype(BF)
+        dside[rows] = low
+        dheaded = mm(v, w[:, 3 * VD :]) + mm(low, a_head[:rank])
+        inputs = mixed[rows].astype(F32)
+        dmixed[rows] = norm_back(dheaded, inputs, rms_scale(inputs), keep_factor(layer)).astype(BF)
+
+        def block(i, carry, q=q):
+            attend(pl.ds(pl.multiple_of(q * chip_rows + i * ROW_BLOCK, ROW_BLOCK), ROW_BLOCK), tree)
+            return carry
+
+        lax.fori_loop(0, chip_rows // ROW_BLOCK, block, 0)
+
+    def out_gradient(at):
+        flat = x[:, :, :, at].reshape(tree, at.size)
+        grad_a9[:, at] = (ADAPTER_SCALE * part * t_mm(side[...], flat)).astype(BF)
+
+    tiles(width, 256, out_gradient)
+    gather.finish()
+    fetch = pltpu.make_async_copy(x_hbm, x, copy_sems.at[1])
+    fetch.start()
 
     fetch.wait()
     for _ in gather_units.chunks():
@@ -1131,7 +1174,6 @@
     sent_sums[tall - rank :] = jnp.broadcast_to(slot[...], (rank, own_sums.shape[1])).astype(BF)
     enter(place, home=True, ring=False, trees=nf)
     moves = [Home(place, landed, home_send.at[0], home_recv.at[0])]
-    moves[0].start(rows_out)
     away = {}
     for i, (source, target) in enumerate(((sent_sums, all_sums), (own_units, all_units))):
         away[i] = TreeMove(place, source, target, home_send.at[i + 1], home_recv.at[i + 1])
@@ -1139,6 +1181,8 @@
     copies = []
     for i in range(2):
         away[i].land()
+        if i == 1:
+            moves[0].start(rows_out)
         slot_of = away[i].slot
         for e in range(1, nf):
             copies.append(
@@ -1207,6 +1251,25 @@
         return jobs[1][len(self.scatters)]
 
 
+class Pace:
+    def __init__(self, loads, stores):
+        self.loads, self.stores = loads, stores
+        for copy in loads:
+            copy.start()
+
+    def ready(self):
+        for copy in self.loads:
+            copy.wait()
+
+    def flush(self):
+        for copy in self.stores:
+            copy.start()
+
+    def end(self):
+        for copy in self.stores:
+            copy.wait()
+
+
 def call(kernel, collective, ins, outs, scratch, plan=None):
     spec = lambda hbm: pl.BlockSpec(memory_space=pl.ANY if hbm else pltpu.VMEM)
     aliases = {}
@@ -1214,12 +1277,35 @@
         first_in, count = len(ins), len(plan.scatters)
         aliases = {first_in + count + i: count + i for i in range(len(plan.spreads))}
         ins, outs, scratch = ins + plan.ins(), plan.outs() + outs, scratch + plan.semaphores()
+    late_in = [i for i, (_, hbm) in enumerate(ins) if hbm == "paced"]
+    late_out = [i for i, (_, _, hbm) in enumerate(outs) if hbm == "paced"]
+    extra = [pltpu.VMEM(ins[i][0].shape, ins[i][0].dtype) for i in late_in]
+    extra += [pltpu.VMEM(outs[i][0], outs[i][1]) for i in late_out]
+    if late_in or late_out:
+        extra.append(pltpu.SemaphoreType.DMA((len(late_in) + len(late_out),)))
+
+        def paced(*refs):
+            refs, held = list(refs[: -len(extra)]), refs[-len(extra) :]
+            loads, stores = [], []
+            for slot, i in enumerate(late_in):
+                loads.append(pltpu.make_async_copy(refs[i], held[slot], held[-1].at[slot]))
+                refs[i] = held[slot]
+            for slot, i in enumerate(late_out, len(late_in)):
+                stores.append(pltpu.make_async_copy(held[slot], refs[len(ins) + i], held[-1].at[slot]))
+                refs[len(ins) + i] = held[slot]
+            pace = Pace(loads, stores)
+            kernel(*refs, pace=pace)
+            pace.end()
+
+        body = paced
+    else:
+        body = kernel
     made = pl.pallas_call(
-        kernel,
+        body,
         out_shape=[jax.ShapeDtypeStruct(shape, kind) for shape, kind, _ in outs],
         in_specs=[spec(hbm) for _, hbm in ins],
         out_specs=[spec(hbm) for _, _, hbm in outs],
-        scratch_shapes=scratch,
+        scratch_shapes=scratch + extra,
         input_output_aliases=aliases,
         compiler_params=pltpu.CompilerParams(
             collective_id=collective, has_side_effects=True, vmem_limit_bytes=62 << 20
@@ -1342,7 +1428,7 @@
     calls = [0]
     whole_x = ((n, 2, rows, width), BF)
     sems = Gather.semaphores(n) + Reduce.scratch(n, rows, width)
-    pair = pltpu.SemaphoreType.DMA((3,))
+    pair = pltpu.SemaphoreType.DMA((4,))
     big = [vmem(*whole_x), vmem(*whole_x)]
 
     def run(kernel, ins, outs, scratch, plan=None):
@@ -1351,6 +1437,7 @@
 
     near = lambda *arrays: [(array, False) for array in arrays]
     far = lambda *arrays: [(array, True) for array in arrays]
+    paced = lambda *arrays: [(array, "paced") for array in arrays]
     out = lambda shape, kind, hbm=False: (shape, kind, hbm)
 
     dma = pltpu.SemaphoreType.DMA
@@ -1390,7 +1477,7 @@
         w_attention = w_a[l]
         lam = lax.dynamic_slice_in_dim(difference_lambda[l], head, 1).reshape(1, 1)
         gain_a, gain_f = gains[l, 0:1], gains[l, 1:2]
-        shared = (a_model[l], a_head[l], cosine, sine, query_bits, key_bits, lam)
+        shared = paced(a_model[l]) + near(a_head[l]) + paced(cosine, sine, query_bits) + near(key_bits, lam)
         plan = plan_of(
             [] if last else [(a_blocks[l + 1], (tall, c_a)), (g_blocks[l + 1], (tall, c_g))],
             [w_g[l], w_d[l]],
@@ -1400,19 +1487,19 @@
             moves("forward", 0, parts(n, 3, 4)) + ([] if last else [("scatter", 1)]),
         )
         got = run(
-            functools.partial(attention_forward, n, nf, l, part, rank, not last, plan),
-            near(residual, gain_a) + far(w_attention) + near(*shared),
+            functools.partial(attention_forward, n, nf, l, part, rank, True, plan),
+            near(residual, gain_a) + far(w_attention) + shared,
             [
                 out((rows, width), F32),
                 out(*whole_x, True),
-                out((tree, VD), BF),
-                out((tree, VD), BF),
-                out((tree, VD), BF),
-                out((tree, 3 * rank), BF),
-                out((tree, 2), F32),
-                out((tree, VD), BF),
-                out((tree, VD), BF),
-                out((tree, rank), BF),
+                out((tree, VD), BF, "paced"),
+                out((tree, VD), BF, "paced"),
+                out((tree, VD), BF, "paced"),
+                out((tree, 3 * rank), BF, "paced"),
+                out((tree, 2), F32, "paced"),
+                out((tree, VD), BF, "paced"),
+                out((tree, VD), BF, "paced"),
+                out((tree, rank), BF, "paced"),
             ],
             big + [vmem((width, 4 * VD), BF), vmem((3 * rank, 3 * VD), BF), pair] + sems,
             plan,
@@ -1433,25 +1520,28 @@
             [] if last else moves("forward", 1, parts(n, 2, 4)),
         )
         ffn = run(
-            functools.partial(ffn_forward, n, nf, units, rank, not last, plan),
-            near(middle, gain_f) + far(w_g[l]) + near(a_model[l], e_model[l]),
-            [
+            functools.partial(ffn_forward, n, nf, units, rank, last, plan),
+            near(middle, gain_f) + far(w_g[l]) + paced(a_model[l]) + near(e_model[l])
+            + (near(own_cotangent) if last else []),
+            ([out(*whole_x, True)] if last else [])
+            + [
                 out((rows, width), F32),
                 out(*whole_x, True),
-                out((tree, units), BF),
-                out((tree, units), BF),
-                out((tree, units), BF),
-                out((tree, 2 * rank), BF),
+                out((tree, units), BF, "paced"),
+                out((tree, units), BF, "paced"),
+                out((tree, units), BF, "paced"),
+                out((tree, 2 * rank), BF, "paced"),
                 out((tree, rank), BF),
             ],
-            big + [vmem((width, 3 * units), BF), vmem((2 * rank, 2 * units), BF), pair] + sems,
+            big + [vmem((width, 3 * units), BF), vmem((2 * rank, 2 * units), BF), pair] + sems
+            + ([vmem(*whole_x)] + Gather.semaphores(n) if last else []),
             plan,
         )
         if not last:
             w_d.append(ffn[0])
             w_d[l], w_a[l + 1], w_g[l + 1], *ffn = ffn[1:]
         else:
-            w_d[l], *ffn = ffn
+            w_d[l], gathered, *ffn = ffn
         saved.append((residual, middle, gain_a, gain_f, shared, kept, ffn[1:]))
         residual = ffn[0]
 
@@ -1462,8 +1552,9 @@
         carry = l == layers - 1
         made = run(
             functools.partial(ffn_backward, n, units, rank, carry),
-            near(grad, middle, gain_f) + far(w_g[l], w_d[l]) + near(a_model[l], e_model[l]) + far(ffn[0]) + near(*ffn[1:])
-            + (near(residual) if carry else []),
+            near(grad) + paced(middle) + near(gain_f) + far(w_g[l], w_d[l]) + paced(a_model[l]) + near(e_model[l])
+            + far(ffn[0]) + paced(*ffn[1:])
+            + (near(residual) + far(gathered) if carry else []),
             ([out((2, rows, width), BF)] if carry else [])
             + [
                 out((rows, width), F32),
@@ -1489,7 +1580,8 @@
         grad, *ffn_grads = made
         grad, own_sum, all_units = run(
             functools.partial(attention_backward, n, l, share, heads_tp, rank),
-            near(grad, residual_in, gain_a) + far(w_a[l]) + near(*shared) + far(kept[0]) + near(*kept[1:], *ffn_grads),
+            near(grad) + paced(residual_in) + near(gain_a) + far(w_a[l]) + shared + far(kept[0])
+            + paced(*kept[1:]) + near(*ffn_grads),
             [
                 out((rows, width), F32),
                 out((12 * rank, block), BF),

time: 865 us -> 829 us (0.958)
  Pallas kernels: 802 us -> 763 us
  waiting for transfers between devices: 0.02 us -> 10.7 us
    pallas_call x10, Pallas kernels: 802 us -> 763 us  [call(): pl.pallas_call(body, out_shape=[jax.ShapeDtypeStruct(shape, kind) for sha...]
    ppermute x6, waiting for transfers between devices: 0.02 us -> 10.7 us  [permute(): return lax.ppermute(x, ('fsdp', 'ctx'), pairs)]
  transfers between devices with their start and end apart: 6 -> 6, of which waited for: 0 -> 1; matrix products, arithmetic and copies ran while one was open for 2% -> 2% of each run, Pallas kernels for 54% -> 45%
where the time goes in v5:
time: 829 us; the launch traced here: 821 us
  Pallas kernels  763 us (92%)
  local copies, waits for them, and re-layouts  22.7 us (3%)
  starting transfers between devices  13.6 us (2%)
  waiting for transfers between devices  10.7 us (1%)
    pallas_call x10, Pallas kernels, call(): pl.pallas_call(body, out_shape=[jax.ShapeDtypeStruct(shape, kind) for sha...  763 us
  transfers between devices with their start and end apart: 6, of which 1 were waited for; matrix products, arithmetic and copies ran while one was open for 2% of the time, Pallas kernels for 45%

profile of v5, /device:TPU:3, one launch (start us, length us, event | category | flops | bytes accessed | tf_op | source)
XLA Modules:
  0.0 821.4 jit_solution(16758833934316145338)
XLA Ops:
  1.4 0.8 pad_add_fusion
  2.2 3.3 collective-permute-start.5
  5.5 0.3 collective-permute-start.4
  5.7 0.9 collective-permute-start.3
  6.6 3.3 collective-permute-start.2
  10.0 3.8 collective-permute-start
  14.0 0.8 fusion.6
  14.7 1.4 slice_bitcast_fusion.2
  16.2 1.9 constant_dynamic-slice_fusion.8
  18.0 0.7 constant_dynamic-slice_fusion.6.refs_9_.refs_10_
  18.7 0.6 constant_dynamic-slice_fusion.3.refs_9_.refs_10_
  19.2 80.6 %shard_map.165 = (bf16[2048,1024]{1,0:T(8,128)(2,1)}, bf16[2048,1536]{1,0:T(8,128)(2,1)}, bf16[2048,768]{1,0:T(8,128)(2,1)}, bf16[4,128,1024]{2,1,0:T(8,128)(2,1...) custom-call(bf16[2,3,128,1024]{3,2,1,0:T(8,128)(2,1)} %bitcast.64, bf16[2,128,1024]{2,1,0:T(8,128)(2,1)} %output.1, ...), custom_call_target="tpu_custom_call" | custom-call | tf_op jit(solution)/shard_map/pallas_call | solution.py:1303
  99.8 2.1 collective-permute-start.1
  102.1 0.6 slice.90
  104.6 1.1 dynamic-slice_bitcast_fusion.2
  105.8 0.2 select_reduce_fusion.1
  106.0 1.3 constant_dynamic-slice_fusion.5
  107.3 0.1 select_reduce_fusion
  107.4 1.9 fusion
  109.3 0.7 fusion.2
  110.0 0.6 pad_maximum_fusion.4
  111.3 0.6 copy.42
  111.9 1.0 copy.32.refs_7_.refs_8_
  112.9 1.0 pad_maximum_fusion.refs_5_.refs_6_
  114.0 1.0 pad_maximum_fusion.1.refs_6_.refs_7_
  115.0 2.6 constant_dynamic-slice_fusion.7
  117.6 10.6 %collective-permute-done.1.refs_0_.refs_1_ = bf16[128,2048]{1,0:T(8,128)(2,1)S(1)} collective-permute-done((bf16[128,2048]{1,0:T(8,128)(2,1)}, bf16[128,2048]{1,0:T(8,128)(2,1)S(1)}, u32[]{:S(2)}, u32[]{:S(2)}) %collective-permute-start.1) | collective-permute-done | bytes 524320 | tf_op jit(solution)/shard_map/ppermute | solution.py:1343
  128.2 0.8 copy-done.3
  129.0 98.1 %shard_map.166 = (bf16[2048,1024]{1,0:T(8,128)(2,1)}, bf16[2048,1536]{1,0:T(8,128)(2,1)}, bf16[2048,1536]{1,0:T(8,128)(2,1)}, bf16[2048,768]{1,0:T(8,128)(2,1)},...) custom-call(bf16[128,2048]{1,0:T(8,128)(2,1)} %copy-done.3, ...), custom_call_target="tpu_custom_call", output_to_operand_aliasing={{2}: (12, {}), {3}: (13, {})} | custom-call | tf_op jit(solution)/shard_map/pallas_call | solution.py:1303
  227.1 103.7 %shard_map.167 = (bf16[2048,768]{1,0:T(8,128)(2,1)}, bf16[2048,768]{1,0:T(8,128)(2,1)}, bf16[2048,1024]{1,0:T(8,128)(2,1)}, bf16[2048,1536]{1,0:T(8,128)(2,1)}, ...) custom-call(f32[128,2048]{1,0:T(8,128)} %get-tuple-element.79.refs_0, ...), custom_call_target="tpu_custom_call", output_to_operand_aliasing={{1}: (6, {}), {2}: (7, {}), {3}: (8, {})} | custom-call | tf_op jit(solution)/shard_map/pallas_call | solution.py:1303
  330.8 91.1 %shard_map.168 = (bf16[2048,1536]{1,0:T(8,128)(2,1)}, bf16[2048,768]{1,0:T(8,128)(2,1)}, f32[128,2048]{1,0:T(8,128)}, bf16[4,2,128,2048]{3,2,1,0:T(8,128)(2,1)},...) custom-call(f32[128,2048]{1,0:T(8,128)} %get-tuple-element.85.refs_0, ...), custom_call_target="tpu_custom_call", output_to_operand_aliasing={{0}: (10, {}), {1}: (11, {})} | custom-call | tf_op jit(solution)/shard_map/pallas_call | solution.py:1303
  421.9 0.8 copy-done.2
  422.7 87.2 %shard_map.169 = (bf16[2048,768]{1,0:T(8,128)(2,1)}, bf16[4,2,128,2048]{3,2,1,0:T(8,128)(2,1)}, f32[128,2048]{1,0:T(8,128)}, bf16[4,2,128,2048]{3,2,1,0:T(8,128)...) custom-call(f32[128,2048]{1,0:T(8,128)} %get-tuple-element.89.refs_0, ...), custom_call_target="tpu_custom_call", output_to_operand_aliasing={{0}: (6, {})} | custom-call | tf_op jit(solution)/shard_map/pallas_call | solution.py:1303
  509.9 51.0 %shard_map.170 = (bf16[2,128,2048]{2,1,0:T(8,128)(2,1)}, f32[128,2048]{1,0:T(8,128)}, bf16[16,2048]{1,0:T(8,128)(2,1)}, bf16[32,2048]{1,0:T(8,128)(2,1)}, bf16[64,768]{1,0:T(8,128)(2,1)}) custom-call(bf16[128,2048]{1,0:T(8,128)(2,1)} %copy-done.2, f32[128,2048]{1,0:T(8,128)} %get-tuple-element.89.refs_0_.refs_1_, ...), custom_call_target="tpu_custom_call" | custom-call | tf_op jit(solution)/shard_map/pallas_call | solution.py:1303
  560.8 73.4 %shard_map.171 = (f32[128,2048]{1,0:T(8,128)}, bf16[192,256]{1,0:T(8,128)(2,1)}, bf16[4,2,64,768]{3,2,1,0:T(8,128)(2,1)}) custom-call(f32[128,2048]{1,0:T(8,128)} %get-tuple-element.102.refs_0_, f32[128,2048]{1,0:T(8,128)} %get-tuple-element.85.refs_0_.refs_1_, f32[1,2048]{1,0:T(1,128)} %get-tuple-element.153.refs_1_.refs_2_, ...), custom_call_target="tpu_custom_call" | custom-call | tf_op jit(solution)/shard_map/pallas_call | solution.py:1303
  634.3 56.1 %shard_map.172 = (f32[128,2048]{1,0:T(8,128)}, bf16[16,2048]{1,0:T(8,128)(2,1)}, bf16[32,2048]{1,0:T(8,128)(2,1)}, bf16[64,768]{1,0:T(8,128)(2,1)}) custom-call(f32[128,2048]{1,0:T(8,128)} %get-tuple-element.115.refs_0_, f32[128,2048]{1,0:T(8,128)} %get-tuple-element.79.refs_0_.refs_1_, f32[1,2048]{1,0:T(1,128)} %get-tuple-element.151.refs_1_.refs_2_, ...), custom_call_target="tpu_custom_call" | custom-call | tf_op jit(solution)/shard_map/pallas_call | solution.py:1303
  690.4 73.9 %shard_map.173 = (f32[128,2048]{1,0:T(8,128)}, bf16[192,256]{1,0:T(8,128)(2,1)}, bf16[4,2,64,768]{3,2,1,0:T(8,128)(2,1)}) custom-call(f32[128,2048]{1,0:T(8,128)} %get-tuple-element.123.refs_0_, bf16[128,2048]{1,0:T(8,128)(2,1)} %copy-done.3, f32[1,2048]{1,0:T(1,128)} %get-tuple-element.152.refs_1_.refs_2_, ...), custom_call_target="tpu_custom_call" | custom-call | tf_op jit(solution)/shard_map/pallas_call | solution.py:1303
  764.4 1.1 dynamic-slice_bitcast_fusion.1
  765.4 1.0 dynamic-slice_bitcast_fusion
  766.6 0.1 constant_dynamic-slice_fusion.2
  766.7 0.1 constant_dynamic-slice_fusion.1
  766.8 0.7 pad_maximum_fusion.2.own_sums
  767.5 0.7 pad_maximum_fusion.3.own_units
  768.2 47.5 %shard_map.174 = (f32[256,2048]{1,0:T(8,128)}, f32[2,11,2,16,256]{4,3,2,1,0:T(8,128)}, f32[2,3,2,16,704]{4,3,2,1,0:T(8,128)}) custom-call(f32[128,2048]{1,0:T(8,128)} %get-tuple-element.136.grad, bf16[384,256]{1,0:T(8,128)(2,1)} %pad_maximum_fusion.2.own_sums, bf16[96,704]{1,0:T(8,128)(2,1)} %pad_maximum_fusion.3.own_units, f32[1,1]{1,0:T(1,128)} %bitcast.24.slot), custom_call_target="tpu_custom_call" | custom-call | tf_op jit(solution)/shard_map/pallas_call | solution.py:1303
  815.8 2.5 copy.56
  818.2 1.3 copy.57
  819.5 0.9 copy.58
  820.4 0.8 copy.59
  (38 shorter events, 0.4 us)
Async XLA Ops:
  0.6 9.3 %copy-start = (bf16[256,2048]{1,0:T(8,128)(2,1)S(1)}, bf16[256,2048]{1,0:T(8,128)(2,1)}, u32[]{:S(2)}) copy-start(bf16[256,2048]{1,0:T(8,128)(2,1)} %param.15) | copy-start | bytes 3145732
  2.2 97.7 %collective-permute-start.5 = (s32[526]{0:T(1024)S(1)}, s32[526]{0:T(1024)S(1)}, u32[]{:S(2)}, u32[]{:S(2)}) collective-permute-start(s32[526]{0:T(1024)S(1)} %pad_add_fusion), channel_id=1, source_target_pairs={{0,10},{2,8},{4,2},{6,0},{8,14},{10,12},{12,6},{14,4},{16,26},{18,... | collective-permute-start | bytes 6320 | tf_op jit(solution)/shard_map/ppermute | solution.py:1343
  5.5 96.5 %collective-permute-start.4 = (s32[526]{0:T(1024)S(1)}, s32[526]{0:T(1024)S(1)}, u32[]{:S(2)}, u32[]{:S(2)}) collective-permute-start(s32[526]{0:T(1024)S(1)} %pad_add_fusion), channel_id=1, source_target_pairs={{0,8},{2,10},{4,0},{6,2},{8,12},{10,14},{12,4},{14,6},{16,24},{18,... | collective-permute-start | bytes 6320 | tf_op jit(solution)/shard_map/ppermute | solution.py:1343
  5.7 96.2 %collective-permute-start.3 = (s32[526]{0:T(1024)S(1)}, s32[526]{0:T(1024)S(1)}, u32[]{:S(2)}, u32[]{:S(2)}) collective-permute-start(s32[526]{0:T(1024)S(1)} %pad_add_fusion), channel_id=1, source_target_pairs={{0,2},{2,0},{4,10},{6,8},{8,6},{10,4},{12,14},{14,12},{16,18},{18,... | collective-permute-start | bytes 6320 | tf_op jit(solution)/shard_map/ppermute | solution.py:1343
  6.6 95.4 %collective-permute-start.2 = (s32[526]{0:T(1024)S(1)}, s32[526]{0:T(1024)S(1)}, u32[]{:S(2)}, u32[]{:S(2)}) collective-permute-start(s32[526]{0:T(1024)S(1)} %pad_add_fusion), channel_id=1, source_target_pairs={{0,0},{2,2},{4,8},{6,10},{8,4},{10,6},{12,12},{14,14},{16,16},{18,... | collective-permute-start | bytes 6320 | tf_op jit(solution)/shard_map/ppermute | solution.py:1343
  10.0 411.9 %collective-permute-start = (bf16[128,2048]{1,0:T(8,128)(2,1)S(1)}, bf16[128,2048]{1,0:T(8,128)(2,1)S(1)}, u32[]{:S(2)}, u32[]{:S(2)}) collective-permute-start(bf16[128,2048]{1,0:T(8,128)(2,1)S(1)} %constant_dynamic-slice_fusion.9), channel_id=1, source_target_pairs={{0,0},{2,2},{4,8},{6,10},{8,4},{10,6},{12,12},{14,14},{16,16},{18,... | collective-permute-start | bytes 1572872 | tf_op jit(solution)/shard_map/ppermute | solution.py:1343
  99.8 28.4 %collective-permute-start.1 = (bf16[128,2048]{1,0:T(8,128)(2,1)}, bf16[128,2048]{1,0:T(8,128)(2,1)S(1)}, u32[]{:S(2)}, u32[]{:S(2)}) collective-permute-start(bf16[128,2048]{1,0:T(8,128)(2,1)} %constant_dynamic-slice_fusion.8), channel_id=1, source_target_pairs={{0,0},{2,2},{4,8},{6,10},{8,4},{10,6},{12,12},{14,14},{16,16},{18,... | collective-permute-start | bytes 1572872 | tf_op jit(solution)/shard_map/ppermute | solution.py:1343
  128.2 0.8 copy-start.3
  421.9 0.8 copy-start.2
  764.3 2.5 copy-start.7
  764.4 2.5 copy-start.8
  815.7 2.5 copy-start.4
  815.7 3.8 copy-start.5
  815.7 5.5 copy-start.1
  818.2 2.2 copy-start.6

commit v6 on v5

--- a/solution.py
+++ b/solution.py
@@ -842,11 +842,6 @@
     keep = pltpu.make_async_copy(x, x_hbm, copy_sems.at[1])
     keep.start()
 
-    if last:
-        for _ in next_gather.chunks():
-            pass
-        keep_next = pltpu.make_async_copy(next_x, next_hbm, copy_sems.at[2])
-        keep_next.start()
     work.complete(0)
     load = pltpu.make_async_copy(plan.late(jobs), w.at[:, pl.ds(2 * units, units)], copy_sems.at[0])
     load.start()
@@ -867,6 +862,10 @@
         reduce.offer(k)
         if k == reduce.order[2]:
             reduce.far()
+    if last:
+        coming = next_gather.chunks()
+        for _ in range(n - 1):
+            next(coming)
     work.at(3)
     for s in range(1, n // 2):
         reduce.near(s)
@@ -876,6 +875,11 @@
         following[at] = residual[at] + total
 
     reduce.end(use)
+    if last:
+        for _ in coming:
+            pass
+        keep_next = pltpu.make_async_copy(next_x, next_hbm, copy_sems.at[2])
+        keep_next.start()
     work.at(5)
     keep.wait()
     if last:
@@ -893,6 +897,9 @@
     if carry:
         final, gathered, final_out, *refs = refs
         *refs, final_rows, home_send, home_recv = refs
+    else:
+        sums, here, sums_out, here_out, *refs = refs
+        *refs, home_send, home_recv = refs
     (grad_out, grad_up_down, grad_in, grad_units,
      x, p, w, kept, dgu, dsmall, dside, raised, copy_sems, *sems) = refs
     place = Place(n)
@@ -903,7 +910,6 @@
     load_down = pltpu.make_async_copy(w_down_hbm, w.at[:, pl.ds(2 * units, units)], copy_sems.at[2])
     load_down.start()
     fetch = pltpu.make_async_copy(x_hbm, kept, copy_sems.at[1])
-    fetch.start()
     gather, reduce = Gather(place, x, *sems[:6]), Reduce(place, p, *sems[6:])
 
     if carry:
@@ -922,9 +928,13 @@
             final_rows[at] = final[at].astype(BF)
 
         by_rows(final.shape[0], last_rows)
-    enter(place, home=carry)
+    enter(place, home=True)
     if not carry:
         gather.begin()
+        going = [
+            TreeMove(place, source, target, home_send.at[i], home_recv.at[i])
+            for i, (source, target) in enumerate(((sums, sums_out), (here, here_out)))
+        ]
     else:
         home = Home(place, final_out, home_send, home_recv)
         home.start(final_rows)
@@ -935,6 +945,7 @@
 
     if carry:
         come.wait()
+    coming = [0] + [k for s in range(1, n // 2) for k in (-s, s)] + [n // 2]
     for q in list(reduce.chips.values()) if carry else gather.chunks():
         rows = pl.ds(pl.multiple_of(q * chip_rows, chip_rows), chip_rows)
         v = x[q].reshape(chip_rows, width)
@@ -962,9 +973,16 @@
         tiles(width, 512, out_tile)
         if carry:
             k = reduce.order[len(reduce.across)]
-            reduce.offer(k)
-            if k == reduce.order[2]:
-                reduce.far()
+        else:
+            k = coming.pop(0)
+        reduce.offer(k)
+        if k == (reduce.order[2] if carry else n // 2):
+            reduce.far()
+
+    fetch.start()
+    if not carry:
+        for move in going:
+            move.start()
 
     def use(at, total):
         inputs = middle[at]
@@ -990,13 +1008,16 @@
 
         tiles(units, step, unit_tile)
 
-    reduce.run(use, adapters, carry)
+    reduce.run(use, adapters, True)
     if not carry:
         gather.finish()
     reduce.finish()
     if carry:
         home.land()
         home.finish()
+    else:
+        for move in going:
+            move.land()
 
 
 def attention_backward(
@@ -1024,7 +1045,6 @@
     all_units[place.q, place.t] = grad_units[...]
     enter(place)
     gather.begin()
-    gather_units.begin()
     dk[...] = jnp.zeros(dk.shape, F32)
     dv[...] = jnp.zeros(dv.shape, F32)
     pace.ready()
@@ -1065,36 +1085,20 @@
 
         lax.fori_loop(0, chip_rows // ROW_BLOCK, block, 0)
 
-    def out_gradient(at):
-        flat = x[:, :, :, at].reshape(tree, at.size)
-        grad_a9[:, at] = (ADAPTER_SCALE * part * t_mm(side[...], flat)).astype(BF)
-
-    tiles(width, 256, out_gradient)
-    gather.finish()
-    fetch = pltpu.make_async_copy(x_hbm, x, copy_sems.at[1])
-    fetch.start()
-
-    fetch.wait()
-    for _ in gather_units.chunks():
-        pass
-
-    def project(i, carry):
-        rows = pl.ds(pl.multiple_of(i * chip_rows, chip_rows), chip_rows)
+    gather_units.begin()
+
+    def send_part(k):
+        q = reduce.chips[k]
+        rows = pl.ds(pl.multiple_of(q * chip_rows, chip_rows), chip_rows)
         for j, source in enumerate((dq, dk)):
             for c in range(2):
                 half = slice(c * HD, (c + 1) * HD)
                 turned = turn(source[rows, half] * score_scale, cosine[rows], -sine[rows])
                 dprojected[rows, j * VD + c * HD : j * VD + (c + 1) * HD] = turned.astype(BF)
         dprojected[rows, 2 * VD :] = dv[rows].astype(BF)
-        dsmall[rows] = (ADAPTER_SCALE * mm_t(dprojected[rows], raised[...])).astype(BF)
-        return carry
-
-    lax.fori_loop(0, n, project, 0)
-
-    def send_part(k):
-        q = reduce.chips[k]
-        rows = pl.ds(pl.multiple_of(q * chip_rows, chip_rows), chip_rows)
-        back, low_back = dprojected[rows], dsmall[rows]
+        back = dprojected[rows]
+        low_back = (ADAPTER_SCALE * mm_t(back, raised[...])).astype(BF)
+        dsmall[rows] = low_back
 
         def out_tile(at):
             made = mm_t(back, w[at, : 3 * VD]) + mm(low_back, a_model[: 3 * rank, at])
@@ -1106,6 +1110,20 @@
     for k in reduce.order[:3]:
         send_part(k)
     reduce.far()
+
+    def out_gradient(at):
+        flat = x[:, :, :, at].reshape(tree, at.size)
+        grad_a9[:, at] = (ADAPTER_SCALE * part * t_mm(side[...], flat)).astype(BF)
+
+    tiles(width, 256, out_gradient)
+    gather.finish()
+    fetch = pltpu.make_async_copy(x_hbm, x, copy_sems.at[1])
+    fetch.start()
+    for k in reduce.order[3:]:
+        send_part(k)
+    for _ in gather_units.chunks():
+        pass
+    fetch.wait()
 
     block = width // (2 * n)
 
@@ -1133,8 +1151,6 @@
             made = of_head[i][:, start : start + block] * own
             p_own[j // 2, j % 2, k * rank : (k + 1) * rank] = made.astype(BF)
 
-    for k in reduce.order[3:]:
-        send_part(k)
     for k in reduce.order:
         reduce_own.offer(k)
     reduce_own.far()
@@ -1158,10 +1174,11 @@
 
 def finish_kernel(
     n, nf, layers, rank,
-    grad, own_sums, own_units, slot,
-    tokens_grad, model_grad, hidden_grad,
-    rows_out, landed, sent_sums, all_sums, all_units, home_send, home_recv, tree_send, tree_recv,
+    grad, own_sums, own_units, slot, *refs,
 ):
+    earlier, refs = refs[: 2 * layers - 2], refs[2 * layers - 2 :]
+    (tokens_grad, model_grad, hidden_grad,
+     rows_out, landed, sent_sums, all_sums, all_units, home_send, home_recv, tree_send, tree_recv) = refs
     place = Place(n)
     own = model_grad.shape[2]
     tall = own_sums.shape[0]
@@ -1176,35 +1193,41 @@
     moves = [Home(place, landed, home_send.at[0], home_recv.at[0])]
     away = {}
     for i, (source, target) in enumerate(((sent_sums, all_sums), (own_units, all_units))):
-        away[i] = TreeMove(place, source, target, home_send.at[i + 1], home_recv.at[i + 1])
+        away[i] = TreeMove(place, source, target.at[:, 0], home_send.at[i + 1], home_recv.at[i + 1])
         away[i].start()
     copies = []
-    for i in range(2):
+
+    def hand_round(source, target, l, i):
+        to = target.at[place.f, l]
+        for e in range(1, nf):
+            sems = tree_send.at[l, i, e], tree_recv.at[l, i, e]
+            copies.append(remote(source, to, *sems, {"fsdp": flip(place.f, e)}))
+
+    for l in range(1, layers):
+        for i, target in enumerate((all_sums, all_units)):
+            source = earlier[2 * l - 2 + i].at[place.f]
+            target[place.f, l] = earlier[2 * l - 2 + i][place.f]
+            hand_round(source, target, l, i)
+    for i, target in enumerate((all_sums, all_units)):
         away[i].land()
         if i == 1:
             moves[0].start(rows_out)
-        slot_of = away[i].slot
-        for e in range(1, nf):
-            copies.append(
-                remote(slot_of, slot_of, tree_send.at[i, e], tree_recv.at[i, e], {"fsdp": flip(place.f, e)})
-            )
+        hand_round(target.at[place.f, 0], target, 0, i)
     moves[0].land()
     for copy in copies:
         copy.wait_recv()
-    block, units = all_sums.shape[2], all_units.shape[2]
-    per_layer = tall // layers
     for b in range(own):
         number = (place.f * own + b).astype(F32)
         keeps = [
-            (all_sums[f, tall - rank : tall - rank + 1, :1].astype(F32) == number).astype(F32) for f in range(nf)
+            (all_sums[f, 0, tall - rank : tall - rank + 1, :1].astype(F32) == number).astype(F32) for f in range(nf)
         ]
         for l in range(layers):
             for k in range(11):
-                at = slice(l * per_layer + k * rank, l * per_layer + (k + 1) * rank)
-                model_grad[l, k, b] = sum(keeps[f] * all_sums[f, at].astype(F32) for f in range(nf))
+                at = slice(k * rank, (k + 1) * rank)
+                model_grad[l, k, b] = sum(keeps[f] * all_sums[f, l, at].astype(F32) for f in range(nf))
             for k in range(3):
-                at = slice((l * 3 + k) * rank, (l * 3 + k + 1) * rank)
-                hidden_grad[l, k, b] = sum(keeps[f] * all_units[f, at].astype(F32) for f in range(nf))
+                at = slice(k * rank, (k + 1) * rank)
+                hidden_grad[l, k, b] = sum(keeps[f] * all_units[f, l, at].astype(F32) for f in range(nf))
     moves[0].finish()
     for core in range(2):
 
@@ -1546,7 +1569,8 @@
         residual = ffn[0]
 
     grad = own_cotangent
-    units_here, sums_here, block = [], [], width // (2 * n)
+    units_here, sums_here, earlier, block = [], [], [], width // (2 * n)
+    wide = hidden_tp // n
     for l in reversed(range(layers)):
         residual_in, middle, gain_a, gain_f, shared, kept, ffn = saved[l]
         carry = l == layers - 1
@@ -1554,8 +1578,8 @@
             functools.partial(ffn_backward, n, units, rank, carry),
             near(grad) + paced(middle) + near(gain_f) + far(w_g[l], w_d[l]) + paced(a_model[l]) + near(e_model[l])
             + far(ffn[0]) + paced(*ffn[1:])
-            + (near(residual) + far(gathered) if carry else []),
-            ([out((2, rows, width), BF)] if carry else [])
+            + (near(residual) + far(gathered) if carry else near(sums_here[0], units_here[0])),
+            ([out((2, rows, width), BF)] if carry else [out((nf, 12 * rank, block), BF), out((nf, 3 * rank, wide), BF)])
             + [
                 out((rows, width), F32),
                 out((rank, width), BF),
@@ -1573,10 +1597,13 @@
                 pair,
             ]
             + sems
-            + ([vmem((rows, width), BF)] + Home.semaphores() if carry else []),
+            + ([vmem((rows, width), BF)] + Home.semaphores() if carry else [dma((2, 2)), dma((2, 2))]),
         )
         if carry:
             outputs, *made = made
+        else:
+            earlier += made[:2]
+            made = made[2:]
         grad, *ffn_grads = made
         grad, own_sum, all_units = run(
             functools.partial(attention_backward, n, l, share, heads_tp, rank),
@@ -1615,10 +1642,9 @@
 
     own = adapters // nf
     dma = pltpu.SemaphoreType.DMA
-    wide = hidden_tp // n
     tokens_grad, grad_model, grad_hidden = run(
         functools.partial(finish_kernel, n, nf, layers, rank),
-        near(grad, jnp.concatenate(sums_here), jnp.concatenate(units_here), slot.astype(F32).reshape(1, 1)),
+        near(grad, sums_here[0], units_here[0], slot.astype(F32).reshape(1, 1), *earlier),
         [
             out((2 * rows, width), F32),
             out((layers, 11, own, rank, block), F32),
@@ -1627,13 +1653,13 @@
         [
             vmem((rows, width), BF),
             vmem((2, rows, width), BF),
-            vmem((layers * 12 * rank, block), BF),
-            vmem((nf, layers * 12 * rank, block), BF),
-            vmem((nf, layers * 3 * rank, wide), BF),
+            vmem((12 * rank, block), BF),
+            vmem((nf, layers, 12 * rank, block), BF),
+            vmem((nf, layers, 3 * rank, wide), BF),
             dma((3, 2)),
             dma((3, 2)),
-            dma((2, nf)),
-            dma((2, nf)),
+            dma((layers, 2, nf)),
+            dma((layers, 2, nf)),
         ],
     )
     return (

time: 829 us -> 816 us (0.984)
  Pallas kernels: 763 us -> 750 us
    pallas_call x10, Pallas kernels: 763 us -> 750 us  [call(): pl.pallas_call(body, out_shape=[jax.ShapeDtypeStruct(shape, kind) for sha...]
  transfers between devices with their start and end apart: 6 -> 6, of which waited for: 1 -> 1; matrix products, arithmetic and copies ran while one was open for 2% -> 2% of each run, Pallas kernels for 45% -> 46%
where the time goes in v6:
time: 816 us; the launch traced here: 808 us
  Pallas kernels  750 us (92%)
  local copies, waits for them, and re-layouts  24 us (3%)
  starting transfers between devices  13.9 us (2%)
  waiting for transfers between devices  10.4 us (1%)
    pallas_call x10, Pallas kernels, call(): pl.pallas_call(body, out_shape=[jax.ShapeDtypeStruct(shape, kind) for sha...  750 us
  transfers between devices with their start and end apart: 6, of which 1 were waited for; matrix products, arithmetic and copies ran while one was open for 2% of the time, Pallas kernels for 46%

profile of v6, /device:TPU:3, one launch (start us, length us, event | category | flops | bytes accessed | tf_op | source)
XLA Modules:
  0.0 808.3 jit_solution(13180416954738401637)
XLA Ops:
  0.6 0.0 copy-start
  1.4 0.8 pad_add_fusion
  2.2 3.3 collective-permute-start.5
  5.5 0.3 collective-permute-start.4
  5.7 0.9 collective-permute-start.3
  6.6 3.3 collective-permute-start.2
  10.0 3.8 collective-permute-start
  14.0 0.8 fusion.6
  14.7 1.4 slice_bitcast_fusion.2
  16.1 1.9 constant_dynamic-slice_fusion.8
  18.0 0.7 constant_dynamic-slice_fusion.6.refs_9_.refs_10_
  18.7 0.6 constant_dynamic-slice_fusion.3.refs_9_.refs_10_
  19.3 80.6 %shard_map.165 = (bf16[2048,1024]{1,0:T(8,128)(2,1)}, bf16[2048,1536]{1,0:T(8,128)(2,1)}, bf16[2048,768]{1,0:T(8,128)(2,1)}, bf16[4,128,1024]{2,1,0:T(8,128)(2,1...) custom-call(bf16[2,3,128,1024]{3,2,1,0:T(8,128)(2,1)} %bitcast.64, bf16[2,128,1024]{2,1,0:T(8,128)(2,1)} %output.1, ...), custom_call_target="tpu_custom_call" | custom-call | tf_op jit(solution)/shard_map/pallas_call | solution.py:1326
  99.9 2.4 collective-permute-start.1
  102.4 0.1 select_add_fusion
  102.4 0.6 slice.90
  105.0 1.1 dynamic-slice_bitcast_fusion.2
  106.1 0.2 select_reduce_fusion.1
  106.3 1.3 constant_dynamic-slice_fusion.5
  107.6 0.1 select_reduce_fusion
  107.8 1.9 fusion
  109.7 0.7 fusion.2
  110.4 0.6 pad_maximum_fusion.2
  111.6 0.6 copy.42
  112.2 1.0 copy.32.refs_7_.refs_8_
  113.3 1.0 pad_maximum_fusion.refs_5_.refs_6_
  114.3 1.0 pad_maximum_fusion.1.refs_6_.refs_7_
  115.3 2.6 constant_dynamic-slice_fusion.7
  117.9 10.3 %collective-permute-done.1.refs_0_.refs_1_ = bf16[128,2048]{1,0:T(8,128)(2,1)S(1)} collective-permute-done((bf16[128,2048]{1,0:T(8,128)(2,1)}, bf16[128,2048]{1,0:T(8,128)(2,1)S(1)}, u32[]{:S(2)}, u32[]{:S(2)}) %collective-permute-start.1) | collective-permute-done | bytes 524320 | tf_op jit(solution)/shard_map/ppermute | solution.py:1366
  128.2 0.8 copy-done.3
  129.0 98.0 %shard_map.166 = (bf16[2048,1024]{1,0:T(8,128)(2,1)}, bf16[2048,1536]{1,0:T(8,128)(2,1)}, bf16[2048,1536]{1,0:T(8,128)(2,1)}, bf16[2048,768]{1,0:T(8,128)(2,1)},...) custom-call(bf16[128,2048]{1,0:T(8,128)(2,1)} %copy-done.3, ...), custom_call_target="tpu_custom_call", output_to_operand_aliasing={{2}: (12, {}), {3}: (13, {})} | custom-call | tf_op jit(solution)/shard_map/pallas_call | solution.py:1326
  227.1 104.1 %shard_map.167 = (bf16[2048,768]{1,0:T(8,128)(2,1)}, bf16[2048,768]{1,0:T(8,128)(2,1)}, bf16[2048,1024]{1,0:T(8,128)(2,1)}, bf16[2048,1536]{1,0:T(8,128)(2,1)}, ...) custom-call(f32[128,2048]{1,0:T(8,128)} %get-tuple-element.81.refs_0, ...), custom_call_target="tpu_custom_call", output_to_operand_aliasing={{1}: (6, {}), {2}: (7, {}), {3}: (8, {})} | custom-call | tf_op jit(solution)/shard_map/pallas_call | solution.py:1326
  331.1 90.5 %shard_map.168 = (bf16[2048,1536]{1,0:T(8,128)(2,1)}, bf16[2048,768]{1,0:T(8,128)(2,1)}, f32[128,2048]{1,0:T(8,128)}, bf16[4,2,128,2048]{3,2,1,0:T(8,128)(2,1)},...) custom-call(f32[128,2048]{1,0:T(8,128)} %get-tuple-element.87.refs_0, ...), custom_call_target="tpu_custom_call", output_to_operand_aliasing={{0}: (10, {}), {1}: (11, {})} | custom-call | tf_op jit(solution)/shard_map/pallas_call | solution.py:1326
  421.7 0.8 copy-done.2
  422.5 83.4 %shard_map.169 = (bf16[2048,768]{1,0:T(8,128)(2,1)}, bf16[4,2,128,2048]{3,2,1,0:T(8,128)(2,1)}, f32[128,2048]{1,0:T(8,128)}, bf16[4,2,128,2048]{3,2,1,0:T(8,128)...) custom-call(f32[128,2048]{1,0:T(8,128)} %get-tuple-element.91.refs_0, ...), custom_call_target="tpu_custom_call", output_to_operand_aliasing={{0}: (6, {})} | custom-call | tf_op jit(solution)/shard_map/pallas_call | solution.py:1326
  505.9 50.1 %shard_map.170 = (bf16[2,128,2048]{2,1,0:T(8,128)(2,1)}, f32[128,2048]{1,0:T(8,128)}, bf16[16,2048]{1,0:T(8,128)(2,1)}, bf16[32,2048]{1,0:T(8,128)(2,1)}, bf16[64,768]{1,0:T(8,128)(2,1)}) custom-call(bf16[128,2048]{1,0:T(8,128)(2,1)} %copy-done.2, f32[128,2048]{1,0:T(8,128)} %get-tuple-element.91.refs_0_.refs_1_, ...), custom_call_target="tpu_custom_call" | custom-call | tf_op jit(solution)/shard_map/pallas_call | solution.py:1326
  556.0 69.2 %shard_map.171 = (f32[128,2048]{1,0:T(8,128)}, bf16[192,256]{1,0:T(8,128)(2,1)}, bf16[4,2,64,768]{3,2,1,0:T(8,128)(2,1)}) custom-call(f32[128,2048]{1,0:T(8,128)} %get-tuple-element.104.refs_0_, f32[128,2048]{1,0:T(8,128)} %get-tuple-element.87.refs_0_.refs_1_, f32[1,2048]{1,0:T(1,128)} %get-tuple-element.157.refs_1_.refs_2_, ...), custom_call_target="tpu_custom_call" | custom-call | tf_op jit(solution)/shard_map/pallas_call | solution.py:1326
  625.2 1.0 dynamic-slice_bitcast_fusion.1
  626.3 0.7 constant_dynamic-slice_fusion.2.refs_14_
  627.0 63.6 %shard_map.172 = (bf16[4,192,256]{2,1,0:T(8,128)(2,1)}, bf16[4,48,704]{2,1,0:T(8,128)(2,1)}, f32[128,2048]{1,0:T(8,128)}, bf16[16,2048]{1,0:T(8,128)(2,1)}, bf16...) custom-call(f32[128,2048]{1,0:T(8,128)} %get-tuple-element.117.refs_0_, f32[128,2048]{1,0:T(8,128)} %get-tuple-element.81.refs_0_.refs_1_, ...), custom_call_target="tpu_custom_call" | custom-call | tf_op jit(solution)/shard_map/pallas_call | solution.py:1326
  690.6 69.2 %shard_map.173 = (f32[128,2048]{1,0:T(8,128)}, bf16[192,256]{1,0:T(8,128)(2,1)}, bf16[4,2,64,768]{3,2,1,0:T(8,128)(2,1)}) custom-call(f32[128,2048]{1,0:T(8,128)} %get-tuple-element.127.refs_0_, bf16[128,2048]{1,0:T(8,128)(2,1)} %copy-done.3, f32[1,2048]{1,0:T(1,128)} %get-tuple-element.156.refs_1_.refs_2_, ...), custom_call_target="tpu_custom_call" | custom-call | tf_op jit(solution)/shard_map/pallas_call | solution.py:1326
  759.9 1.0 dynamic-slice_bitcast_fusion
  761.0 0.7 constant_dynamic-slice_fusion.1.own_units
  761.7 40.9 %shard_map.174 = (f32[256,2048]{1,0:T(8,128)}, f32[2,11,2,16,256]{4,3,2,1,0:T(8,128)}, f32[2,3,2,16,704]{4,3,2,1,0:T(8,128)}) custom-call(f32[128,2048]{1,0:T(8,128)} %get-tuple-element.140.grad, bf16[192,256]{1,0:T(8,128)(2,1)} %get-tuple-element.141.own_sums, bf16[48,704]{1,0:T(8,128)(2,1)} %constant_dynamic-slice_fusion.1.own_units, ...), custom_call_target="tpu_custom_call" | custom-call | tf_op jit(solution)/shard_map/pallas_call | solution.py:1326
  802.6 2.5 copy.56
  805.1 1.3 copy.57
  806.4 0.9 copy.58
  807.3 0.8 copy.59
  (32 shorter events, 0.3 us)
Async XLA Ops:
  0.6 9.3 %copy-start = (bf16[256,2048]{1,0:T(8,128)(2,1)S(1)}, bf16[256,2048]{1,0:T(8,128)(2,1)}, u32[]{:S(2)}) copy-start(bf16[256,2048]{1,0:T(8,128)(2,1)} %param.15) | copy-start | bytes 3145732
  2.2 97.8 %collective-permute-start.5 = (s32[526]{0:T(1024)S(1)}, s32[526]{0:T(1024)S(1)}, u32[]{:S(2)}, u32[]{:S(2)}) collective-permute-start(s32[526]{0:T(1024)S(1)} %pad_add_fusion), channel_id=1, source_target_pairs={{0,10},{2,8},{4,2},{6,0},{8,14},{10,12},{12,6},{14,4},{16,26},{18,... | collective-permute-start | bytes 6320 | tf_op jit(solution)/shard_map/ppermute | solution.py:1366
  5.5 96.8 %collective-permute-start.4 = (s32[526]{0:T(1024)S(1)}, s32[526]{0:T(1024)S(1)}, u32[]{:S(2)}, u32[]{:S(2)}) collective-permute-start(s32[526]{0:T(1024)S(1)} %pad_add_fusion), channel_id=1, source_target_pairs={{0,8},{2,10},{4,0},{6,2},{8,12},{10,14},{12,4},{14,6},{16,24},{18,... | collective-permute-start | bytes 6320 | tf_op jit(solution)/shard_map/ppermute | solution.py:1366
  5.7 96.6 %collective-permute-start.3 = (s32[526]{0:T(1024)S(1)}, s32[526]{0:T(1024)S(1)}, u32[]{:S(2)}, u32[]{:S(2)}) collective-permute-start(s32[526]{0:T(1024)S(1)} %pad_add_fusion), channel_id=1, source_target_pairs={{0,2},{2,0},{4,10},{6,8},{8,6},{10,4},{12,14},{14,12},{16,18},{18,... | collective-permute-start | bytes 6320 | tf_op jit(solution)/shard_map/ppermute | solution.py:1366
  6.6 95.7 %collective-permute-start.2 = (s32[526]{0:T(1024)S(1)}, s32[526]{0:T(1024)S(1)}, u32[]{:S(2)}, u32[]{:S(2)}) collective-permute-start(s32[526]{0:T(1024)S(1)} %pad_add_fusion), channel_id=1, source_target_pairs={{0,0},{2,2},{4,8},{6,10},{8,4},{10,6},{12,12},{14,14},{16,16},{18,... | collective-permute-start | bytes 6320 | tf_op jit(solution)/shard_map/ppermute | solution.py:1366
  10.0 411.7 %collective-permute-start = (bf16[128,2048]{1,0:T(8,128)(2,1)S(1)}, bf16[128,2048]{1,0:T(8,128)(2,1)S(1)}, u32[]{:S(2)}, u32[]{:S(2)}) collective-permute-start(bf16[128,2048]{1,0:T(8,128)(2,1)S(1)} %constant_dynamic-slice_fusion.9), channel_id=1, source_target_pairs={{0,0},{2,2},{4,8},{6,10},{8,4},{10,6},{12,12},{14,14},{16,16},{18,... | collective-permute-start | bytes 1572872 | tf_op jit(solution)/shard_map/ppermute | solution.py:1366
  99.9 28.3 %collective-permute-start.1 = (bf16[128,2048]{1,0:T(8,128)(2,1)}, bf16[128,2048]{1,0:T(8,128)(2,1)S(1)}, u32[]{:S(2)}, u32[]{:S(2)}) collective-permute-start(bf16[128,2048]{1,0:T(8,128)(2,1)} %constant_dynamic-slice_fusion.8), channel_id=1, source_target_pairs={{0,0},{2,2},{4,8},{6,10},{8,4},{10,6},{12,12},{14,14},{16,16},{18,... | collective-permute-start | bytes 1572872 | tf_op jit(solution)/shard_map/ppermute | solution.py:1366
  128.2 0.8 copy-start.3
  421.7 0.8 copy-start.2
  802.6 2.5 copy-start.4
  802.6 3.8 copy-start.5
  802.6 5.5 copy-start.1
  805.1 2.2 copy-start.6

commit v7 on v6

--- a/solution.py
+++ b/solution.py
@@ -530,23 +530,30 @@
         self._add(half, 0)
         self._add(half, 1)
         if self.lean:
+
+            def body(even):
+                for piece in range(2):
+                    self._copy(-1 if even else 1, 0, piece).start()
+
+            when_even(self.place, body)
+        else:
+            self._copy(1, 0, 0).start()
+            self._copy(-1, 0, 1).start()
+
+    def free(self):
+        k = self.place.n // 2 - 1
+        if self.lean:
             self.across[1].wait_recv()
             self.across[-1].wait_recv()
 
             def body(even):
                 sign = -1 if even else 1
                 for piece in range(2):
-                    self._copy(sign, 0, piece).start()
-                for piece in range(2):
                     self._add(sign, piece)
                     self._copy(sign, 1, piece).start()
 
             when_even(self.place, body)
-            return
-        self._copy(1, 0, 0).start()
-        self._copy(-1, 0, 1).start()
-        if half > 1:
-            k = half - 1
+        elif k:
             for sign, piece in ((1, 1), (-1, 0)):
                 self.across[sign * k].wait_recv()
                 self._add(sign * k, piece)
@@ -611,6 +618,7 @@
             for k in self.order:
                 self.offer(k)
             self.far()
+            self.free()
         for s in range(1, self.place.n // 2):
             self.near(s)
         if before is not None:
@@ -769,8 +777,10 @@
 
         tiles(width, 512, out_tile)
         reduce.offer(k)
+        if k == reduce.order[0]:
+            reduce.far()
         if k == reduce.order[2]:
-            reduce.far()
+            reduce.free()
     work.at(3)
     for s in range(1, n // 2):
         reduce.near(s)
@@ -860,8 +870,10 @@
 
         tiles(width, 512, out_tile)
         reduce.offer(k)
+        if k == reduce.order[0]:
+            reduce.far()
         if k == reduce.order[2]:
-            reduce.far()
+            reduce.free()
     if last:
         coming = next_gather.chunks()
         for _ in range(n - 1):
@@ -976,8 +988,10 @@
         else:
             k = coming.pop(0)
         reduce.offer(k)
+        if k == n // 2:
+            reduce.far()
         if k == (reduce.order[2] if carry else n // 2):
-            reduce.far()
+            reduce.free()
 
     fetch.start()
     if not carry:
@@ -1109,7 +1123,9 @@
 
     for k in reduce.order[:3]:
         send_part(k)
-    reduce.far()
+        if k == n // 2:
+            reduce.far()
+    reduce.free()
 
     def out_gradient(at):
         flat = x[:, :, :, at].reshape(tree, at.size)
@@ -1154,6 +1170,7 @@
     for k in reduce.order:
         reduce_own.offer(k)
     reduce_own.far()
+    reduce_own.free()
     for s in range(1, n // 2):
         reduce.near(s)
         reduce_own.near(s)
@@ -1501,11 +1518,12 @@
         lam = lax.dynamic_slice_in_dim(difference_lambda[l], head, 1).reshape(1, 1)
         gain_a, gain_f = gains[l, 0:1], gains[l, 1:2]
         shared = paced(a_model[l]) + near(a_head[l]) + paced(cosine, sine, query_bits) + near(key_bits, lam)
+        come = 2 if l else 1
         plan = plan_of(
             [] if last else [(a_blocks[l + 1], (tall, c_a)), (g_blocks[l + 1], (tall, c_g))],
             [w_g[l], w_d[l]],
-            moves("forward", 0, parts(n, 0, 1)) + moves("spread", 0, parts(n, 1, 4)),
-            moves("forward", 0, parts(n, 1, 2)) + ([] if last else [("scatter", 0)]),
+            moves("forward", 0, parts(n, 0, come)) + moves("spread", 0, parts(n, come, 4)),
+            moves("forward", 0, parts(n, come, 2)) + ([] if last else [("scatter", 0)]),
             moves("spread", 1, parts(n, 0, 2)) + moves("forward", 0, parts(n, 2, 3)),
             moves("forward", 0, parts(n, 3, 4)) + ([] if last else [("scatter", 1)]),
         )
@@ -1539,7 +1557,7 @@
             moves("forward", 0, parts(n, 2, 3)),
             moves("forward", 0, parts(n, 3, 4)) + ([] if last else moves("spread", 1, parts(n, 0, 4)) + [("scatter", 0)]),
             [] if last else moves("forward", 1, parts(n, 0, 1)),
-            [] if last else moves("forward", 1, parts(n, 1, 2)) + moves("spread", 2, parts(n, 0, 1)),
+            [] if last else moves("forward", 1, parts(n, 1, 2)) + moves("spread", 2, parts(n, 0, 2)),
             [] if last else moves("forward", 1, parts(n, 2, 4)),
         )
         ffn = run(

time: 816 us -> 808 us (level)
  no operation moved by 1% of the time
where the time goes in v7:
time: 808 us; the launch traced here: 801 us
  Pallas kernels  742 us (92%)
  local copies, waits for them, and re-layouts  24 us (3%)
  starting transfers between devices  13.6 us (2%)
  waiting for transfers between devices  10.6 us (1%)
    pallas_call x10, Pallas kernels, call(): pl.pallas_call(body, out_shape=[jax.ShapeDtypeStruct(shape, kind) for sha...  742 us
  transfers between devices with their start and end apart: 6, of which 1 were waited for; matrix products, arithmetic and copies ran while one was open for 2% of the time, Pallas kernels for 46%

profile of v7, /device:TPU:3, one launch (start us, length us, event | category | flops | bytes accessed | tf_op | source)
XLA Modules:
  0.0 800.5 jit_solution(12317473212987673185)
XLA Ops:
  0.6 0.0 copy-start
  1.4 0.8 pad_add_fusion
  2.2 3.3 collective-permute-start.5
  5.5 0.3 collective-permute-start.4
  5.7 0.9 collective-permute-start.3
  6.6 3.3 collective-permute-start.2
  10.0 3.8 collective-permute-start
  14.0 0.8 fusion.6
  14.7 1.4 slice_bitcast_fusion.2
  16.1 1.9 constant_dynamic-slice_fusion.8
  18.0 0.7 constant_dynamic-slice_fusion.6.refs_9_.refs_10_
  18.7 0.6 constant_dynamic-slice_fusion.3.refs_9_.refs_10_
  19.3 80.6 %shard_map.165 = (bf16[2048,1024]{1,0:T(8,128)(2,1)}, bf16[2048,1536]{1,0:T(8,128)(2,1)}, bf16[2048,768]{1,0:T(8,128)(2,1)}, bf16[4,128,1024]{2,1,0:T(8,128)(2,1...) custom-call(bf16[2,3,128,1024]{3,2,1,0:T(8,128)(2,1)} %bitcast.64, bf16[2,128,1024]{2,1,0:T(8,128)(2,1)} %output.1, ...), custom_call_target="tpu_custom_call" | custom-call | tf_op jit(solution)/shard_map/pallas_call | solution.py:1343
  99.9 2.1 collective-permute-start.1
  102.1 0.1 select_add_fusion
  102.2 0.6 slice.90
  104.7 1.1 dynamic-slice_bitcast_fusion.2
  105.8 0.2 select_reduce_fusion.1
  106.0 1.3 constant_dynamic-slice_fusion.5
  107.3 0.1 select_reduce_fusion
  107.5 1.9 fusion
  109.4 0.7 fusion.2
  110.1 0.6 pad_maximum_fusion.2
  111.4 0.6 copy.42
  112.0 1.0 copy.32.refs_7_.refs_8_
  113.0 1.0 pad_maximum_fusion.refs_5_.refs_6_
  114.0 1.0 pad_maximum_fusion.1.refs_6_.refs_7_
  115.0 2.6 constant_dynamic-slice_fusion.7
  117.6 10.6 %collective-permute-done.1.refs_0_.refs_1_ = bf16[128,2048]{1,0:T(8,128)(2,1)S(1)} collective-permute-done((bf16[128,2048]{1,0:T(8,128)(2,1)}, bf16[128,2048]{1,0:T(8,128)(2,1)S(1)}, u32[]{:S(2)}, u32[]{:S(2)}) %collective-permute-start.1) | collective-permute-done | bytes 524320 | tf_op jit(solution)/shard_map/ppermute | solution.py:1383
  128.2 0.8 copy-done.3
  129.0 98.0 %shard_map.166 = (bf16[2048,1024]{1,0:T(8,128)(2,1)}, bf16[2048,1536]{1,0:T(8,128)(2,1)}, bf16[2048,1536]{1,0:T(8,128)(2,1)}, bf16[2048,768]{1,0:T(8,128)(2,1)},...) custom-call(bf16[128,2048]{1,0:T(8,128)(2,1)} %copy-done.3, ...), custom_call_target="tpu_custom_call", output_to_operand_aliasing={{2}: (12, {}), {3}: (13, {})} | custom-call | tf_op jit(solution)/shard_map/pallas_call | solution.py:1343
  227.1 114.6 %shard_map.167 = (bf16[2048,768]{1,0:T(8,128)(2,1)}, bf16[2048,768]{1,0:T(8,128)(2,1)}, bf16[2048,1024]{1,0:T(8,128)(2,1)}, bf16[2048,1536]{1,0:T(8,128)(2,1)}, ...) custom-call(f32[128,2048]{1,0:T(8,128)} %get-tuple-element.81.refs_0, ...), custom_call_target="tpu_custom_call", output_to_operand_aliasing={{1}: (6, {}), {2}: (7, {}), {3}: (8, {})} | custom-call | tf_op jit(solution)/shard_map/pallas_call | solution.py:1343
  341.7 77.2 %shard_map.168 = (bf16[2048,1536]{1,0:T(8,128)(2,1)}, bf16[2048,768]{1,0:T(8,128)(2,1)}, f32[128,2048]{1,0:T(8,128)}, bf16[4,2,128,2048]{3,2,1,0:T(8,128)(2,1)},...) custom-call(f32[128,2048]{1,0:T(8,128)} %get-tuple-element.87.refs_0, ...), custom_call_target="tpu_custom_call", output_to_operand_aliasing={{0}: (10, {}), {1}: (11, {})} | custom-call | tf_op jit(solution)/shard_map/pallas_call | solution.py:1343
  418.9 0.8 copy-done.2
  419.7 80.9 %shard_map.169 = (bf16[2048,768]{1,0:T(8,128)(2,1)}, bf16[4,2,128,2048]{3,2,1,0:T(8,128)(2,1)}, f32[128,2048]{1,0:T(8,128)}, bf16[4,2,128,2048]{3,2,1,0:T(8,128)...) custom-call(f32[128,2048]{1,0:T(8,128)} %get-tuple-element.91.refs_0, ...), custom_call_target="tpu_custom_call", output_to_operand_aliasing={{0}: (6, {})} | custom-call | tf_op jit(solution)/shard_map/pallas_call | solution.py:1343
  500.6 48.9 %shard_map.170 = (bf16[2,128,2048]{2,1,0:T(8,128)(2,1)}, f32[128,2048]{1,0:T(8,128)}, bf16[16,2048]{1,0:T(8,128)(2,1)}, bf16[32,2048]{1,0:T(8,128)(2,1)}, bf16[64,768]{1,0:T(8,128)(2,1)}) custom-call(bf16[128,2048]{1,0:T(8,128)(2,1)} %copy-done.2, f32[128,2048]{1,0:T(8,128)} %get-tuple-element.91.refs_0_.refs_1_, ...), custom_call_target="tpu_custom_call" | custom-call | tf_op jit(solution)/shard_map/pallas_call | solution.py:1343
  549.6 69.5 %shard_map.171 = (f32[128,2048]{1,0:T(8,128)}, bf16[192,256]{1,0:T(8,128)(2,1)}, bf16[4,2,64,768]{3,2,1,0:T(8,128)(2,1)}) custom-call(f32[128,2048]{1,0:T(8,128)} %get-tuple-element.104.refs_0_, f32[128,2048]{1,0:T(8,128)} %get-tuple-element.87.refs_0_.refs_1_, f32[1,2048]{1,0:T(1,128)} %get-tuple-element.157.refs_1_.refs_2_, ...), custom_call_target="tpu_custom_call" | custom-call | tf_op jit(solution)/shard_map/pallas_call | solution.py:1343
  619.1 1.0 dynamic-slice_bitcast_fusion.1
  620.2 0.7 constant_dynamic-slice_fusion.2.refs_14_
  620.9 63.0 %shard_map.172 = (bf16[4,192,256]{2,1,0:T(8,128)(2,1)}, bf16[4,48,704]{2,1,0:T(8,128)(2,1)}, f32[128,2048]{1,0:T(8,128)}, bf16[16,2048]{1,0:T(8,128)(2,1)}, bf16...) custom-call(f32[128,2048]{1,0:T(8,128)} %get-tuple-element.117.refs_0_, f32[128,2048]{1,0:T(8,128)} %get-tuple-element.81.refs_0_.refs_1_, ...), custom_call_target="tpu_custom_call" | custom-call | tf_op jit(solution)/shard_map/pallas_call | solution.py:1343
  683.9 69.0 %shard_map.173 = (f32[128,2048]{1,0:T(8,128)}, bf16[192,256]{1,0:T(8,128)(2,1)}, bf16[4,2,64,768]{3,2,1,0:T(8,128)(2,1)}) custom-call(f32[128,2048]{1,0:T(8,128)} %get-tuple-element.127.refs_0_, bf16[128,2048]{1,0:T(8,128)(2,1)} %copy-done.3, f32[1,2048]{1,0:T(1,128)} %get-tuple-element.156.refs_1_.refs_2_, ...), custom_call_target="tpu_custom_call" | custom-call | tf_op jit(solution)/shard_map/pallas_call | solution.py:1343
  752.9 1.0 dynamic-slice_bitcast_fusion
  754.0 0.7 constant_dynamic-slice_fusion.1.own_units
  754.7 40.1 %shard_map.174 = (f32[256,2048]{1,0:T(8,128)}, f32[2,11,2,16,256]{4,3,2,1,0:T(8,128)}, f32[2,3,2,16,704]{4,3,2,1,0:T(8,128)}) custom-call(f32[128,2048]{1,0:T(8,128)} %get-tuple-element.140.grad, bf16[192,256]{1,0:T(8,128)(2,1)} %get-tuple-element.141.own_sums, bf16[48,704]{1,0:T(8,128)(2,1)} %constant_dynamic-slice_fusion.1.own_units, ...), custom_call_target="tpu_custom_call" | custom-call | tf_op jit(solution)/shard_map/pallas_call | solution.py:1343
  794.9 2.5 copy.56
  797.3 1.3 copy.57
  798.6 0.9 copy.58
  799.5 0.8 copy.59
  (32 shorter events, 0.3 us)
Async XLA Ops:
  0.6 9.3 %copy-start = (bf16[256,2048]{1,0:T(8,128)(2,1)S(1)}, bf16[256,2048]{1,0:T(8,128)(2,1)}, u32[]{:S(2)}) copy-start(bf16[256,2048]{1,0:T(8,128)(2,1)} %param.15) | copy-start | bytes 3145732
  2.2 97.8 %collective-permute-start.5 = (s32[526]{0:T(1024)S(1)}, s32[526]{0:T(1024)S(1)}, u32[]{:S(2)}, u32[]{:S(2)}) collective-permute-start(s32[526]{0:T(1024)S(1)} %pad_add_fusion), channel_id=1, source_target_pairs={{0,10},{2,8},{4,2},{6,0},{8,14},{10,12},{12,6},{14,4},{16,26},{18,... | collective-permute-start | bytes 6320 | tf_op jit(solution)/shard_map/ppermute | solution.py:1383
  5.5 96.5 %collective-permute-start.4 = (s32[526]{0:T(1024)S(1)}, s32[526]{0:T(1024)S(1)}, u32[]{:S(2)}, u32[]{:S(2)}) collective-permute-start(s32[526]{0:T(1024)S(1)} %pad_add_fusion), channel_id=1, source_target_pairs={{0,8},{2,10},{4,0},{6,2},{8,12},{10,14},{12,4},{14,6},{16,24},{18,... | collective-permute-start | bytes 6320 | tf_op jit(solution)/shard_map/ppermute | solution.py:1383
  5.7 96.3 %collective-permute-start.3 = (s32[526]{0:T(1024)S(1)}, s32[526]{0:T(1024)S(1)}, u32[]{:S(2)}, u32[]{:S(2)}) collective-permute-start(s32[526]{0:T(1024)S(1)} %pad_add_fusion), channel_id=1, source_target_pairs={{0,2},{2,0},{4,10},{6,8},{8,6},{10,4},{12,14},{14,12},{16,18},{18,... | collective-permute-start | bytes 6320 | tf_op jit(solution)/shard_map/ppermute | solution.py:1383
  6.6 95.4 %collective-permute-start.2 = (s32[526]{0:T(1024)S(1)}, s32[526]{0:T(1024)S(1)}, u32[]{:S(2)}, u32[]{:S(2)}) collective-permute-start(s32[526]{0:T(1024)S(1)} %pad_add_fusion), channel_id=1, source_target_pairs={{0,0},{2,2},{4,8},{6,10},{8,4},{10,6},{12,12},{14,14},{16,16},{18,... | collective-permute-start | bytes 6320 | tf_op jit(solution)/shard_map/ppermute | solution.py:1383
  10.0 408.9 %collective-permute-start = (bf16[128,2048]{1,0:T(8,128)(2,1)S(1)}, bf16[128,2048]{1,0:T(8,128)(2,1)S(1)}, u32[]{:S(2)}, u32[]{:S(2)}) collective-permute-start(bf16[128,2048]{1,0:T(8,128)(2,1)S(1)} %constant_dynamic-slice_fusion.9), channel_id=1, source_target_pairs={{0,0},{2,2},{4,8},{6,10},{8,4},{10,6},{12,12},{14,14},{16,16},{18,... | collective-permute-start | bytes 1572872 | tf_op jit(solution)/shard_map/ppermute | solution.py:1383
  99.9 28.3 %collective-permute-start.1 = (bf16[128,2048]{1,0:T(8,128)(2,1)}, bf16[128,2048]{1,0:T(8,128)(2,1)S(1)}, u32[]{:S(2)}, u32[]{:S(2)}) collective-permute-start(bf16[128,2048]{1,0:T(8,128)(2,1)} %constant_dynamic-slice_fusion.8), channel_id=1, source_target_pairs={{0,0},{2,2},{4,8},{6,10},{8,4},{10,6},{12,12},{14,14},{16,16},{18,... | collective-permute-start | bytes 1572872 | tf_op jit(solution)/shard_map/ppermute | solution.py:1383
  128.2 0.8 copy-start.3
  418.9 0.8 copy-start.2
  794.8 2.5 copy-start.4
  794.8 3.8 copy-start.5
  794.9 5.5 copy-start.1
  797.3 2.2 copy-start.6

commit v8 on v7

--- a/solution.py
+++ b/solution.py
@@ -151,7 +151,7 @@
                 copy.wait_send()
 
 
-def enter(place, nf=0, scatters=False, home=False, ring=True, trees=0):
+def enter(place, nf=0, scatters=False, home=False, ring=True, trees=0, partner=False):
     bar = pltpu.get_barrier_semaphore()
     devices = [{"tp": 1 - place.t}]
     guide = Spread(place, nf, None, 0)
@@ -162,6 +162,8 @@
     if nf:
         devices += [guide.partner()] + [guide.line(e) for e in guide.links]
     devices += [{"fsdp": flip(place.f, e)} for e in range(1, trees)]
+    if partner:
+        devices.append(guide.partner())
     for device in devices:
         pl.semaphore_signal(bar, inc=1, device_id=device, device_id_type=MESH)
     count = len(devices)
@@ -1194,8 +1196,8 @@
     grad, own_sums, own_units, slot, *refs,
 ):
     earlier, refs = refs[: 2 * layers - 2], refs[2 * layers - 2 :]
-    (tokens_grad, model_grad, hidden_grad,
-     rows_out, landed, sent_sums, all_sums, all_units, home_send, home_recv, tree_send, tree_recv) = refs
+    (landed, model_grad, hidden_grad,
+     rows_out, passing, sent_sums, all_sums, all_units, home_send, home_recv, tree_send, tree_recv, relay_send, relay_recv) = refs
     place = Place(n)
     own = model_grad.shape[2]
     tall = own_sums.shape[0]
@@ -1206,8 +1208,26 @@
     by_rows(grad.shape[0], cut)
     sent_sums[...] = own_sums[...]
     sent_sums[tall - rank :] = jnp.broadcast_to(slot[...], (rank, own_sums.shape[1])).astype(BF)
-    enter(place, home=True, ring=False, trees=nf)
-    moves = [Home(place, landed, home_send.at[0], home_recv.at[0])]
+    enter(place, home=True, ring=False, trees=nf, partner=True)
+    top = grad.shape[0] // 2
+    low, high = pl.ds(0, top), pl.ds(top, top)
+    slot_here = landed.at[place.t]
+    partner = {"ctx": (1 - place.c_hi) * place.h + place.c_lo}
+    beside = {"fsdp": place.f_hi * 2 + 1 - place.f_lo}
+
+    def make(src, dst, i, device):
+        return pltpu.make_async_remote_copy(
+            src_ref=src, dst_ref=dst, send_sem=relay_send.at[i], recv_sem=relay_recv.at[i],
+            device_id=device, device_id_type=MESH,
+        )
+
+    straight = make(rows_out.at[low], slot_here.at[low], 0, place.home)
+    to_relay = make(rows_out.at[high], passing, 1, beside)
+    from_relay = make(passing, slot_here.at[high], 2, partner)
+    stay = pltpu.make_async_copy(rows_out, slot_here, relay_recv.at[3])
+    cross = make(slot_here, slot_here, 4, {"tp": 1 - place.t})
+    is_away, is_relay = place.away == 1, place.away == 0
+
     away = {}
     for i, (source, target) in enumerate(((sent_sums, all_sums), (own_units, all_units))):
         away[i] = TreeMove(place, source, target.at[:, 0], home_send.at[i + 1], home_recv.at[i + 1])
@@ -1228,9 +1248,19 @@
     for i, target in enumerate((all_sums, all_units)):
         away[i].land()
         if i == 1:
-            moves[0].start(rows_out)
+
+            @pl.when(is_away)
+            def leave():
+                straight.start()
+                to_relay.start()
+
+            pl.when(is_relay)(stay.start)
         hand_round(target.at[place.f, 0], target, 0, i)
-    moves[0].land()
+    @pl.when(is_relay)
+    def hand_on():
+        to_relay.wait_recv()
+        from_relay.start()
+
     for copy in copies:
         copy.wait_recv()
     for b in range(own):
@@ -1245,14 +1275,20 @@
             for k in range(3):
                 at = slice(k * rank, (k + 1) * rank)
                 hidden_grad[l, k, b] = sum(keeps[f] * all_units[f, l, at].astype(F32) for f in range(nf))
-    moves[0].finish()
-    for core in range(2):
-
-        def widen(at, core=core):
-            rows = landed.shape[1]
-            tokens_grad[pl.ds(pl.multiple_of(core * rows + at.start, 16), at.size)] = landed[core, at].astype(F32)
-
-        by_rows(landed.shape[1], widen)
+
+    @pl.when(is_relay)
+    def rest():
+        stay.wait()
+        from_relay.wait_send()
+
+    @pl.when(is_away)
+    def arrive():
+        straight.wait()
+        to_relay.wait_send()
+        from_relay.wait_recv()
+
+    cross.start()
+    cross.wait()
     for copy in copies:
         copy.wait_send()
 
@@ -1525,7 +1561,8 @@
             moves("forward", 0, parts(n, 0, come)) + moves("spread", 0, parts(n, come, 4)),
             moves("forward", 0, parts(n, come, 2)) + ([] if last else [("scatter", 0)]),
             moves("spread", 1, parts(n, 0, 2)) + moves("forward", 0, parts(n, 2, 3)),
-            moves("forward", 0, parts(n, 3, 4)) + ([] if last else [("scatter", 1)]),
+            moves("forward", 0, parts(n, 3, 4)),
+            [] if last else [("scatter", 1)],
         )
         got = run(
             functools.partial(attention_forward, n, nf, l, part, rank, True, plan),
@@ -1664,13 +1701,13 @@
         functools.partial(finish_kernel, n, nf, layers, rank),
         near(grad, sums_here[0], units_here[0], slot.astype(F32).reshape(1, 1), *earlier),
         [
-            out((2 * rows, width), F32),
+            out((2, rows, width), BF),
             out((layers, 11, own, rank, block), F32),
             out((layers, 3, own, rank, wide), F32),
         ],
         [
             vmem((rows, width), BF),
-            vmem((2, rows, width), BF),
+            vmem((rows // 2, width), BF),
             vmem((12 * rank, block), BF),
             vmem((nf, layers, 12 * rank, block), BF),
             vmem((nf, layers, 3 * rank, wide), BF),
@@ -1678,11 +1715,13 @@
             dma((3, 2)),
             dma((layers, 2, nf)),
             dma((layers, 2, nf)),
+            dma((5,)),
+            dma((5,)),
         ],
     )
     return (
         outputs.reshape(2 * rows, width),
-        tokens_grad,
+        tokens_grad.reshape(2 * rows, width).astype(F32),
         grad_model,
         grad_hidden,
     )

time: 808 us -> 806 us (level)
  no operation moved by 1% of the time
where the time goes in v8:
time: 806 us; the launch traced here: 799 us
  Pallas kernels  738 us (92%)
  local copies, waits for them, and re-layouts  22.5 us (3%)
  starting transfers between devices  13.6 us (2%)
  waiting for transfers between devices  10.7 us (1%)
  other arithmetic  8.65 us (1%)
    pallas_call x10, Pallas kernels, call(): pl.pallas_call(body, out_shape=[jax.ShapeDtypeStruct(shape, kind) for sha...  738 us
  transfers between devices with their start and end apart: 6, of which 1 were waited for; matrix products, arithmetic and copies ran while one was open for 2% of the time, Pallas kernels for 46%

profile of v8, /device:TPU:3, one launch (start us, length us, event | category | flops | bytes accessed | tf_op | source)
XLA Modules:
  0.0 798.6 jit_solution(3224745197446462921)
XLA Ops:
  0.6 0.0 copy-start
  1.4 0.8 pad_add_fusion
  2.2 3.3 collective-permute-start.5
  5.5 0.3 collective-permute-start.4
  5.7 0.9 collective-permute-start.3
  6.6 3.3 collective-permute-start.2
  10.0 3.8 collective-permute-start
  14.0 0.8 fusion.6
  14.7 1.4 slice_bitcast_fusion.2
  16.2 1.9 constant_dynamic-slice_fusion.8
  18.0 0.6 constant_dynamic-slice_fusion.6.refs_9_.refs_10_
  18.7 0.7 constant_dynamic-slice_fusion.3.refs_9_.refs_10_
  19.3 80.6 %shard_map.165 = (bf16[2048,1024]{1,0:T(8,128)(2,1)}, bf16[2048,1536]{1,0:T(8,128)(2,1)}, bf16[2048,768]{1,0:T(8,128)(2,1)}, bf16[4,128,1024]{2,1,0:T(8,128)(2,1...) custom-call(bf16[2,3,128,1024]{3,2,1,0:T(8,128)(2,1)} %bitcast.67, bf16[2,128,1024]{2,1,0:T(8,128)(2,1)} %output.1, ...), custom_call_target="tpu_custom_call" | custom-call | tf_op jit(solution)/shard_map/pallas_call | solution.py:1379
  99.9 2.1 collective-permute-start.1
  102.0 0.1 select_add_fusion
  102.1 0.6 slice.90
  104.7 1.1 dynamic-slice_bitcast_fusion.2
  105.8 0.2 select_reduce_fusion.1
  106.0 1.3 constant_dynamic-slice_fusion.5
  107.3 0.1 select_reduce_fusion
  107.5 1.9 fusion
  109.4 0.7 fusion.2
  110.0 0.6 pad_maximum_fusion.2
  111.3 0.6 copy.42
  111.9 1.0 copy.32.refs_7_.refs_8_
  112.9 1.0 pad_maximum_fusion.refs_5_.refs_6_
  113.9 1.0 pad_maximum_fusion.1.refs_6_.refs_7_
  115.0 2.6 constant_dynamic-slice_fusion.7
  117.6 10.7 %collective-permute-done.1.refs_0_.refs_1_ = bf16[128,2048]{1,0:T(8,128)(2,1)S(1)} collective-permute-done((bf16[128,2048]{1,0:T(8,128)(2,1)}, bf16[128,2048]{1,0:T(8,128)(2,1)S(1)}, u32[]{:S(2)}, u32[]{:S(2)}) %collective-permute-start.1) | collective-permute-done | bytes 524320 | tf_op jit(solution)/shard_map/ppermute | solution.py:1419
  128.2 0.8 copy-done.3
  129.0 95.1 %shard_map.166 = (bf16[2048,1024]{1,0:T(8,128)(2,1)}, bf16[2048,1536]{1,0:T(8,128)(2,1)}, bf16[2048,1536]{1,0:T(8,128)(2,1)}, bf16[2048,768]{1,0:T(8,128)(2,1)},...) custom-call(bf16[128,2048]{1,0:T(8,128)(2,1)} %copy-done.3, ...), custom_call_target="tpu_custom_call", output_to_operand_aliasing={{2}: (12, {}), {3}: (13, {})} | custom-call | tf_op jit(solution)/shard_map/pallas_call | solution.py:1379
  224.1 117.1 %shard_map.167 = (bf16[2048,768]{1,0:T(8,128)(2,1)}, bf16[2048,768]{1,0:T(8,128)(2,1)}, bf16[2048,1024]{1,0:T(8,128)(2,1)}, bf16[2048,1536]{1,0:T(8,128)(2,1)}, ...) custom-call(f32[128,2048]{1,0:T(8,128)} %get-tuple-element.81.refs_0, ...), custom_call_target="tpu_custom_call", output_to_operand_aliasing={{1}: (6, {}), {2}: (7, {}), {3}: (8, {})} | custom-call | tf_op jit(solution)/shard_map/pallas_call | solution.py:1379
  341.2 76.5 %shard_map.168 = (bf16[2048,1536]{1,0:T(8,128)(2,1)}, bf16[2048,768]{1,0:T(8,128)(2,1)}, f32[128,2048]{1,0:T(8,128)}, bf16[4,2,128,2048]{3,2,1,0:T(8,128)(2,1)},...) custom-call(f32[128,2048]{1,0:T(8,128)} %get-tuple-element.87.refs_0, ...), custom_call_target="tpu_custom_call", output_to_operand_aliasing={{0}: (10, {}), {1}: (11, {})} | custom-call | tf_op jit(solution)/shard_map/pallas_call | solution.py:1379
  417.7 0.8 copy-done.2
  418.5 80.7 %shard_map.169 = (bf16[2048,768]{1,0:T(8,128)(2,1)}, bf16[4,2,128,2048]{3,2,1,0:T(8,128)(2,1)}, f32[128,2048]{1,0:T(8,128)}, bf16[4,2,128,2048]{3,2,1,0:T(8,128)...) custom-call(f32[128,2048]{1,0:T(8,128)} %get-tuple-element.91.refs_0, ...), custom_call_target="tpu_custom_call", output_to_operand_aliasing={{0}: (6, {})} | custom-call | tf_op jit(solution)/shard_map/pallas_call | solution.py:1379
  499.2 49.3 %shard_map.170 = (bf16[2,128,2048]{2,1,0:T(8,128)(2,1)}, f32[128,2048]{1,0:T(8,128)}, bf16[16,2048]{1,0:T(8,128)(2,1)}, bf16[32,2048]{1,0:T(8,128)(2,1)}, bf16[64,768]{1,0:T(8,128)(2,1)}) custom-call(bf16[128,2048]{1,0:T(8,128)(2,1)} %copy-done.2, f32[128,2048]{1,0:T(8,128)} %get-tuple-element.91.refs_0_.refs_1_, ...), custom_call_target="tpu_custom_call" | custom-call | tf_op jit(solution)/shard_map/pallas_call | solution.py:1379
  548.5 69.1 %shard_map.171 = (f32[128,2048]{1,0:T(8,128)}, bf16[192,256]{1,0:T(8,128)(2,1)}, bf16[4,2,64,768]{3,2,1,0:T(8,128)(2,1)}) custom-call(f32[128,2048]{1,0:T(8,128)} %get-tuple-element.104.refs_0_, f32[128,2048]{1,0:T(8,128)} %get-tuple-element.87.refs_0_.refs_1_, f32[1,2048]{1,0:T(1,128)} %get-tuple-element.157.refs_1_.refs_2_, ...), custom_call_target="tpu_custom_call" | custom-call | tf_op jit(solution)/shard_map/pallas_call | solution.py:1379
  617.7 1.0 dynamic-slice_bitcast_fusion.1
  618.8 0.7 constant_dynamic-slice_fusion.2.refs_14_
  619.5 63.5 %shard_map.172 = (bf16[4,192,256]{2,1,0:T(8,128)(2,1)}, bf16[4,48,704]{2,1,0:T(8,128)(2,1)}, f32[128,2048]{1,0:T(8,128)}, bf16[16,2048]{1,0:T(8,128)(2,1)}, bf16...) custom-call(f32[128,2048]{1,0:T(8,128)} %get-tuple-element.117.refs_0_, f32[128,2048]{1,0:T(8,128)} %get-tuple-element.81.refs_0_.refs_1_, ...), custom_call_target="tpu_custom_call" | custom-call | tf_op jit(solution)/shard_map/pallas_call | solution.py:1379
  683.0 68.4 %shard_map.173 = (f32[128,2048]{1,0:T(8,128)}, bf16[192,256]{1,0:T(8,128)(2,1)}, bf16[4,2,64,768]{3,2,1,0:T(8,128)(2,1)}) custom-call(f32[128,2048]{1,0:T(8,128)} %get-tuple-element.127.refs_0_, bf16[128,2048]{1,0:T(8,128)(2,1)} %copy-done.3, f32[1,2048]{1,0:T(1,128)} %get-tuple-element.156.refs_1_.refs_2_, ...), custom_call_target="tpu_custom_call" | custom-call | tf_op jit(solution)/shard_map/pallas_call | solution.py:1379
  751.4 1.0 dynamic-slice_bitcast_fusion
  752.5 0.7 constant_dynamic-slice_fusion.1.own_units
  753.2 38.2 %shard_map.174 = (bf16[2,128,2048]{2,1,0:T(8,128)(2,1)}, f32[2,11,2,16,256]{4,3,2,1,0:T(8,128)}, f32[2,3,2,16,704]{4,3,2,1,0:T(8,128)}) custom-call(f32[128,2048]{1,0:T(8,128)} %get-tuple-element.140.grad, bf16[192,256]{1,0:T(8,128)(2,1)} %get-tuple-element.141.own_sums, bf16[48,704]{1,0:T(8,128)(2,1)} %constant_dynamic-slice_fusion.1.own_units, ...), custom_call_target="tpu_custom_call" | custom-call | tf_op jit(solution)/shard_map/pallas_call | solution.py:1379
  791.5 2.9 bitcast_convert_fusion
  794.4 2.3 copy.55
  796.7 0.9 copy.56
  797.6 0.8 copy.57
  (30 shorter events, 0.3 us)
Async XLA Ops:
  0.6 9.3 %copy-start = (bf16[256,2048]{1,0:T(8,128)(2,1)S(1)}, bf16[256,2048]{1,0:T(8,128)(2,1)}, u32[]{:S(2)}) copy-start(bf16[256,2048]{1,0:T(8,128)(2,1)} %param.15) | copy-start | bytes 3145732
  2.2 97.7 %collective-permute-start.5 = (s32[526]{0:T(1024)S(1)}, s32[526]{0:T(1024)S(1)}, u32[]{:S(2)}, u32[]{:S(2)}) collective-permute-start(s32[526]{0:T(1024)S(1)} %pad_add_fusion), channel_id=1, source_target_pairs={{0,10},{2,8},{4,2},{6,0},{8,14},{10,12},{12,6},{14,4},{16,26},{18,... | collective-permute-start | bytes 6320 | tf_op jit(solution)/shard_map/ppermute | solution.py:1419
  5.5 96.5 %collective-permute-start.4 = (s32[526]{0:T(1024)S(1)}, s32[526]{0:T(1024)S(1)}, u32[]{:S(2)}, u32[]{:S(2)}) collective-permute-start(s32[526]{0:T(1024)S(1)} %pad_add_fusion), channel_id=1, source_target_pairs={{0,8},{2,10},{4,0},{6,2},{8,12},{10,14},{12,4},{14,6},{16,24},{18,... | collective-permute-start | bytes 6320 | tf_op jit(solution)/shard_map/ppermute | solution.py:1419
  5.7 96.3 %collective-permute-start.3 = (s32[526]{0:T(1024)S(1)}, s32[526]{0:T(1024)S(1)}, u32[]{:S(2)}, u32[]{:S(2)}) collective-permute-start(s32[526]{0:T(1024)S(1)} %pad_add_fusion), channel_id=1, source_target_pairs={{0,2},{2,0},{4,10},{6,8},{8,6},{10,4},{12,14},{14,12},{16,18},{18,... | collective-permute-start | bytes 6320 | tf_op jit(solution)/shard_map/ppermute | solution.py:1419
  6.6 95.4 %collective-permute-start.2 = (s32[526]{0:T(1024)S(1)}, s32[526]{0:T(1024)S(1)}, u32[]{:S(2)}, u32[]{:S(2)}) collective-permute-start(s32[526]{0:T(1024)S(1)} %pad_add_fusion), channel_id=1, source_target_pairs={{0,0},{2,2},{4,8},{6,10},{8,4},{10,6},{12,12},{14,14},{16,16},{18,... | collective-permute-start | bytes 6320 | tf_op jit(solution)/shard_map/ppermute | solution.py:1419
  10.0 407.7 %collective-permute-start = (bf16[128,2048]{1,0:T(8,128)(2,1)S(1)}, bf16[128,2048]{1,0:T(8,128)(2,1)S(1)}, u32[]{:S(2)}, u32[]{:S(2)}) collective-permute-start(bf16[128,2048]{1,0:T(8,128)(2,1)S(1)} %constant_dynamic-slice_fusion.9), channel_id=1, source_target_pairs={{0,0},{2,2},{4,8},{6,10},{8,4},{10,6},{12,12},{14,14},{16,16},{18,... | collective-permute-start | bytes 1572872 | tf_op jit(solution)/shard_map/ppermute | solution.py:1419
  99.9 28.3 %collective-permute-start.1 = (bf16[128,2048]{1,0:T(8,128)(2,1)}, bf16[128,2048]{1,0:T(8,128)(2,1)S(1)}, u32[]{:S(2)}, u32[]{:S(2)}) collective-permute-start(bf16[128,2048]{1,0:T(8,128)(2,1)} %constant_dynamic-slice_fusion.8), channel_id=1, source_target_pairs={{0,0},{2,2},{4,8},{6,10},{8,4},{10,6},{12,12},{14,14},{16,16},{18,... | collective-permute-start | bytes 1572872 | tf_op jit(solution)/shard_map/ppermute | solution.py:1419
  128.2 0.8 copy-start.3
  417.7 0.8 copy-start.2
  791.4 5.3 copy-start.4
  791.4 6.1 copy-start.5
  791.4 6.9 copy-start.1

commit v9 on v8

--- a/solution.py
+++ b/solution.py
@@ -460,7 +460,7 @@
             copy.wait_send()
 
 
-def by_rows(count, body, step=16):
+def by_rows(count, body, step=32):
     def one(i, carry):
         body(pl.ds(pl.multiple_of(i * step, step), step))
         return carry

time: 806 us -> 801 us (level)
  no operation moved by 1% of the time
where the time goes in v9:
time: 801 us; the launch traced here: 793 us
  Pallas kernels  733 us (92%)
  local copies, waits for them, and re-layouts  22.5 us (3%)
  starting transfers between devices  13.7 us (2%)
  waiting for transfers between devices  10.6 us (1%)
  other arithmetic  8.65 us (1%)
    pallas_call x10, Pallas kernels, call(): pl.pallas_call(body, out_shape=[jax.ShapeDtypeStruct(shape, kind) for sha...  733 us
  transfers between devices with their start and end apart: 6, of which 1 were waited for; matrix products, arithmetic and copies ran while one was open for 2% of the time, Pallas kernels for 46%

profile of v9, /device:TPU:3, one launch (start us, length us, event | category | flops | bytes accessed | tf_op | source)
XLA Modules:
  0.0 793.5 jit_solution(16770615089770109503)
XLA Ops:
  0.6 0.0 copy-start
  1.4 0.8 pad_add_fusion
  2.2 3.3 collective-permute-start.5
  5.5 0.3 collective-permute-start.4
  5.7 0.9 collective-permute-start.3
  6.6 3.3 collective-permute-start.2
  10.0 3.8 collective-permute-start
  14.0 0.8 fusion.6
  14.7 1.4 slice_bitcast_fusion.2
  16.2 1.9 constant_dynamic-slice_fusion.8
  18.0 0.6 constant_dynamic-slice_fusion.6.refs_9_.refs_10_
  18.7 0.7 constant_dynamic-slice_fusion.3.refs_9_.refs_10_
  19.3 80.6 %shard_map.165 = (bf16[2048,1024]{1,0:T(8,128)(2,1)}, bf16[2048,1536]{1,0:T(8,128)(2,1)}, bf16[2048,768]{1,0:T(8,128)(2,1)}, bf16[4,128,1024]{2,1,0:T(8,128)(2,1...) custom-call(bf16[2,3,128,1024]{3,2,1,0:T(8,128)(2,1)} %bitcast.67, bf16[2,128,1024]{2,1,0:T(8,128)(2,1)} %output.1, ...), custom_call_target="tpu_custom_call" | custom-call | tf_op jit(solution)/shard_map/pallas_call | solution.py:1379
  99.9 2.2 collective-permute-start.1
  102.2 0.1 select_add_fusion
  102.2 0.6 slice.90
  104.8 1.1 dynamic-slice_bitcast_fusion.2
  105.9 0.2 select_reduce_fusion.1
  106.1 1.3 constant_dynamic-slice_fusion.5
  107.4 0.1 select_reduce_fusion
  107.6 1.9 fusion
  109.5 0.7 fusion.2
  110.2 0.6 pad_maximum_fusion.2
  111.4 0.6 copy.42
  112.0 1.0 copy.32.refs_7_.refs_8_
  113.1 1.0 pad_maximum_fusion.refs_5_.refs_6_
  114.1 1.0 pad_maximum_fusion.1.refs_6_.refs_7_
  115.1 2.6 constant_dynamic-slice_fusion.7
  117.7 10.6 %collective-permute-done.1.refs_0_.refs_1_ = bf16[128,2048]{1,0:T(8,128)(2,1)S(1)} collective-permute-done((bf16[128,2048]{1,0:T(8,128)(2,1)}, bf16[128,2048]{1,0:T(8,128)(2,1)S(1)}, u32[]{:S(2)}, u32[]{:S(2)}) %collective-permute-start.1) | collective-permute-done | bytes 524320 | tf_op jit(solution)/shard_map/ppermute | solution.py:1419
  128.2 0.8 copy-done.3
  129.0 94.6 %shard_map.166 = (bf16[2048,1024]{1,0:T(8,128)(2,1)}, bf16[2048,1536]{1,0:T(8,128)(2,1)}, bf16[2048,1536]{1,0:T(8,128)(2,1)}, bf16[2048,768]{1,0:T(8,128)(2,1)},...) custom-call(bf16[128,2048]{1,0:T(8,128)(2,1)} %copy-done.3, ...), custom_call_target="tpu_custom_call", output_to_operand_aliasing={{2}: (12, {}), {3}: (13, {})} | custom-call | tf_op jit(solution)/shard_map/pallas_call | solution.py:1379
  223.6 116.7 %shard_map.167 = (bf16[2048,768]{1,0:T(8,128)(2,1)}, bf16[2048,768]{1,0:T(8,128)(2,1)}, bf16[2048,1024]{1,0:T(8,128)(2,1)}, bf16[2048,1536]{1,0:T(8,128)(2,1)}, ...) custom-call(f32[128,2048]{1,0:T(8,128)} %get-tuple-element.81.refs_0, ...), custom_call_target="tpu_custom_call", output_to_operand_aliasing={{1}: (6, {}), {2}: (7, {}), {3}: (8, {})} | custom-call | tf_op jit(solution)/shard_map/pallas_call | solution.py:1379
  340.4 76.1 %shard_map.168 = (bf16[2048,1536]{1,0:T(8,128)(2,1)}, bf16[2048,768]{1,0:T(8,128)(2,1)}, f32[128,2048]{1,0:T(8,128)}, bf16[4,2,128,2048]{3,2,1,0:T(8,128)(2,1)},...) custom-call(f32[128,2048]{1,0:T(8,128)} %get-tuple-element.87.refs_0, ...), custom_call_target="tpu_custom_call", output_to_operand_aliasing={{0}: (10, {}), {1}: (11, {})} | custom-call | tf_op jit(solution)/shard_map/pallas_call | solution.py:1379
  416.5 0.8 copy-done.2
  417.3 80.3 %shard_map.169 = (bf16[2048,768]{1,0:T(8,128)(2,1)}, bf16[4,2,128,2048]{3,2,1,0:T(8,128)(2,1)}, f32[128,2048]{1,0:T(8,128)}, bf16[4,2,128,2048]{3,2,1,0:T(8,128)...) custom-call(f32[128,2048]{1,0:T(8,128)} %get-tuple-element.91.refs_0, ...), custom_call_target="tpu_custom_call", output_to_operand_aliasing={{0}: (6, {})} | custom-call | tf_op jit(solution)/shard_map/pallas_call | solution.py:1379
  497.6 48.3 %shard_map.170 = (bf16[2,128,2048]{2,1,0:T(8,128)(2,1)}, f32[128,2048]{1,0:T(8,128)}, bf16[16,2048]{1,0:T(8,128)(2,1)}, bf16[32,2048]{1,0:T(8,128)(2,1)}, bf16[64,768]{1,0:T(8,128)(2,1)}) custom-call(bf16[128,2048]{1,0:T(8,128)(2,1)} %copy-done.2, f32[128,2048]{1,0:T(8,128)} %get-tuple-element.91.refs_0_.refs_1_, ...), custom_call_target="tpu_custom_call" | custom-call | tf_op jit(solution)/shard_map/pallas_call | solution.py:1379
  545.8 68.5 %shard_map.171 = (f32[128,2048]{1,0:T(8,128)}, bf16[192,256]{1,0:T(8,128)(2,1)}, bf16[4,2,64,768]{3,2,1,0:T(8,128)(2,1)}) custom-call(f32[128,2048]{1,0:T(8,128)} %get-tuple-element.104.refs_0_, f32[128,2048]{1,0:T(8,128)} %get-tuple-element.87.refs_0_.refs_1_, f32[1,2048]{1,0:T(1,128)} %get-tuple-element.157.refs_1_.refs_2_, ...), custom_call_target="tpu_custom_call" | custom-call | tf_op jit(solution)/shard_map/pallas_call | solution.py:1379
  614.3 1.0 dynamic-slice_bitcast_fusion.1
  615.4 0.7 constant_dynamic-slice_fusion.2.refs_14_
  616.1 62.7 %shard_map.172 = (bf16[4,192,256]{2,1,0:T(8,128)(2,1)}, bf16[4,48,704]{2,1,0:T(8,128)(2,1)}, f32[128,2048]{1,0:T(8,128)}, bf16[16,2048]{1,0:T(8,128)(2,1)}, bf16...) custom-call(f32[128,2048]{1,0:T(8,128)} %get-tuple-element.117.refs_0_, f32[128,2048]{1,0:T(8,128)} %get-tuple-element.81.refs_0_.refs_1_, ...), custom_call_target="tpu_custom_call" | custom-call | tf_op jit(solution)/shard_map/pallas_call | solution.py:1379
  678.8 67.4 %shard_map.173 = (f32[128,2048]{1,0:T(8,128)}, bf16[192,256]{1,0:T(8,128)(2,1)}, bf16[4,2,64,768]{3,2,1,0:T(8,128)(2,1)}) custom-call(f32[128,2048]{1,0:T(8,128)} %get-tuple-element.127.refs_0_, bf16[128,2048]{1,0:T(8,128)(2,1)} %copy-done.3, f32[1,2048]{1,0:T(1,128)} %get-tuple-element.156.refs_1_.refs_2_, ...), custom_call_target="tpu_custom_call" | custom-call | tf_op jit(solution)/shard_map/pallas_call | solution.py:1379
  746.3 1.0 dynamic-slice_bitcast_fusion
  747.4 0.7 constant_dynamic-slice_fusion.1.own_units
  748.1 38.1 %shard_map.174 = (bf16[2,128,2048]{2,1,0:T(8,128)(2,1)}, f32[2,11,2,16,256]{4,3,2,1,0:T(8,128)}, f32[2,3,2,16,704]{4,3,2,1,0:T(8,128)}) custom-call(f32[128,2048]{1,0:T(8,128)} %get-tuple-element.140.grad, bf16[192,256]{1,0:T(8,128)(2,1)} %get-tuple-element.141.own_sums, bf16[48,704]{1,0:T(8,128)(2,1)} %constant_dynamic-slice_fusion.1.own_units, ...), custom_call_target="tpu_custom_call" | custom-call | tf_op jit(solution)/shard_map/pallas_call | solution.py:1379
  786.3 2.9 bitcast_convert_fusion
  789.2 2.3 copy.55
  791.5 0.9 copy.56
  792.4 0.8 copy.57
  (30 shorter events, 0.3 us)
Async XLA Ops:
  0.6 9.3 %copy-start = (bf16[256,2048]{1,0:T(8,128)(2,1)S(1)}, bf16[256,2048]{1,0:T(8,128)(2,1)}, u32[]{:S(2)}) copy-start(bf16[256,2048]{1,0:T(8,128)(2,1)} %param.15) | copy-start | bytes 3145732
  2.2 97.7 %collective-permute-start.5 = (s32[526]{0:T(1024)S(1)}, s32[526]{0:T(1024)S(1)}, u32[]{:S(2)}, u32[]{:S(2)}) collective-permute-start(s32[526]{0:T(1024)S(1)} %pad_add_fusion), channel_id=1, source_target_pairs={{0,10},{2,8},{4,2},{6,0},{8,14},{10,12},{12,6},{14,4},{16,26},{18,... | collective-permute-start | bytes 6320 | tf_op jit(solution)/shard_map/ppermute | solution.py:1419
  5.5 96.6 %collective-permute-start.4 = (s32[526]{0:T(1024)S(1)}, s32[526]{0:T(1024)S(1)}, u32[]{:S(2)}, u32[]{:S(2)}) collective-permute-start(s32[526]{0:T(1024)S(1)} %pad_add_fusion), channel_id=1, source_target_pairs={{0,8},{2,10},{4,0},{6,2},{8,12},{10,14},{12,4},{14,6},{16,24},{18,... | collective-permute-start | bytes 6320 | tf_op jit(solution)/shard_map/ppermute | solution.py:1419
  5.7 96.4 %collective-permute-start.3 = (s32[526]{0:T(1024)S(1)}, s32[526]{0:T(1024)S(1)}, u32[]{:S(2)}, u32[]{:S(2)}) collective-permute-start(s32[526]{0:T(1024)S(1)} %pad_add_fusion), channel_id=1, source_target_pairs={{0,2},{2,0},{4,10},{6,8},{8,6},{10,4},{12,14},{14,12},{16,18},{18,... | collective-permute-start | bytes 6320 | tf_op jit(solution)/shard_map/ppermute | solution.py:1419
  6.6 95.5 %collective-permute-start.2 = (s32[526]{0:T(1024)S(1)}, s32[526]{0:T(1024)S(1)}, u32[]{:S(2)}, u32[]{:S(2)}) collective-permute-start(s32[526]{0:T(1024)S(1)} %pad_add_fusion), channel_id=1, source_target_pairs={{0,0},{2,2},{4,8},{6,10},{8,4},{10,6},{12,12},{14,14},{16,16},{18,... | collective-permute-start | bytes 6320 | tf_op jit(solution)/shard_map/ppermute | solution.py:1419
  10.0 406.5 %collective-permute-start = (bf16[128,2048]{1,0:T(8,128)(2,1)S(1)}, bf16[128,2048]{1,0:T(8,128)(2,1)S(1)}, u32[]{:S(2)}, u32[]{:S(2)}) collective-permute-start(bf16[128,2048]{1,0:T(8,128)(2,1)S(1)} %constant_dynamic-slice_fusion.9), channel_id=1, source_target_pairs={{0,0},{2,2},{4,8},{6,10},{8,4},{10,6},{12,12},{14,14},{16,16},{18,... | collective-permute-start | bytes 1572872 | tf_op jit(solution)/shard_map/ppermute | solution.py:1419
  99.9 28.3 %collective-permute-start.1 = (bf16[128,2048]{1,0:T(8,128)(2,1)}, bf16[128,2048]{1,0:T(8,128)(2,1)S(1)}, u32[]{:S(2)}, u32[]{:S(2)}) collective-permute-start(bf16[128,2048]{1,0:T(8,128)(2,1)} %constant_dynamic-slice_fusion.8), channel_id=1, source_target_pairs={{0,0},{2,2},{4,8},{6,10},{8,4},{10,6},{12,12},{14,14},{16,16},{18,... | collective-permute-start | bytes 1572872 | tf_op jit(solution)/shard_map/ppermute | solution.py:1419
  128.2 0.8 copy-start.3
  416.5 0.8 copy-start.2
  786.2 5.3 copy-start.4
  786.2 6.1 copy-start.5
  786.3 6.9 copy-start.1
